TPU v7x, 32 devices: a whole 2x2x4 slice. The times are simulated.
32 devices in a mesh: dp: 16 (over z, y, x), pipe: 2 (over core).
Axes of the slice: x: 2, y: 2, z: 4, core: 2. Of those that a mesh axis runs over, the one named last changes fastest.
Arguments:
- layer_ends: bfloat16 [2, 16384, 1024], P('pipe', 'dp'), may hold values from -6 to 6
- segment_ids: int32 [32, 512], P('dp'), may hold values from 0 to 7, never falling along the last dimension, each value on 1 to 256 neighbouring positions
- mixture: int32 [16384], P('dp'), may hold values from 0 to 15
- noise: float32 [16384, 512], P('dp'), may hold values from -5 to 5
- plan_step: int32 [1], replicated, may hold values from 0 to 1999
- ln1_gain: bfloat16 [1024], P(('dp', 'pipe')), may hold values from 0.5 to 1.5
- w_qkv: bfloat16 [1024, 3072], P(('dp', 'pipe')), may hold values from -0.1875 to 0.1875
- w_out: bfloat16 [1024, 1024], P(('dp', 'pipe')), may hold values from -0.75 to 0.75
- ln2_gain: bfloat16 [1024], P(('dp', 'pipe')), may hold values from 0.5 to 1.5
- w_up: bfloat16 [1024, 4096], P(('dp', 'pipe')), may hold values from -0.1875 to 0.1875
- w_down: bfloat16 [4096, 1024], P(('dp', 'pipe')), may hold values from -0.09375 to 0.09375
- w_latent: bfloat16 [1024, 1024], P(('dp', 'pipe')), may hold values from -0.09375 to 0.09375
- w_decode: bfloat16 [512, 1024], P(('dp', 'pipe')), may hold values from -0.25 to 0.25
- decode_bias: bfloat16 [1024], P(('dp', 'pipe')), may hold values from -3 to 3
- comp_mean: bfloat16 [16, 512], P(None, ('dp', 'pipe')), may hold values from -4 to 4
- comp_logvar: bfloat16 [16, 512], P(None, ('dp', 'pipe')), may hold values from -0.5 to 0.5
Outputs:
- result_ends: float32 [2, 16384, 1024], P('pipe', 'dp')
- grad_ln1_gain: float32 [1024], P(('dp', 'pipe'))
- grad_qkv: float32 [1024, 3072], P(('dp', 'pipe'))
- grad_out: float32 [1024, 1024], P(('dp', 'pipe'))
- grad_ln2_gain: float32 [1024], P(('dp', 'pipe'))
- grad_up: float32 [1024, 4096], P(('dp', 'pipe'))
- grad_down: float32 [4096, 1024], P(('dp', 'pipe'))
- grad_latent: float32 [1024, 1024], P(('dp', 'pipe'))
- grad_decode: float32 [512, 1024], P(('dp', 'pipe'))
- grad_bias: float32 [1024], P(('dp', 'pipe'))
- grad_comp_mean: float32 [16, 512], P(None, ('dp', 'pipe'))
- grad_comp_logvar: float32 [16, 512], P(None, ('dp', 'pipe'))
Inputs may be any that keep to these rules, and one draw needn't show every extreme that they name: `segment_ids`: within each row of 512 cells ids never fall; each slide covers 1 to 256 cells, and one covers exactly that many.
All inputs are finite; a program needn't handle non-finite values.
Results may differ from a plain program's by a relative error of at most 0.012.
The roundings to bfloat16 on the way count: a program that leaves them out, or rounds other values in their place, can miss the bound.
Values may be sent and summed in bfloat16 or wider, within the bound.
No kernel may reach another device: no remote copies, remote signals or barrier semaphores. Data moves between devices by JAX's collectives and lax.ppermute only.
A program may use at most 448 MiB of HBM per device.

v0:
```python
import jax
import jax.numpy as jnp
from jax import lax
from jax.sharding import PartitionSpec as P

HEADS = 16
WARM = 1000


HIGHEST = lax.Precision.HIGHEST
FREE_BITS = 0.8
SOFTNESS = 0.2
BLOCK_ROWS = 512
NEGATIVE = -1e30


def for_sending(value):
    return jax.tree.map(lambda a: a.astype(jnp.bfloat16) if a.dtype == jnp.float32 else a, value)


def from_behind(value, axis, by):
    length = lax.axis_size(axis)
    pairs = [(i, i + by) for i in range(length) if 0 <= i + by < length]
    return lax.ppermute(value, axis, pairs)


def matmul(left_side, right_side):
    return jnp.dot(left_side, right_side, preferred_element_type=jnp.float32)


def left_product(left_side, right_side):
    return lax.dot_general(
        left_side, right_side, (((0,), (0,)), ((), ())), preferred_element_type=jnp.float32
    )


def right_product(left_side, right_side):
    return lax.dot_general(
        left_side, right_side, (((1,), (1,)), ((), ())), preferred_element_type=jnp.float32
    )


def layer_norm(tensor):
    centred = tensor - jnp.mean(tensor, axis=-1, keepdims=True)
    return centred * lax.rsqrt(jnp.mean(centred * centred, axis=-1, keepdims=True) + 1e-05)


def scaled_norm(tensor, gain_vec):
    return layer_norm(tensor) * gain_vec


def gelu_exact(tensor):
    return jax.nn.gelu(tensor, approximate=False)


def split_heads(packed):
    cell_count = packed.shape[0]
    model_width = packed.shape[1] // 3
    shaped = packed.reshape(cell_count, 3, HEADS, model_width // HEADS)
    return (shaped[:, 0], shaped[:, 1], shaped[:, 2])


def block_probs(query_block, key_rows, segment_block, segments):
    head_size = query_block.shape[2]
    scores = jnp.einsum(
        "qhd,khd->hqk", query_block, key_rows, preferred_element_type=jnp.float32
    ) * head_size ** (-0.5)
    same_slide = segment_block[:, None] == segments[None, :]
    scores = jnp.where(same_slide[None, :, :], scores, NEGATIVE)
    row_max = jnp.max(scores, axis=-1, keepdims=True)
    powers = jnp.exp(scores - row_max)
    return powers / jnp.sum(powers, axis=-1, keepdims=True)


def attention_forward(packed, segments):
    queries, key_rows, value_rows = split_heads(packed)
    cell_count = packed.shape[0]
    step_rows = min(BLOCK_ROWS, cell_count)
    pieces = []
    for start_row in range(0, cell_count, step_rows):
        attn_weights = block_probs(
            queries[start_row : start_row + step_rows],
            key_rows,
            segments[start_row : start_row + step_rows],
            segments,
        )
        mixed_rows = jnp.einsum(
            "hqk,khd->qhd",
            attn_weights.astype(jnp.bfloat16),
            value_rows,
            preferred_element_type=jnp.float32,
        )
        pieces.append(mixed_rows.reshape(mixed_rows.shape[0], -1))
    return jnp.concatenate(pieces, axis=0)


def attention_backward(packed, segments, grad_mixed):
    queries, key_rows, value_rows = split_heads(packed)
    cell_count, model_width = grad_mixed.shape
    head_size = model_width // HEADS
    score_scale = head_size ** (-0.5)
    grad_heads = grad_mixed.reshape(cell_count, HEADS, head_size)
    step_rows = min(BLOCK_ROWS, cell_count)
    grad_keys = jnp.zeros((cell_count, HEADS, head_size), jnp.float32)
    grad_values = jnp.zeros((cell_count, HEADS, head_size), jnp.float32)
    query_grads = []
    for start_row in range(0, cell_count, step_rows):
        query_block = queries[start_row : start_row + step_rows]
        attn_weights = block_probs(
            query_block, key_rows, segments[start_row : start_row + step_rows], segments
        )
        weights_low = attn_weights.astype(jnp.bfloat16)
        grad_block = grad_heads[start_row : start_row + step_rows]
        grad_values = grad_values + jnp.einsum(
            "hqk,qhd->khd", weights_low, grad_block, preferred_element_type=jnp.float32
        )
        grad_weights = jnp.einsum(
            "qhd,khd->hqk", grad_block, value_rows, preferred_element_type=jnp.float32
        )
        grad_scores = attn_weights * (
            grad_weights - jnp.sum(grad_weights * attn_weights, axis=-1, keepdims=True)
        )
        scores_low = grad_scores.astype(jnp.bfloat16)
        query_grads.append(
            jnp.einsum("hqk,khd->qhd", scores_low, key_rows, preferred_element_type=jnp.float32)
            * score_scale
        )
        grad_keys = (
            grad_keys
            + jnp.einsum(
                "hqk,qhd->khd", scores_low, query_block, preferred_element_type=jnp.float32
            )
            * score_scale
        )
    grad_queries = jnp.concatenate(query_grads, axis=0)
    return jnp.concatenate(
        [
            grad_queries.reshape(cell_count, model_width),
            grad_keys.reshape(cell_count, model_width),
            grad_values.reshape(cell_count, model_width),
        ],
        axis=1,
    )


def phase_one_parts(inputs_low, segments, params):
    gain_one, w_qkv, w_out, gain_two, w_up, w_down = params
    inputs = inputs_low.astype(jnp.float32)
    first_in = scaled_norm(inputs, gain_one.astype(jnp.float32)).astype(jnp.bfloat16)
    packed = matmul(first_in, w_qkv).astype(jnp.bfloat16)
    mixed_rows = attention_forward(packed, segments).astype(jnp.bfloat16)
    middle = inputs + matmul(mixed_rows, w_out)
    second_in = scaled_norm(middle, gain_two.astype(jnp.float32)).astype(jnp.bfloat16)
    up_proj = matmul(second_in, w_up)
    hidden = gelu_exact(up_proj).astype(jnp.bfloat16)
    carried = (middle + matmul(hidden, w_down)).astype(jnp.bfloat16)
    return (inputs, first_in, packed, mixed_rows, middle, second_in, up_proj, hidden, carried)


def phase_one_backward(inputs_low, segments, grad_carried, params, sums):
    gain_one, w_qkv, w_out, gain_two, w_up, w_down = params
    inputs, first_in, packed, mixed_rows, middle, second_in, up_proj, hidden, carried = (
        phase_one_parts(inputs_low, segments, params)
    )
    sum_gain_one, sum_qkv, sum_out, sum_gain_two, sum_up, sum_down = sums
    sum_down = sum_down + left_product(hidden, grad_carried)
    grad_hidden = right_product(grad_carried, w_down)
    gelu_value, gelu_pull = jax.vjp(gelu_exact, up_proj)
    grad_up = gelu_pull(grad_hidden)[0].astype(jnp.bfloat16)
    sum_up = sum_up + left_product(second_in, grad_up)
    grad_second = right_product(grad_up, w_up)
    normed_two, pull_two = jax.vjp(scaled_norm, middle, gain_two.astype(jnp.float32))
    norm_grad, gain_grad = pull_two(grad_second)
    sum_gain_two = sum_gain_two + gain_grad
    grad_middle = grad_carried.astype(jnp.float32) + norm_grad
    grad_branch = grad_middle.astype(jnp.bfloat16)
    sum_out = sum_out + left_product(mixed_rows, grad_branch)
    grad_mixed = right_product(grad_branch, w_out).astype(jnp.bfloat16)
    grad_packed = attention_backward(packed, segments, grad_mixed).astype(jnp.bfloat16)
    sum_qkv = sum_qkv + left_product(first_in, grad_packed)
    grad_first = right_product(grad_packed, w_qkv)
    normed_one, pull_one = jax.vjp(scaled_norm, inputs, gain_one.astype(jnp.float32))
    norm_grad_one, gain_grad_one = pull_one(grad_first)
    sum_gain_one = sum_gain_one + gain_grad_one
    grad_inputs = grad_middle + norm_grad_one
    return (grad_inputs, (sum_gain_one, sum_qkv, sum_out, sum_gain_two, sum_up, sum_down))


def latent_piece(mean_part, logvar_part, noise_part, centre, spread):
    sample = mean_part + jnp.exp(0.5 * logvar_part) * noise_part
    gap = mean_part - centre
    diverge = 0.5 * (
        spread - logvar_part + (jnp.exp(logvar_part) + gap * gap) * jnp.exp(-spread) - 1.0
    )
    return (sample, diverge)


def phase_two_parts(carried, mixture_rows, noise_rows, params):
    w_latent, w_decode, decode_bias, comp_mean, comp_logvar = params
    moments = matmul(carried, w_latent)
    latent = moments.shape[1] // 2
    choose = (
        mixture_rows[:, None] == jnp.arange(comp_mean.shape[0], dtype=jnp.int32)[None, :]
    ).astype(jnp.float32)
    centre = jnp.dot(choose, comp_mean.astype(jnp.float32), precision=HIGHEST)
    spread = jnp.dot(choose, comp_logvar.astype(jnp.float32), precision=HIGHEST)
    sample, diverge = latent_piece(
        moments[:, :latent], moments[:, latent:], noise_rows, centre, spread
    )
    sample_low = sample.astype(jnp.bfloat16)
    decoded = matmul(sample_low, w_decode) + decode_bias.astype(jnp.float32)
    return (moments, choose, centre, spread, sample_low, decoded, diverge)


def phase_two_backward(carried, mixture_rows, noise_rows, grad_output, weight_vec, params, sums):
    w_latent, w_decode, decode_bias, comp_mean, comp_logvar = params
    moments, choose, centre, spread, sample_low, decoded, diverge = phase_two_parts(
        carried, mixture_rows, noise_rows, params
    )
    sum_latent, sum_decode, sum_bias, sum_mean, sum_logvar = sums
    sum_decode = sum_decode + left_product(sample_low, grad_output)
    sum_bias = sum_bias + jnp.sum(grad_output.astype(jnp.float32), axis=0)
    grad_sample = right_product(grad_output, w_decode)
    latent = moments.shape[1] // 2
    piece_value, piece_pull = jax.vjp(
        latent_piece, moments[:, :latent], moments[:, latent:], noise_rows, centre, spread
    )
    grad_mean, grad_logvar, noise_grad, grad_centre, grad_spread = piece_pull(
        (grad_sample, jnp.broadcast_to(weight_vec[None, :], diverge.shape))
    )
    grad_moments = jnp.concatenate([grad_mean, grad_logvar], axis=1).astype(jnp.bfloat16)
    sum_latent = sum_latent + left_product(carried, grad_moments)
    sum_mean = sum_mean + lax.dot_general(
        choose, grad_centre, (((0,), (0,)), ((), ())), precision=HIGHEST
    )
    sum_logvar = sum_logvar + lax.dot_general(
        choose, grad_spread, (((0,), (0,)), ((), ())), precision=HIGHEST
    )
    grad_carried = right_product(grad_moments, w_latent).astype(jnp.bfloat16)
    return (grad_carried, (sum_latent, sum_decode, sum_bias, sum_mean, sum_logvar))


def local(
    layer_ends,
    segment_ids,
    mixture,
    noise,
    plan_step,
    ln1_gain,
    w_qkv,
    w_out,
    ln2_gain,
    w_up,
    w_down,
    w_latent,
    w_decode,
    decode_bias,
    comp_mean,
    comp_logvar,
):
    gathered = (
        lax.all_gather(ln1_gain, ("dp", "pipe"), axis=0, tiled=True),
        lax.all_gather(w_qkv, ("dp", "pipe"), axis=0, tiled=True),
        lax.all_gather(w_out, ("dp", "pipe"), axis=0, tiled=True),
        lax.all_gather(ln2_gain, ("dp", "pipe"), axis=0, tiled=True),
        lax.all_gather(w_up, ("dp", "pipe"), axis=0, tiled=True),
        lax.all_gather(w_down, ("dp", "pipe"), axis=0, tiled=True),
        lax.all_gather(w_latent, ("dp", "pipe"), axis=0, tiled=True),
        lax.all_gather(w_decode, ("dp", "pipe"), axis=0, tiled=True),
        lax.all_gather(decode_bias, ("dp", "pipe"), axis=0, tiled=True),
        lax.all_gather(comp_mean, ("dp", "pipe"), axis=1, tiled=True),
        lax.all_gather(comp_logvar, ("dp", "pipe"), axis=1, tiled=True),
    )
    first_params = gathered[:6]
    second_params = gathered[6:]
    pipe_rank = lax.axis_index("pipe")
    rounds = segment_ids.shape[0]
    cell_count = segment_ids.shape[1]
    model_width = layer_ends.shape[2]
    latent = noise.shape[1]
    stream = layer_ends[0]
    kl_weight = jnp.minimum(1.0, (plan_step[0] + 1).astype(jnp.float32) / WARM)
    total_cells = rounds * cell_count * lax.axis_size("dp")
    blank_rows = jnp.zeros((cell_count, model_width), jnp.bfloat16)
    blank_grad = jnp.zeros((cell_count, model_width), jnp.float32)
    blank_kl = jnp.zeros((latent,), jnp.float32)

    def rows_of(tensor, batch_index):
        return tensor[batch_index * cell_count : (batch_index + 1) * cell_count]

    received = []
    outputs = []
    kl_sum = blank_kl
    for clock_tick in range(rounds + 1):
        ahead_batch = min(clock_tick, rounds - 1)
        behind = max(clock_tick - 1, 0)
        incoming = received[behind] if clock_tick > 0 else blank_rows

        def forward_one(ahead_batch=ahead_batch):
            one_parts = phase_one_parts(
                rows_of(stream, ahead_batch), segment_ids[ahead_batch], first_params
            )
            return (one_parts[-1], blank_rows, blank_kl)

        def forward_two(behind=behind, incoming=incoming):
            two_parts = phase_two_parts(
                incoming, rows_of(mixture, behind), rows_of(noise, behind), second_params
            )
            return (blank_rows, two_parts[5].astype(jnp.bfloat16), jnp.sum(two_parts[6], axis=0))

        def forward_spare():
            return (blank_rows, blank_rows, blank_kl)

        first_branch = 0 if clock_tick < rounds else 2
        second_branch = 1 if clock_tick > 0 else 2
        branch = jnp.where(pipe_rank == 0, first_branch, second_branch)
        outgoing, produced, kl_part = lax.switch(branch, [forward_one, forward_two, forward_spare])
        if clock_tick > 0:
            outputs.append(produced)
            kl_sum = kl_sum + lax.psum(kl_part, "dp")
        if clock_tick < rounds:
            received.append(
                jax.tree.map(
                    lambda part, own: part.astype(own.dtype),
                    from_behind(for_sending(outgoing), "pipe", 1),
                    outgoing,
                )
            )
    kl_mean = kl_sum / total_cells
    weight_vec = kl_weight * jax.nn.sigmoid((kl_mean - FREE_BITS) / SOFTNESS)
    sums_one = tuple((jnp.zeros(weight.shape, jnp.float32) for weight in first_params))
    sums_two = tuple((jnp.zeros(weight.shape, jnp.float32) for weight in second_params))
    returned = blank_rows
    input_grads = []
    for clock_tick in range(rounds + 1):
        ahead_batch = min(clock_tick, rounds - 1)
        behind = max(clock_tick - 1, 0)

        def backward_two(sums_first, sums_second, returned_rows, ahead_batch=ahead_batch):
            grad_carried, sums_second = phase_two_backward(
                received[ahead_batch],
                rows_of(mixture, ahead_batch),
                rows_of(noise, ahead_batch),
                rows_of(stream, ahead_batch),
                weight_vec,
                second_params,
                sums_second,
            )
            return (grad_carried, blank_grad, sums_first, sums_second)

        def backward_one(sums_first, sums_second, returned_rows, behind=behind):
            grad_inputs, sums_first = phase_one_backward(
                rows_of(stream, behind),
                segment_ids[behind],
                returned_rows,
                first_params,
                sums_first,
            )
            return (blank_rows, grad_inputs, sums_first, sums_second)

        def backward_spare(sums_first, sums_second, returned_rows):
            return (blank_rows, blank_grad, sums_first, sums_second)

        first_branch = 0 if clock_tick < rounds else 2
        second_branch = 1 if clock_tick > 0 else 2
        branch = jnp.where(pipe_rank == 1, first_branch, second_branch)
        outgoing, grad_inputs, sums_one, sums_two = lax.switch(
            branch, [backward_two, backward_one, backward_spare], sums_one, sums_two, returned
        )
        if clock_tick > 0:
            input_grads.append(grad_inputs)
        if clock_tick < rounds:
            returned = jax.tree.map(
                lambda part, own: part.astype(own.dtype),
                from_behind(for_sending(outgoing), "pipe", -1),
                outgoing,
            )
    grad_stream = jnp.concatenate(input_grads, axis=0)
    out_stream = jnp.concatenate(outputs, axis=0).astype(jnp.float32)
    result_ends = jnp.where(pipe_rank == 0, grad_stream, out_stream)[None]
    grad_gain_one, grad_qkv, grad_out, grad_gain_two, grad_up, grad_down = sums_one
    grad_latent, grad_decode, grad_bias, grad_mean, grad_logvar = sums_two
    reduced = (
        lax.psum_scatter(grad_gain_one, ("dp", "pipe"), scatter_dimension=0, tiled=True),
        lax.psum_scatter(grad_qkv, ("dp", "pipe"), scatter_dimension=0, tiled=True),
        lax.psum_scatter(grad_out, ("dp", "pipe"), scatter_dimension=0, tiled=True),
        lax.psum_scatter(grad_gain_two, ("dp", "pipe"), scatter_dimension=0, tiled=True),
        lax.psum_scatter(grad_up, ("dp", "pipe"), scatter_dimension=0, tiled=True),
        lax.psum_scatter(grad_down, ("dp", "pipe"), scatter_dimension=0, tiled=True),
        lax.psum_scatter(grad_latent, ("dp", "pipe"), scatter_dimension=0, tiled=True),
        lax.psum_scatter(grad_decode, ("dp", "pipe"), scatter_dimension=0, tiled=True),
        lax.psum_scatter(grad_bias, ("dp", "pipe"), scatter_dimension=0, tiled=True),
        lax.psum_scatter(grad_mean, ("dp", "pipe"), scatter_dimension=1, tiled=True),
        lax.psum_scatter(grad_logvar, ("dp", "pipe"), scatter_dimension=1, tiled=True),
    )
    return (
        result_ends,
        reduced[0],
        reduced[1],
        reduced[2],
        reduced[3],
        reduced[4],
        reduced[5],
        reduced[6],
        reduced[7],
        reduced[8],
        reduced[9],
        reduced[10],
    )


def solution(mesh):
    return jax.shard_map(
        local,
        mesh=mesh,
        in_specs=(
            P("pipe", "dp", None),
            P("dp", None),
            P("dp"),
            P("dp", None),
            P(),
            P(("dp", "pipe")),
            P(("dp", "pipe"), None),
            P(("dp", "pipe"), None),
            P(("dp", "pipe")),
            P(("dp", "pipe"), None),
            P(("dp", "pipe"), None),
            P(("dp", "pipe"), None),
            P(("dp", "pipe"), None),
            P(("dp", "pipe")),
            P(None, ("dp", "pipe")),
            P(None, ("dp", "pipe")),
        ),
        out_specs=(
            P("pipe", "dp", None),
            P(("dp", "pipe")),
            P(("dp", "pipe"), None),
            P(("dp", "pipe"), None),
            P(("dp", "pipe")),
            P(("dp", "pipe"), None),
            P(("dp", "pipe"), None),
            P(("dp", "pipe"), None),
            P(("dp", "pipe"), None),
            P(("dp", "pipe")),
            P(None, ("dp", "pipe")),
            P(None, ("dp", "pipe")),
        ),
        check_vma=False,
    )
```

profile of v0, /device:TPU:8, one launch (start us, length us, event | category | flops | bytes accessed | tf_op | source)
XLA Modules:
  0.0 2228.8 jit_solution(2427748996337902968)
XLA Ops:
  13.7 40.6 %all-reduce.7 = (bf16[1024]{0:T(1024)(128)(2,1)S(1)}, bf16[1024]{0:T(1024)(128)(2,1)S(1)}, bf16[1024]{0:T(1024)(128)(2,1)S(1)}) all-reduce(bf16[1024]{0:T(1024)(128)(2,1)S(1)} %dynamic-update-slice, bf16[1024]{0:T(1024)(128)(2,1)S(1)} %dynamic-update-slice.1, ...), channel_id=1, replica_groups=mesh['dp'=16,'pipe'=2] {'dp','pipe'}, use_global_device_ids=true, to_apply=%add | all-reduce | flops 3072 | bytes 12288
  67.5 72.2 %all-gather.7.cloned.1.call-done = bf16[1024,3072]{1,0:T(8,128)(2,1)} async-done(((bf16[32,3072]{1,0:T(8,128)(2,1)}), bf16[1024,3072]{1,0:T(8,128)(2,1)}) %all-gather.7.cloned.1.call-update) | async-done | bytes 6291472 | tf_op jit(solution)/shard_map/all_gather | solution.py:263
  139.7 78.9 %all-gather.11.cloned.1.call-done = bf16[1024,4096]{1,0:T(8,128)(2,1)} async-done(((bf16[32,4096]{1,0:T(8,128)(2,1)}), bf16[1024,4096]{1,0:T(8,128)(2,1)}) %all-gather.11.cloned.1.call-update) | async-done | bytes 8388624 | tf_op jit(solution)/shard_map/all_gather | solution.py:266
  218.6 78.8 %all-gather.13.cloned.1.call-done = bf16[4096,1024]{1,0:T(8,128)(2,1)} async-done(((bf16[128,1024]{1,0:T(8,128)(2,1)}), bf16[4096,1024]{1,0:T(8,128)(2,1)}) %all-gather.13.cloned.1.call-update) | async-done | bytes 8388624 | tf_op jit(solution)/shard_map/all_gather | solution.py:267
  297.4 64.3 %conditional.6 = (bf16[512,1024]{1,0:T(8,128)(2,1)S(1)}) conditional(s32[]{:T(128)} %clamp.20, (bf16[1024,1024]{1,0:T(8,128)(2,1)}, bf16[1024]{0:T(1024)(128)(2,1)S(1)}, bf16[1024,3072]{1,0:T(8,128)(2,1)}, s32[2,512]{1,0:T(2,128)}, bf16[1024,1024]{1,0:T(8,128)(2,1)}, /*index=5*/bf16[1024]{0:T(1024)(128)(2,1)S(1)}, ...), branch_computations={%region_0.7_spmd, %region_7.8_spmd, %region_8.9_spmd} | conditional | flops 14134546432 | bytes 102381664 | solution.py:317
  331.4 29.9 %add_convert_fusion = bf16[512,1024]{1,0:T(8,128)(2,1)S(1)} fusion(f32[512,1024]{1,0:T(8,128)S(1)} %get-tuple-element.940, bf16[4096,1024]{1,0:T(8,128)(2,1)} %get-tuple-element.317, bf16[1024,4096]{1,0:T(8,128)(2,1)} %get-tuple-element.316, f32[1024]{0:T(1024)S(1)} %convert_element_type.221, f32[512]{0:T(512)S(1)} %add_rsqrt_fusion, ...), kind=kOutput, calls=%fused_computation.38 | convolution fusion | flops 8729395200 | bytes 19931136 | tf_op jit(solution)/shard_map/cond/branch_0_fun/dot_general | solution.py:28
  364.1 33.1 %all_gather.39 = bf16[16,512]{0,1:T(8,128)(2,1)S(1)} all-gather(bf16[16,16]{0,1:T(8,128)(2,1)S(1)} %copy.207), channel_id=1, replica_groups=mesh['dp'=16,'pipe'=2] {'dp','pipe'}, dimensions={1}, use_global_device_ids=true | all-gather | bytes 16896 | tf_op jit(solution)/shard_map/all_gather | solution.py:272
  397.3 37.0 %all_gather.41 = bf16[16,512]{0,1:T(8,128)(2,1)S(1)} all-gather(bf16[16,16]{0,1:T(8,128)(2,1)S(1)} %copy.208), channel_id=1, replica_groups=mesh['dp'=16,'pipe'=2] {'dp','pipe'}, dimensions={1}, use_global_device_ids=true | all-gather | bytes 16896 | tf_op jit(solution)/shard_map/all_gather | solution.py:271
  434.3 67.0 %conditional.7 = (bf16[512,1024]{1,0:T(8,128)(2,1)}, f32[512]{0:T(512)S(1)}, bf16[1,512,1024]{2,1,0:T(8,128)(2,1)S(1)}) conditional(s32[]{:T(128)} %clamp.19, (bf16[1024,1024]{1,0:T(8,128)(2,1)}, bf16[1024]{0:T(1024)(128)(2,1)S(1)}, bf16[1024,3072]{1,0:T(8,128)(2,1)}, s32[2,512]{1,0:T(2,128)}, bf16[1024,1024]{1,0:T(8,128)(2,1)}, ...), branch_computations={%region_9.16_spmd, %region_16.18_spmd, %region_18.19_spmd} | conditional | flops 14134546432 | bytes 103432312 | solution.py:317
  469.8 30.9 %add_convert_fusion.1 = bf16[512,1024]{1,0:T(8,128)(2,1)} fusion(f32[512,1024]{1,0:T(8,128)S(1)} %get-tuple-element.944, bf16[4096,1024]{1,0:T(8,128)(2,1)} %get-tuple-element.325, bf16[1024,4096]{1,0:T(8,128)(2,1)} %get-tuple-element.324, f32[1024]{0:T(1024)S(1)} %convert_element_type.233, f32[512]{0:T(512)S(1)} %add_rsqrt_fusion.2, ...), kind=kOutput, calls=%fused_computation.130 | convolution fusion | flops 8729395200 | bytes 19931136 | tf_op jit(solution)/shard_map/cond/branch_0_fun/dot_general | solution.py:28
  506.4 38.2 %psum.16 = f32[512]{0:T(512)S(1)} all-reduce(f32[512]{0:T(512)S(1)} %add.288), channel_id=1, replica_groups=mesh['dp'=16,'pipe'=2] {'dp'}, use_global_device_ids=true, to_apply=%region_19.20 | all-reduce | flops 512 | bytes 4096 | tf_op jit(solution)/shard_map/psum | solution.py:320
  545.2 40.8 %conditional.9 = (bf16[512,1024]{1,0:T(8,128)(2,1)}, f32[1024]{0:T(1024)}, f32[1024,3072]{1,0:T(8,128)}, f32[1024,1024]{1,0:T(8,128)}, f32[1024]{0:T(1024)}, /*i...) conditional(s32[]{:T(128)} %clamp.22, ...), branch_computations={%region_25.27_spmd, %region_27.39_spmd, %region_39.40_spmd} | conditional | flops 37861715968 | bytes 461343264 | solution.py:367
  608.1 198.0 %conditional.10 = (bf16[512,1024]{1,0:T(8,128)(2,1)}, f32[1024]{0:T(1024)}, f32[1024,3072]{1,0:T(8,128)}, f32[1024,1024]{1,0:T(8,128)}, f32[1024]{0:T(1024)}, /*...) conditional(s32[]{:T(128)} %clamp.18, ...), branch_computations={%region_40.0_spmd, %region_42.56_spmd, %region_56.57_spmd} | conditional | flops 38007996416 | bytes 569373696 | solution.py:367
  810.9 199.6 %conditional.11 = (f32[1024]{0:T(1024)}, f32[1024,3072]{1,0:T(8,128)}, f32[1024,1024]{1,0:T(8,128)}, f32[1024]{0:T(1024)}, f32[1024,4096]{1,0:T(8,128)}, /*index...) conditional(s32[]{:T(128)} %clamp.23, ...), branch_computations={%region_57.0_spmd, %region_59.73_spmd, %region_73.74_spmd} | conditional | flops 38007996416 | bytes 585110528 | solution.py:367
  971.7 26.8 %convolution_add_fusion.11 = f32[4096,1024]{1,0:T(8,128)} fusion(f32[4096,1024]{1,0:T(8,128)} %get-tuple-element.444, bf16[512,1024]{1,0:T(8,128)(2,1)S(1)} %get-tuple-element.435, f32[512,4096]{1,0:T(8,128)} %fusion.378), kind=kOutput, calls=%fused_computation.529 | convolution fusion | flops 4435476480 | bytes 42991616 | tf_op jit(solution)/shard_map/cond/branch_1_fun/dot_general | solution.py:32
  1018.0 45.0 %all-reduce.6 = (f32[1024]{0:T(1024)S(1)}, f32[1024]{0:T(1024)S(1)}, f32[1024]{0:T(1024)S(1)}) all-reduce(f32[1024]{0:T(1024)} %get-tuple-element.546, f32[1024]{0:T(1024)} %get-tuple-element.549, f32[1024]{0:T(1024)S(1)} %copy-done.84), channel_id=2, replica_groups=mesh['dp'=16,'pipe'=2] {'dp','pipe'}, use_global_device_ids=true, to_apply=%region_74.75.clone | all-reduce | flops 3072 | bytes 24576
  1070.3 59.4 %reduce-scatter.25.cloned.1.call-done = f32[16,16]{1,0:T(8,128)} async-done(((f32[512,16]{1,0:T(8,128)}), f32[16,16]{1,0:T(8,128)}) %reduce-scatter.25.cloned.1.call-update) | async-done | bytes 1040
  1131.0 130.3 %reduce-scatter.27.cloned.1.call-done = f32[16,16]{1,0:T(8,128)} async-done(((f32[512,16]{1,0:T(8,128)}), f32[16,16]{1,0:T(8,128)}) %reduce-scatter.27.cloned.1.call-update) | async-done | bytes 1040
  1262.7 133.9 %reduce-scatter.23.cloned.1.call-done = f32[16,1024]{1,0:T(8,128)} async-done(((f32[512,1024]{1,0:T(8,128)}), f32[16,1024]{1,0:T(8,128)}) %reduce-scatter.23.cloned.1.call-update) | async-done | bytes 65552 | tf_op jit(solution)/shard_map/reduce_scatter | solution.py:391
  1396.6 139.5 %reduce-scatter.15.cloned.1.call-done = f32[32,1024]{1,0:T(8,128)} async-done(((f32[1024,1024]{1,0:T(8,128)}), f32[32,1024]{1,0:T(8,128)}) %reduce-scatter.15.cloned.1.call-update) | async-done | bytes 131088 | tf_op jit(solution)/shard_map/reduce_scatter | solution.py:386
  1536.1 139.8 %reduce-scatter.21.cloned.1.call-done = f32[32,1024]{1,0:T(8,128)} async-done(((f32[1024,1024]{1,0:T(8,128)}), f32[32,1024]{1,0:T(8,128)}) %reduce-scatter.21.cloned.1.call-update) | async-done | bytes 131088 | tf_op jit(solution)/shard_map/reduce_scatter | solution.py:390
  1675.9 177.3 %reduce-scatter.13.cloned.1.call-done = f32[32,3072]{1,0:T(8,128)} async-done(((f32[1024,3072]{1,0:T(8,128)}), f32[32,3072]{1,0:T(8,128)}) %reduce-scatter.13.cloned.1.call-update) | async-done | bytes 393232 | tf_op jit(solution)/shard_map/reduce_scatter | solution.py:385
  1853.2 181.7 %reduce-scatter.17.cloned.1.call-done = f32[32,4096]{1,0:T(8,128)} async-done(((f32[1024,4096]{1,0:T(8,128)}), f32[32,4096]{1,0:T(8,128)}) %reduce-scatter.17.cloned.1.call-update) | async-done | bytes 524304 | tf_op jit(solution)/shard_map/reduce_scatter | solution.py:388
  2034.9 187.2 %reduce-scatter.19.cloned.1.call-done = f32[128,1024]{1,0:T(8,128)} async-done(((f32[4096,1024]{1,0:T(8,128)}), f32[128,1024]{1,0:T(8,128)}) %reduce-scatter.19.cloned.1.call-update) | async-done | bytes 524304 | tf_op jit(solution)/shard_map/reduce_scatter | solution.py:389
  (355 shorter events, 531.2 us)
Async XLA Ops:
  7.2 60.4 %all-gather.9.cloned.1.call-start = ((), (), s32[]{:S(2)}) async-start(), calls=%async_computation.9 | async-start | bytes 2162688 | tf_op jit(solution)/shard_map/all_gather | solution.py:264
  7.9 131.8 %all-gather.7.cloned.1.call-start = ((), (), s32[]{:S(2)}) async-start(), calls=%async_computation.8 | async-start | bytes 6488064 | tf_op jit(solution)/shard_map/all_gather | solution.py:263
  8.7 209.9 %all-gather.11.cloned.1.call-start = ((), (), s32[]{:S(2)}) async-start(), calls=%async_computation.10 | async-start | bytes 8650752 | tf_op jit(solution)/shard_map/all_gather | solution.py:266
  9.4 288.0 %all-gather.13.cloned.1.call-start = ((), (), s32[]{:S(2)}) async-start(), calls=%async_computation.11 | async-start | bytes 8650752 | tf_op jit(solution)/shard_map/all_gather | solution.py:267
  10.0 424.3 %all-gather.17.cloned.1.call-start = ((), (), s32[]{:S(2)}) async-start(), calls=%async_computation.13 | async-start | bytes 1081344 | tf_op jit(solution)/shard_map/all_gather | solution.py:269
  10.6 423.7 %all-gather.15.cloned.1.call-start = ((), (), s32[]{:S(2)}) async-start(), calls=%async_computation.12 | async-start | bytes 2162688 | tf_op jit(solution)/shard_map/all_gather | solution.py:268
  11.1 1118.5 %reduce-scatter.25.cloned.1.call-start = ((), (), s32[]{:S(2)}) async-start(), calls=%async_computation.20 | async-start | bytes 270336
  54.3 553.8 %copy-start.85 = (bf16[1024]{0:T(1024)(128)(2,1)}, bf16[1024]{0:T(1024)(128)(2,1)S(1)}, u32[]{:S(2)}) copy-start(bf16[1024]{0:T(1024)(128)(2,1)S(1)} %get-tuple-element.928) | copy-start | bytes 6148
  54.3 553.8 %copy-start.86 = (bf16[1024]{0:T(1024)(128)(2,1)}, bf16[1024]{0:T(1024)(128)(2,1)S(1)}, u32[]{:S(2)}) copy-start(bf16[1024]{0:T(1024)(128)(2,1)S(1)} %get-tuple-element.929) | copy-start | bytes 6148
  297.4 66.7 %copy-start.106 = (bf16[16,16]{1,0:T(8,128)(2,1)S(1)}, bf16[16,16]{1,0:T(8,128)(2,1)}, u32[]{:S(2)}) copy-start(bf16[16,16]{1,0:T(8,128)(2,1)} %param.48) | copy-start | bytes 1540
  297.4 136.9 %copy-start.92 = (s32[1024]{0:T(1024)S(1)}, s32[1024]{0:T(1024)}, u32[]{:S(2)}) copy-start(s32[1024]{0:T(1024)} %param.36) | copy-start | bytes 12292
  361.7 72.6 %collective-permute-start = (bf16[512,1024]{1,0:T(8,128)(2,1)S(1)}, bf16[512,1024]{1,0:T(8,128)(2,1)}, u32[]{:S(2)}, u32[]{:S(2)}) collective-permute-start(bf16[512,1024]{1,0:T(8,128)(2,1)S(1)} %get-tuple-element.1110), channel_id=1, source_target_pairs={{0,1},{2,3},{4,5},{6,7},{8,9},{10,11},{12,13},{14,15},{16,17},{18,... | collective-permute-start | bytes 3145736 | tf_op jit(solution)/shard_map/ppermute | solution.py:24
  501.3 3.9 collective-permute-start.1
  587.8 20.3 collective-permute-start.2
  608.1 202.8 %copy-start.94 = (s32[1024]{0:T(1024)S(1)}, s32[1024]{0:T(1024)}, u32[]{:S(2)}) copy-start(s32[1024]{0:T(1024)} %param.36) | copy-start | bytes 12292
  608.3 77.8 %copy-start.42 = (bf16[512,1024]{1,0:T(8,128)(2,1)}, bf16[512,1024]{1,0:T(8,128)(2,1)S(1)}, u32[]{:S(2)}) copy-start(bf16[512,1024]{1,0:T(8,128)(2,1)S(1)} %get-tuple-element.384) | copy-start | bytes 3145732 | tf_op jit(solution)/shard_map/cond
  806.2 4.8 collective-permute-start.3
  1012.2 249.2 %reduce-scatter.27.cloned.1.call-start = ((), (), s32[]{:S(2)}) async-start(), calls=%async_computation.21 | async-start | bytes 270336
  1013.8 382.7 %reduce-scatter.23.cloned.1.call-start = ((), (), s32[]{:S(2)}) async-start(), calls=%async_computation.19 | async-start | bytes 2162688 | tf_op jit(solution)/shard_map/reduce_scatter | solution.py:391
  1014.6 521.5 %reduce-scatter.15.cloned.1.call-start = ((), (), s32[]{:S(2)}) async-start(), calls=%async_computation.15 | async-start | bytes 4325376 | tf_op jit(solution)/shard_map/reduce_scatter | solution.py:386
  1015.2 660.7 %reduce-scatter.21.cloned.1.call-start = ((), (), s32[]{:S(2)}) async-start(), calls=%async_computation.18 | async-start | bytes 4325376 | tf_op jit(solution)/shard_map/reduce_scatter | solution.py:390
  1015.9 837.3 %reduce-scatter.13.cloned.1.call-start = ((), (), s32[]{:S(2)}) async-start(), calls=%async_computation.14 | async-start | bytes 12976128 | tf_op jit(solution)/shard_map/reduce_scatter | solution.py:385
  1016.5 1018.4 %reduce-scatter.17.cloned.1.call-start = ((), (), s32[]{:S(2)}) async-start(), calls=%async_computation.16 | async-start | bytes 17301504 | tf_op jit(solution)/shard_map/reduce_scatter | solution.py:388
  1017.2 1204.9 %reduce-scatter.19.cloned.1.call-start = ((), (), s32[]{:S(2)}) async-start(), calls=%async_computation.17 | async-start | bytes 17301504 | tf_op jit(solution)/shard_map/reduce_scatter | solution.py:389
  (74 other events, 958.0 us)
Sparse Core Ops, SparseCore 0:
  10.9 56.6 all-gather.8
  70.4 69.2 all-gather.6
  142.6 75.9 all-gather.10
  221.3 76.0 all-gather.12
  300.1 51.4 all-gather.16
  354.3 55.6 all-gather.14
  1012.3 117.3 reduce-scatter.24
  1132.0 129.3 reduce-scatter.26
  1264.2 132.3 reduce-scatter.22
  1399.4 136.6 reduce-scatter.14
  1539.1 136.8 reduce-scatter.20
  1683.4 169.7 reduce-scatter.12
  1856.0 178.7 reduce-scatter.16
  2037.6 184.4 reduce-scatter.18
where the time goes:
time: 2240 us; the launch traced here: 2230 us
  waiting for transfers between devices  1420 us (63%)
  matrix products  433 us (19%)
  blocking collectives  194 us (9%)
  local copies, waits for them, and re-layouts  77.6 us (3%)
  other arithmetic  55.5 us (2%)
  loops' own time  23.4 us (1%)
    unnamed x16, waiting for transfers between devices  197 us
    reduce_scatter x1, waiting for transfers between devices, local(): lax.psum_scatter(grad_down, ('dp', 'pipe'), scatter_dimension=0, tiled=True)  187 us
    reduce_scatter x1, waiting for transfers between devices, local(): lax.psum_scatter(grad_up, ('dp', 'pipe'), scatter_dimension=0, tiled=True)  182 us
    reduce_scatter x1, waiting for transfers between devices, local(): lax.psum_scatter(grad_qkv, ('dp', 'pipe'), scatter_dimension=0, tiled=True)  177 us
    reduce_scatter x1, waiting for transfers between devices, local(): lax.psum_scatter(grad_latent, ('dp', 'pipe'), scatter_dimension=0, tiled=...  140 us
    reduce_scatter x1, waiting for transfers between devices, local(): lax.psum_scatter(grad_out, ('dp', 'pipe'), scatter_dimension=0, tiled=True)  140 us
    reduce_scatter x1, waiting for transfers between devices, local(): lax.psum_scatter(grad_decode, ('dp', 'pipe'), scatter_dimension=0, tiled=...  134 us
    dot_general x8, matrix products, left_product(): lax.dot_general(left_side, right_side, (((0,), (0,)), ((), ())), preferre...  116 us
  transfers between devices with their start and end apart: 18, of which 15 were waited for; matrix products, arithmetic and copies ran while one was open for 4% of the time, Pallas kernels for 0%

commit v1 on v0

v1 whole, which is shorter than its diff:
```python
import functools

import jax
import jax.numpy as jnp
from jax import lax
from jax.experimental import pallas as pl
from jax.experimental.pallas import tpu as pltpu
from jax.sharding import PartitionSpec as P

HEADS = 16
WARM = 1000
HIGHEST = lax.Precision.HIGHEST
FREE_BITS = 0.8
SOFTNESS = 0.2
NEGATIVE = -1e30
EVERY = ("dp", "pipe")
LOW = jnp.bfloat16
FULL = jnp.float32


def after(value, *others):
    return lax.optimization_barrier((value,) + others)[0]


def swap_bits(mask):
    return (mask & 1) * 2 + (mask >> 1)


def send(value, even, odd):
    count = lax.axis_size("dp") * lax.axis_size("pipe")
    pairs = [(i, i ^ (odd if i & 1 else even)) for i in range(count)]
    return lax.ppermute(value, EVERY, pairs)


def send_core(value):
    return send(value, 1, 1)


def far_masks():
    return range(1, lax.axis_size("dp") // 4)


def far_exchange(value, mask):
    return send(value, mask * 8, mask * 8)


def near_first(value):
    return send(value, 2, 4)


def near_second(value):
    return send(value, 4, 2)


def place():
    return jnp.stack([lax.axis_index("dp"), lax.axis_index("pipe")]).astype(jnp.int32)


def slot_owner(place_ref, slot, far, other_core):
    turn, step = divmod(slot, far)
    core = place_ref[1]
    if other_core:
        core = 1 - core
    near = jnp.where(core == 0, turn, swap_bits(turn))
    return (place_ref[0] ^ (4 * step)) ^ near, core


def copy_through(copies, sems):
    into = [pltpu.make_async_copy(src, mid, sems.at[0, i]) for i, (src, mid, _) in enumerate(copies)]
    out = [pltpu.make_async_copy(mid, dst, sems.at[1, i]) for i, (_, mid, dst) in enumerate(copies)]
    for one in into:
        one.start()
    for one, two in zip(into, out):
        one.wait()
        two.start()
    for two in out:
        two.wait()


def unpack(parts, pieces):
    half, rows, cols = parts[0].shape
    far = half // 2
    count = half * 2

    def kernel(place_ref, own_a, own_b, other_a, other_b, *rest):
        outs = rest[: len(pieces)]
        middles, sems = rest[len(pieces) : -1], rest[-1]
        copies = []
        for refs, other in (((own_a, own_b), False), ((other_a, other_b), True)):
            for slot in range(count):
                dp_index, core = slot_owner(place_ref, slot, far, other)
                source = refs[slot // half].at[slot % half]
                for (row, height, col, width), middle, out in zip(pieces, middles, outs):
                    copies.append(
                        (
                            source.at[pl.ds(row, height), pl.ds(col, width)],
                            middle.at[dp_index, core],
                            out.at[dp_index, core],
                        )
                    )
        copy_through(copies, sems)

    anywhere = pl.BlockSpec(memory_space=pl.ANY)
    shapes = [(count, 2, p[1], p[3]) for p in pieces]
    size = 4 * count * rows * cols
    outs = pl.pallas_call(
        kernel,
        out_shape=[jax.ShapeDtypeStruct(shape, LOW) for shape in shapes],
        in_specs=[pl.BlockSpec(memory_space=pltpu.SMEM)] + [anywhere] * 4,
        out_specs=[anywhere] * len(pieces),
        scratch_shapes=[pltpu.VMEM(shape, LOW) for shape in shapes]
        + [pltpu.SemaphoreType.DMA((2, 2 * count * len(pieces)))],
        compiler_params=pltpu.CompilerParams(vmem_limit_bytes=size + (2 << 20)),
        cost_estimate=pl.CostEstimate(flops=0, bytes_accessed=2 * size, transcendentals=0),
        name="unpack",
    )(place(), *parts)
    return [o.reshape(count * 2 * p[1], p[3]) for o, p in zip(outs, pieces)]


def pack(grads, pieces, far):
    count = far * 4
    rows = max(p[0] + p[1] for p in pieces)
    cols = max(p[2] + p[3] for p in pieces)
    shaped = [g.reshape(count, 2, p[1], p[3]) for g, p in zip(grads, pieces)]

    def kernel(place_ref, *rest):
        ins = rest[: len(pieces)]
        outs, middles, sems = rest[len(pieces) : -3], rest[-3:-1], rest[-1]
        copies = []
        for out, middle, other in zip(outs, middles, (False, True)):
            for slot in range(count):
                dp_index, core = slot_owner(place_ref, slot, far, other)
                for (row, height, col, width), source in zip(pieces, ins):
                    copies.append(
                        (
                            source.at[dp_index, core],
                            middle.at[slot, pl.ds(row, height), pl.ds(col, width)],
                            out.at[slot, pl.ds(row, height), pl.ds(col, width)],
                        )
                    )
        copy_through(copies, sems)

    anywhere = pl.BlockSpec(memory_space=pl.ANY)
    size = 4 * count * rows * cols
    return pl.pallas_call(
        kernel,
        out_shape=[jax.ShapeDtypeStruct((count, rows, cols), LOW)] * 2,
        in_specs=[pl.BlockSpec(memory_space=pltpu.SMEM)] + [anywhere] * len(pieces),
        out_specs=[anywhere] * 2,
        scratch_shapes=[pltpu.VMEM((count, rows, cols), LOW)] * 2
        + [pltpu.SemaphoreType.DMA((2, 2 * count * len(pieces)))],
        compiler_params=pltpu.CompilerParams(vmem_limit_bytes=size + (2 << 20)),
        cost_estimate=pl.CostEstimate(flops=0, bytes_accessed=2 * size, transcendentals=0),
        name="pack",
    )(place(), *shaped)


def gather(shard, pieces):
    if shard.shape[0] % 16:
        whole = lax.all_gather(shard, EVERY, axis=0, tiled=False)
        return [
            whole[:, p[0] : p[0] + p[1], p[2] : p[2] + p[3]].reshape(-1, p[3]) for p in pieces
        ]
    block = shard[None]
    far = jnp.concatenate([block] + [far_exchange(block, m) for m in far_masks()], axis=0)
    eight = jnp.concatenate([far, near_first(far)], axis=0)
    rest = near_second(eight)
    return unpack((eight, rest, send_core(eight), send_core(rest)), pieces)


def add_low(one, two):
    return (one.astype(FULL) + two.astype(FULL)).astype(LOW)


def scatter(grads, pieces, rows):
    if rows % 16:
        count = lax.axis_size("dp") * 2
        height = max(p[0] + p[1] for p in pieces)
        columns = max(p[2] + p[3] for p in pieces)
        whole = jnp.zeros((count, height, columns), LOW)
        for grad, p in zip(grads, pieces):
            whole = whole.at[:, p[0] : p[0] + p[1], p[2] : p[2] + p[3]].set(
                grad.reshape(count, p[1], p[3])
            )
        return lax.psum_scatter(whole, EVERY, scatter_dimension=0, tiled=True)[0].astype(FULL)
    far = lax.axis_size("dp") // 4
    own, other = pack(grads, pieces, far)
    got = send_core(other)
    half = 2 * far
    outgoing = add_low(own[half:], got[half:])
    kept = add_low(own[:half], got[:half])
    got = near_second(outgoing)
    outgoing = add_low(kept[far:], got[far:])
    kept = add_low(kept[:far], got[:far])
    got = near_first(outgoing)
    total = kept.astype(FULL) + got.astype(FULL)
    low = total.astype(LOW)
    result = total[0]
    for mask in far_masks():
        result = result + far_exchange(low[mask : mask + 1], mask)[0].astype(FULL)
    return result


def sum_everywhere(value):
    bit = 1
    count = lax.axis_size("dp") * 2
    while bit < count:
        value = value + send(value, bit, bit)
        bit *= 2
    return value


def matmul(left_side, right_side):
    return jnp.dot(left_side, right_side, preferred_element_type=FULL)


def left_product(left_side, right_side):
    return lax.dot_general(
        left_side, right_side, (((0,), (0,)), ((), ())), preferred_element_type=FULL
    )


def right_product(left_side, right_side):
    return lax.dot_general(
        left_side, right_side, (((1,), (1,)), ((), ())), preferred_element_type=FULL
    )


def norm_parts(tensor):
    centred = tensor - jnp.mean(tensor, axis=-1, keepdims=True)
    scale = lax.rsqrt(jnp.mean(centred * centred, axis=-1, keepdims=True) + 1e-05)
    return centred * scale, scale


def norm_back(normed, scale, grad, gain):
    inner = grad * gain
    return scale * (
        inner
        - jnp.mean(inner, axis=-1, keepdims=True)
        - normed * jnp.mean(inner * normed, axis=-1, keepdims=True)
    )


def head_lanes(value, head, size):
    lane = lax.broadcasted_iota(jnp.int32, value.shape, 1)
    return jnp.where((lane // size) == head, value, jnp.zeros_like(value))


def attention_forward(packed, segments):
    cells, three = packed.shape
    width = three // 3
    size = width // HEADS
    pair = 128 // size
    steps = HEADS // pair

    def kernel(seg_col, seg_row, q_ref, k_ref, v_ref, out_ref, attn_ref):
        same = seg_col[...] == seg_row[...]
        queries, keys = q_ref[...], k_ref[...]
        values = jnp.transpose(v_ref[...])
        outs = []
        for head in range(pair):
            scores = right_product(head_lanes(keys, head, size), queries) * size ** (-0.5)
            scores = jnp.where(same, scores, NEGATIVE)
            powers = jnp.exp(scores - jnp.max(scores, axis=0, keepdims=True))
            attn = powers * (1.0 / jnp.sum(powers, axis=0, keepdims=True))
            attn_ref[head] = attn
            outs.append(matmul(values[head * size : (head + 1) * size], attn.astype(LOW)))
        out_ref[...] = jnp.transpose(jnp.concatenate(outs, axis=0)).astype(LOW)

    return pl.pallas_call(
        kernel,
        grid=(steps,),
        in_specs=[
            pl.BlockSpec((cells, 1), lambda i: (0, 0)),
            pl.BlockSpec((1, cells), lambda i: (0, 0)),
            pl.BlockSpec((cells, 128), lambda i: (0, i)),
            pl.BlockSpec((cells, 128), lambda i: (0, i + steps)),
            pl.BlockSpec((cells, 128), lambda i: (0, i + 2 * steps)),
        ],
        out_specs=[
            pl.BlockSpec((cells, 128), lambda i: (0, i)),
            pl.BlockSpec((pair, cells, cells), lambda i: (i, 0, 0)),
        ],
        out_shape=[
            jax.ShapeDtypeStruct((cells, width), LOW),
            jax.ShapeDtypeStruct((HEADS, cells, cells), FULL),
        ],
        compiler_params=pltpu.CompilerParams(vmem_limit_bytes=32 << 20),
        cost_estimate=pl.CostEstimate(
            flops=4 * cells * cells * width, bytes_accessed=24 << 20, transcendentals=cells * cells * HEADS
        ),
        name="attention_forward",
    )(segments[:, None], segments[None, :], packed, packed, packed)


def attention_backward(packed, attn, grad_mixed):
    cells, three = packed.shape
    width = three // 3
    size = width // HEADS
    pair = 128 // size
    steps = HEADS // pair

    def kernel(q_ref, k_ref, v_ref, g_ref, attn_ref, out_ref):
        queries, keys, values, grad = q_ref[...], k_ref[...], v_ref[...], g_ref[...]
        keys_t = jnp.transpose(keys)
        grad_q, grad_k, grad_v = [], 0.0, 0.0
        for head in range(pair):
            attn = attn_ref[head]
            grad_attn = right_product(head_lanes(values, head, size), grad)
            inner = jnp.sum(grad_attn * attn, axis=0, keepdims=True)
            grad_scores = (attn * (grad_attn - inner)).astype(LOW)
            grad_q.append(matmul(keys_t[head * size : (head + 1) * size], grad_scores))
            grad_k += head_lanes(matmul(grad_scores, queries), head, size)
            grad_v += head_lanes(matmul(attn.astype(LOW), grad), head, size)
        scale = size ** (-0.5)
        out_ref[0] = (jnp.transpose(jnp.concatenate(grad_q, axis=0)) * scale).astype(LOW)
        out_ref[1] = (grad_k * scale).astype(LOW)
        out_ref[2] = grad_v.astype(LOW)

    return pl.pallas_call(
        kernel,
        grid=(steps,),
        in_specs=[
            pl.BlockSpec((cells, 128), lambda i: (0, i)),
            pl.BlockSpec((cells, 128), lambda i: (0, i + steps)),
            pl.BlockSpec((cells, 128), lambda i: (0, i + 2 * steps)),
            pl.BlockSpec((cells, 128), lambda i: (0, i)),
            pl.BlockSpec((pair, cells, cells), lambda i: (i, 0, 0)),
        ],
        out_specs=pl.BlockSpec((3, cells, 128), lambda i: (0, 0, i)),
        out_shape=jax.ShapeDtypeStruct((3, cells, width), LOW),
        compiler_params=pltpu.CompilerParams(vmem_limit_bytes=32 << 20),
        cost_estimate=pl.CostEstimate(
            flops=10 * cells * cells * width, bytes_accessed=24 << 20, transcendentals=0
        ),
        name="attention_backward",
    )(packed, packed, packed, grad_mixed, attn)


def local(
    layer_ends,
    segment_ids,
    mixture,
    noise,
    plan_step,
    ln1_gain,
    w_qkv,
    w_out,
    ln2_gain,
    w_up,
    w_down,
    w_latent,
    w_decode,
    decode_bias,
    comp_mean,
    comp_logvar,
):
    core = lax.axis_index("pipe")
    cells = segment_ids.shape[1]
    devices = lax.axis_size("dp") * 2
    width = layer_ends.shape[2]
    latent = noise.shape[1]
    comps = comp_mean.shape[0]
    total_cells = cells * devices

    rows = w_qkv.shape[0]
    small = jnp.concatenate(
        [ln1_gain, ln2_gain, decode_bias, comp_mean.reshape(-1), comp_logvar.reshape(-1)]
    )
    small_count = small.shape[0]
    small = jnp.pad(small, (0, rows * 128 - small_count)).reshape(rows, 128)
    qkv_cols, out_cols, up_cols = w_qkv.shape[1], w_out.shape[1], w_up.shape[1]
    first_pieces = (
        (0, rows, 0, qkv_cols),
        (0, rows, qkv_cols, out_cols),
        (0, rows, qkv_cols + out_cols, 128),
    )
    up_pieces = ((0, rows, 0, up_cols),)
    down_rows, decode_rows = w_down.shape[0], w_decode.shape[0]
    down_pieces = ((0, down_rows, 0, width),)
    last_pieces = ((0, rows, 0, width), (rows, decode_rows, 0, width))
    qkv, out_proj, small_all = gather(
        jnp.concatenate([w_qkv, w_out, small], axis=1), first_pieces
    )
    (up,) = gather(w_up, up_pieces)
    (down,) = gather(w_down, down_pieces)
    to_latent, decode = gather(jnp.concatenate([w_latent, w_decode], axis=0), last_pieces)
    small_all = small_all.reshape(devices, rows * 128)
    piece = rows * 3
    gain_one = small_all[:, :rows].reshape(-1).astype(FULL)
    gain_two = small_all[:, rows : 2 * rows].reshape(-1).astype(FULL)
    bias = small_all[:, 2 * rows : 3 * rows].reshape(-1).astype(FULL)
    comp_cols = latent // devices

    def comp_table(start):
        flat = small_all[:, start : start + comps * comp_cols].reshape(devices, comps, comp_cols)
        return flat.transpose(1, 0, 2).reshape(comps, latent)

    means = comp_table(piece)
    spreads = comp_table(piece + comps * comp_cols)

    def my_rows(tensor, which):
        return lax.dynamic_slice_in_dim(tensor, which * cells, cells, axis=0)

    kept = my_rows(layer_ends[0], core)
    got = send_core(my_rows(layer_ends[0], 1 - core))
    inputs_low = jnp.where(core == 0, kept, got)
    cotangent = jnp.where(core == 0, got, kept)
    segments = lax.dynamic_index_in_dim(segment_ids, core, keepdims=False)
    mixture_rows = my_rows(mixture, core)
    noise_rows = my_rows(noise, core)

    inputs = inputs_low.astype(FULL)
    normed_one, scale_one = norm_parts(inputs)
    first_in = (normed_one * gain_one).astype(LOW)
    packed = matmul(first_in, qkv).astype(LOW)
    mixed, attn = attention_forward(packed, segments)
    middle = inputs + matmul(mixed, out_proj)
    normed_two, scale_two = norm_parts(middle)
    second_in = (normed_two * gain_two).astype(LOW)
    up_proj = matmul(second_in, up)
    gate = 0.5 * (1.0 + lax.erf(up_proj * (0.5**0.5)))
    hidden = (up_proj * gate).astype(LOW)
    slope = gate + up_proj * jnp.exp(-0.5 * up_proj * up_proj) * (0.5 / jnp.pi) ** 0.5
    carried = (middle + matmul(hidden, down)).astype(LOW)
    moments = matmul(carried, to_latent)
    mean_part, logvar = moments[:, :latent], moments[:, latent:]
    choose = mixture_rows[:, None] == jnp.arange(comps, dtype=jnp.int32)[None, :]
    centre = matmul(choose.astype(LOW), means)
    spread = matmul(choose.astype(LOW), spreads)
    deviation = jnp.exp(0.5 * logvar)
    sample = (mean_part + deviation * noise_rows).astype(LOW)
    gap = mean_part - centre
    shrink = jnp.exp(-spread)
    variance = jnp.exp(logvar)
    diverge = 0.5 * (spread - logvar + (variance + gap * gap) * shrink - 1.0)
    kl_sum = sum_everywhere(jnp.sum(diverge, axis=0))
    decoded = (matmul(sample, decode) + bias).astype(LOW)

    kl_weight = jnp.minimum(1.0, (plan_step[0] + 1).astype(FULL) / WARM)
    coef = kl_weight * jax.nn.sigmoid((kl_sum / total_cells - FREE_BITS) / SOFTNESS)
    grad_decode = left_product(sample, cotangent).astype(LOW)
    grad_bias = jnp.sum(cotangent.astype(FULL), axis=0)
    grad_sample = right_product(cotangent, decode)
    grad_centre = coef * (-(gap * shrink))
    grad_spread = coef * (1.0 - (variance + gap * gap) * shrink) * 0.5
    grad_mu = grad_sample - grad_centre
    grad_logvar = grad_sample * noise_rows * deviation * 0.5 + coef * (variance * shrink - 1.0) * 0.5
    grad_moments = jnp.concatenate([grad_mu, grad_logvar], axis=1).astype(LOW)
    chosen = choose.astype(FULL)
    table = (((0,), (0,)), ((), ()))
    grad_mean = lax.dot_general(chosen, grad_centre, table, precision=HIGHEST)
    grad_spreads = lax.dot_general(chosen, grad_spread, table, precision=HIGHEST)
    grad_latent = left_product(carried, grad_moments).astype(LOW)
    grad_carried = right_product(grad_moments, to_latent).astype(LOW)
    last_sum = scatter([grad_latent, grad_decode], last_pieces, rows + decode_rows)

    grad_down = left_product(hidden, grad_carried).astype(LOW)
    down_sum = scatter([grad_down], down_pieces, down_rows)
    grad_up_proj = (right_product(grad_carried, down) * slope).astype(LOW)
    grad_up = left_product(second_in, grad_up_proj).astype(LOW)
    up_sum = scatter([grad_up], up_pieces, rows)
    grad_second = right_product(grad_up_proj, up)
    grad_gain_two = jnp.sum(normed_two * grad_second, axis=0)
    grad_middle = grad_carried.astype(FULL) + norm_back(normed_two, scale_two, grad_second, gain_two)
    grad_branch = grad_middle.astype(LOW)
    grad_out = left_product(mixed, grad_branch).astype(LOW)
    grad_mixed = right_product(grad_branch, out_proj).astype(LOW)
    grad_packed = attention_backward(packed, attn, grad_mixed)
    grad_packed = jnp.concatenate([grad_packed[0], grad_packed[1], grad_packed[2]], axis=1)
    grad_qkv = left_product(first_in, grad_packed).astype(LOW)
    grad_first = right_product(grad_packed, qkv)
    grad_gain_one = jnp.sum(normed_one * grad_first, axis=0)
    grad_inputs = grad_middle + norm_back(normed_one, scale_one, grad_first, gain_one)

    def comp_rows(tensor):
        return tensor.reshape(comps, devices, comp_cols).transpose(1, 0, 2).reshape(devices, -1)

    small_grads = jnp.concatenate(
        [
            grad_gain_one.reshape(devices, rows),
            grad_gain_two.reshape(devices, rows),
            grad_bias.reshape(devices, rows),
            comp_rows(grad_mean),
            comp_rows(grad_spreads),
        ],
        axis=1,
    )
    small_grads = jnp.pad(small_grads, ((0, 0), (0, rows * 128 - small_count)))
    small_grads = small_grads.astype(LOW).reshape(devices * rows, 128)
    first_sum = scatter([grad_qkv, grad_out, small_grads], first_pieces, rows)

    decoded_there = send_core(decoded)
    inputs_there = send_core(grad_inputs)
    result = jnp.where(
        core == 0,
        jnp.concatenate([grad_inputs, inputs_there], axis=0),
        jnp.concatenate([decoded_there, decoded], axis=0).astype(FULL),
    )[None]
    small_sum = first_sum[:, qkv_cols + out_cols :].reshape(-1)
    comp_size = comps * comp_cols
    return (
        result,
        small_sum[:rows],
        first_sum[:, :qkv_cols],
        first_sum[:, qkv_cols : qkv_cols + out_cols],
        small_sum[rows : 2 * rows],
        up_sum,
        down_sum,
        last_sum[:rows],
        last_sum[rows:],
        small_sum[2 * rows : 3 * rows],
        small_sum[piece : piece + comp_size].reshape(comps, comp_cols),
        small_sum[piece + comp_size : piece + 2 * comp_size].reshape(comps, comp_cols),
    )


def solution(mesh):
    split = P(EVERY)
    wide = P(EVERY, None)
    tall = P(None, EVERY)
    ends = P("pipe", "dp", None)
    return jax.shard_map(
        local,
        mesh=mesh,
        in_specs=(
            ends,
            P("dp", None),
            P("dp"),
            P("dp", None),
            P(),
            split,
            wide,
            wide,
            split,
            wide,
            wide,
            wide,
            wide,
            split,
            tall,
            tall,
        ),
        out_specs=(ends, split, wide, wide, split, wide, wide, wide, wide, split, tall, tall),
        check_vma=False,
    )
```

time: 2240 us -> 652 us (0.29)
  waiting for transfers between devices: 1420 us -> 278 us
  matrix products: 433 us -> 87.6 us
  blocking collectives: 194 us -> 0 us
  Pallas kernels: 0 us -> 95.4 us
  starting transfers between devices: 7.66 us -> 70.1 us
  loops' own time: 23.4 us -> 0 us
    reduce_scatter x6 -> x0, waiting for transfers between devices: 959 us -> none  [the longest x1 187 us: local(): lax.psum_scatter(grad_down, ('dp', 'pipe'), scatter_dimension=0, tiled=True)]
    ppermute x4 -> x60, waiting for transfers between devices: 23.4 us -> 278 us  [send(): return lax.ppermute(value, EVERY, pairs)]
    all_gather x6 -> x0, waiting for transfers between devices: 243 us -> none  [the longest x1 78.9 us: local(): lax.all_gather(w_up, ('dp', 'pipe'), axis=0, tiled=True)]
    unnamed x16 -> x0, waiting for transfers between devices: 197 us -> none
    dot_general x24 -> x10, matrix products: 191 us -> 29.9 us  [the longest x8 26.7 us: matmul(): return jnp.dot(left_side, right_side, preferred_element_type=FULL)]
    pallas_call x0 -> x10, Pallas kernels: none -> 95.4 us  [the longest x4 36.6 us: unpack(): pl.pallas_call(kernel, out_shape=[jax.ShapeDtypeStruct(shape, LOW) for sh...]
    dot_general x8 -> x6, matrix products: 116 us -> 23.8 us  [left_product(): lax.dot_general(left_side, right_side, (((0,), (0,)), ((), ())), preferre...]
    unnamed x2 -> x0, blocking collectives: 85.6 us -> none
  transfers between devices with their start and end apart: 18 -> 60, of which waited for: 15 -> 27; matrix products, arithmetic and copies ran while one was open for 4% -> 12% of each run, Pallas kernels for 0% -> 6%
where the time goes in v1:
time: 652 us; the launch traced here: 642 us
  waiting for transfers between devices  278 us (43%)
  Pallas kernels  95.4 us (15%)
  matrix products  87.6 us (13%)
  starting transfers between devices  70.1 us (11%)
  local copies, waits for them, and re-layouts  69 us (11%)
  other arithmetic  39.5 us (6%)
    ppermute x60, waiting for transfers between devices, send(): return lax.ppermute(value, EVERY, pairs)  278 us
    ppermute x60, starting transfers between devices, send(): return lax.ppermute(value, EVERY, pairs)  70.1 us
    unnamed x186, local copies, waits for them, and re-layouts  54 us
    pallas_call x4, Pallas kernels, unpack(): pl.pallas_call(kernel, out_shape=[jax.ShapeDtypeStruct(shape, LOW) for sh...  36.6 us
    dot_general x6, matrix products, right_product(): lax.dot_general(left_side, right_side, (((1,), (1,)), ((), ())), preferre...  33.9 us
    pallas_call x4, Pallas kernels, pack(): pl.pallas_call(kernel, out_shape=[jax.ShapeDtypeStruct((count, rows, cols...  27.4 us
    dot_general x8, matrix products, matmul(): return jnp.dot(left_side, right_side, preferred_element_type=FULL)  26.7 us
    dot_general x6, matrix products, left_product(): lax.dot_general(left_side, right_side, (((0,), (0,)), ((), ())), preferre...  23.8 us
  transfers between devices with their start and end apart: 60, of which 27 were waited for; matrix products, arithmetic and copies ran while one was open for 12% of the time, Pallas kernels for 6%

profile of v1, /device:TPU:8, one launch (start us, length us, event | category | flops | bytes accessed | tf_op | source)
XLA Modules:
  0.0 642.5 jit_solution(940007748249350880)
XLA Ops:
  32.9 7.4 %collective-permute-done.17 = bf16[1,32,4096]{2,1,0:T(8,128)(2,1)} collective-permute-done((bf16[1,32,4096]{2,1,0:T(8,128)(2,1)}, bf16[1,32,4096]{2,1,0:T(8,128)(2,1)}, u32[]{:S(2)}, u32[]{:S(2)}) %collective-permute-start.17) | collective-permute-done | bytes 262176 | tf_op jit(solution)/shard_map/ppermute | solution.py:32
  43.3 12.0 %collective-permute-done.16 = bf16[1,32,4096]{2,1,0:T(8,128)(2,1)} collective-permute-done((bf16[1,32,4096]{2,1,0:T(8,128)(2,1)}, bf16[1,32,4096]{2,1,0:T(8,128)(2,1)}, u32[]{:S(2)}, u32[]{:S(2)}) %collective-permute-start.16) | collective-permute-done | bytes 262176 | tf_op jit(solution)/shard_map/ppermute | solution.py:32
  84.4 17.5 %collective-permute-done.25 = bf16[4,128,1024]{2,1,0:T(8,128)(2,1)S(1)} collective-permute-done((bf16[4,128,1024]{2,1,0:T(8,128)(2,1)S(1)}, bf16[4,128,1024]{2,1,0:T(8,128)(2,1)S(1)}, u32[]{:S(2)}, u32[]{:S(2)}) %collective-permute-start.25) | collective-permute-done | bytes 1048608 | tf_op jit(solution)/shard_map/ppermute | solution.py:32
  102.1 11.4 %collective-permute-done.11 = bf16[4,32,4224]{2,1,0:T(8,128)(2,1)S(1)} collective-permute-done((bf16[4,32,4224]{2,1,0:T(8,128)(2,1)S(1)}, bf16[4,32,4224]{2,1,0:T(8,128)(2,1)S(1)}, u32[]{:S(2)}, u32[]{:S(2)}) %collective-permute-start.11) | collective-permute-done | bytes 1081376 | tf_op jit(solution)/shard_map/ppermute | solution.py:32
  120.6 72.9 %collective-permute-done.5.own_b = bf16[8,48,1024]{2,1,0:T(8,128)(2,1)S(1)} collective-permute-done((bf16[8,48,1024]{2,1,0:T(8,128)(2,1)S(1)}, bf16[8,48,1024]{2,1,0:T(8,128)(2,1)S(1)}, u32[]{:S(2)}, u32[]{:S(2)}) %collective-permute-start.5) | collective-permute-done | bytes 786464 | tf_op jit(solution)/shard_map/ppermute | solution.py:32
  201.9 11.6 %unpack.4 = (bf16[16,2,32,1024]{3,2,1,0:T(8,128)(2,1)S(1)}, bf16[16,2,16,1024]{3,2,1,0:T(8,128)(2,1)S(1)}) custom-call(s32[2]{0:T(128)S(1)} %pad_add_fusion.place_ref, bf16[8,48,1024]{2,1,0:T(8,128)(2,1)S(1)} %constant_dynamic-update-slice_fusion.own_a, bf16[8,48,1024]{2,1,0:T(8,128)(2,1)S(1)} %copy-done.23, bf16[8,48,1024]{2,1,0:T(8,128)(2,1)S(1)} %copy-done.21, ...), custom_call_target="tpu_custom_call" | custom-call | bytes 6291456 | tf_op jit(solution)/shard_map/unpack/pallas_call | solution.py:106
  230.7 16.8 %unpack.5 = (bf16[16,2,32,3072]{3,2,1,0:T(8,128)(2,1)S(1)}, bf16[16,2,32,1024]{3,2,1,0:T(8,128)(2,1)S(1)}, bf16[16,2,32,128]{3,2,1,0:T(8,128)(2,1)S(1)}) custom-call(s32[2]{0:T(128)S(1)} %pad_add_fusion.place_ref, bf16[8,32,4224]{2,1,0:T(8,128)(2,1)} %constant_dynamic-update-slice_fusion.5.own_a, bf16[8,32,4224]{2,1,0:T(8,128)(2,1)} %collective-permute-done.12.own_b, ...), custom_call_target="tpu_custom_call" | custom-call | bytes 17301504 | tf_op jit(solution)/shard_map/unpack/pallas_call | solution.py:106
  259.4 13.6 %attention_forward.1 = (bf16[512,1024]{1,0:T(8,128)(2,1)S(1)}, f32[16,512,512]{2,1,0:T(8,128)S(1)}) custom-call(s32[512,1]{1,0:T(8,128)S(1)} %copy.69.seg_col, s32[1,512]{1,0:T(1,128)S(1)} %constant_dynamic-slice_fusion.1.seg_row, bf16[512,3072]{1,0:T(8,128)(2,1)S(1)} %convolution_convert_fusion.3.q_ref.k_ref.v_ref, ...), custom_call_target="tpu_custom_call" | custom-call | flops 1073741824 | bytes 25165824 | tf_op jit(solution)/shard_map/attention_forward/pallas_call | solution.py:270
  282.0 8.8 %multiply_convert_fusion = (bf16[512,4096]{1,0:T(8,128)(2,1)S(1)}, f32[512,4096]{1,0:T(8,128)}) fusion(bf16[1024,4096]{1,0:T(8,128)(2,1)S(1)} %bitcast.115, f32[512,1024]{1,0:T(8,128)S(1)} %get-tuple-element.99, f32[1024]{0:T(1024)S(1)} %reshape.306, f32[512]{0:T(512)S(1)} %add_rsqrt_fusion, f32[512]{0:T(512)S(1)} %broadcast_multiply_fusion.4), kind=kOutput, calls=%fused_computation.7 | convolution fusion | flops 4307550208 | bytes 23076864 | tf_op jit(solution)/shard_map/dot_general | solution.py:214
  329.2 10.8 %fusion.5 = bf16[512,4096]{1,0:T(8,128)(2,1)} fusion(f32[512,4096]{1,0:T(8,128)} %get-tuple-element.101, bf16[512,1024]{1,0:T(8,128)(2,1)} %convolution_convert_fusion.7, bf16[4096,1024]{1,0:T(8,128)(2,1)S(1)} %bitcast.112), kind=kOutput, calls=%fused_computation.6 | convolution fusion | flops 4315938816 | bytes 22020096 | tf_op jit(solution)/shard_map/dot_general | solution.py:224
  340.1 7.1 %multiply_reduce_fusion = (bf16[1024]{0:T(1024)(128)(2,1)S(1)}, f32[512]{0:T(512)S(1)}, f32[512]{0:T(512)S(1)}, f32[512,1024]{1,0:T(8,128)S(1)}) fusion(f32[512,1024]{1,0:T(8,128)S(1)} %copy-done.47, f32[512]{0:T(512)S(1)} %add_rsqrt_fusion, f32[512]{0:T(512)S(1)} %broadcast_multiply_fusion.4, f32[1024]{0:T(1024)S(1)} %reshape.306, ...), kind=kOutput, calls=%fused_computation.46 | convolution fusion | flops 4299159552 | bytes 16791552 | tf_op jit(solution)/shard_map/dot_general | solution.py:224
  355.1 7.3 %convolution_convert_fusion.1 = bf16[1024,4096]{1,0:T(8,128)(2,1)} fusion(bf16[512,4096]{1,0:T(8,128)(2,1)S(1)} %copy-done.72, f32[512,1024]{1,0:T(8,128)S(1)} %copy-done.48, f32[1024]{0:T(1024)S(1)} %reshape.306, f32[512]{0:T(512)S(1)} %add_rsqrt_fusion, f32[512]{0:T(512)S(1)} %broadcast_multiply_fusion.4), kind=kOutput, calls=%fused_computation.10 | convolution fusion | flops 4301258752 | bytes 14688256 | tf_op jit(solution)/shard_map/dot_general | solution.py:218
  362.4 7.3 %convolution_convert_fusion = bf16[4096,1024]{1,0:T(8,128)(2,1)S(1)} fusion(bf16[512,4096]{1,0:T(8,128)(2,1)} %copy-done.71, bf16[512,1024]{1,0:T(8,128)(2,1)S(1)} %copy-done.58), kind=kOutput, calls=%fused_computation.9 | convolution fusion | flops 4299161600 | bytes 13631488 | tf_op jit(solution)/shard_map/dot_general | solution.py:218
  370.5 17.9 %attention_backward.1 = bf16[3,512,1024]{2,1,0:T(8,128)(2,1)S(1)} custom-call(bf16[512,3072]{1,0:T(8,128)(2,1)S(1)} %copy-done.3, bf16[512,3072]{1,0:T(8,128)(2,1)S(1)} %copy-done.3, bf16[512,3072]{1,0:T(8,128)(2,1)S(1)} %copy-done.3, bf16[512,1024]{1,0:T(8,128)(2,1)S(1)} %convolution_convert_fusion.6.g_ref, f32[16,512,512]{2,1,0:T(8,128)} %copy-done.4), custom_call_target="tpu_custom_call" | custom-call | flops 2684354560 | bytes 25165824 | tf_op jit(solution)/shard_map/attention_backward/pallas_call | solution.py:320
  388.7 9.6 %pack.7 = (bf16[16,48,1024]{2,1,0:T(8,128)(2,1)S(1)}, bf16[16,48,1024]{2,1,0:T(8,128)(2,1)}) custom-call(s32[2]{0:T(128)S(1)} %pad_add_fusion.place_ref, bf16[16,2,32,1024]{3,2,1,0:T(8,128)(2,1)S(1)} %bitcast.125, bf16[16,2,16,1024]{3,2,1,0:T(8,128)(2,1)S(1)} %bitcast.127), custom_call_target="tpu_custom_call" | custom-call | bytes 6291456 | tf_op jit(solution)/shard_map/pack/pallas_call | solution.py:145
  406.2 8.0 %fusion.17 = (bf16[1024]{0:T(1024)(128)(2,1)S(1)}, f32[512]{0:T(512)S(1)}, f32[512]{0:T(512)S(1)}, f32[512,1024]{1,0:T(8,128)}) fusion(bf16[512,1024]{1,0:T(8,128)(2,1)S(1)} %copy-done.42, f32[512]{0:T(512)S(1)} %add_rsqrt_fusion.1, f32[512]{0:T(512)S(1)} %broadcast_multiply_fusion.5, f32[1024]{0:T(1024)S(1)} %reshape.305, ...), kind=kOutput, calls=%fused_computation.38 | convolution fusion | flops 3235379200 | bytes 12597248 | tf_op jit(solution)/shard_map/dot_general | solution.py:224
  431.9 9.1 %pack.4 = (bf16[16,32,4224]{2,1,0:T(8,128)(2,1)S(1)}, bf16[16,32,4224]{2,1,0:T(8,128)(2,1)}) custom-call(s32[2]{0:T(128)S(1)} %pad_add_fusion.place_ref, bf16[16,2,32,3072]{3,2,1,0:T(8,128)(2,1)S(1)} %bitcast.121, bf16[16,2,32,1024]{3,2,1,0:T(8,128)(2,1)S(1)} %bitcast.124, bf16[16,2,32,128]{3,2,1,0:T(8,128)(2,1)S(1)} %bitcast.126), custom_call_target="tpu_custom_call" | custom-call | bytes 17301504 | tf_op jit(solution)/shard_map/pack/pallas_call | solution.py:145
  450.3 8.7 %collective-permute-done.55 = bf16[8,48,1024]{2,1,0:T(8,128)(2,1)} collective-permute-done((bf16[8,48,1024]{2,1,0:T(8,128)(2,1)}, bf16[8,48,1024]{2,1,0:T(8,128)(2,1)}, u32[]{:S(2)}, u32[]{:S(2)}) %collective-permute-start.55) | collective-permute-done | bytes 786464 | tf_op jit(solution)/shard_map/ppermute | solution.py:32
  501.4 31.7 %collective-permute-done.43 = bf16[8,32,4096]{2,1,0:T(8,128)(2,1)S(1)} collective-permute-done((bf16[8,32,4096]{2,1,0:T(8,128)(2,1)S(1)}, bf16[8,32,4096]{2,1,0:T(8,128)(2,1)S(1)}, u32[]{:S(2)}, u32[]{:S(2)}) %collective-permute-start.43) | collective-permute-done | bytes 2097184 | tf_op jit(solution)/shard_map/ppermute | solution.py:32
  534.9 32.6 %collective-permute-done.37 = bf16[8,32,4224]{2,1,0:T(8,128)(2,1)S(1)} collective-permute-done((bf16[8,32,4224]{2,1,0:T(8,128)(2,1)S(1)}, bf16[8,32,4224]{2,1,0:T(8,128)(2,1)S(1)}, u32[]{:S(2)}, u32[]{:S(2)}) %collective-permute-start.37) | collective-permute-done | bytes 2162720 | tf_op jit(solution)/shard_map/ppermute | solution.py:32
  575.7 7.3 %collective-permute-done.38 = bf16[4,32,4224]{2,1,0:T(8,128)(2,1)S(1)} collective-permute-done((bf16[4,32,4224]{2,1,0:T(8,128)(2,1)S(1)}, bf16[4,32,4224]{2,1,0:T(8,128)(2,1)S(1)}, u32[]{:S(2)}, u32[]{:S(2)}) %collective-permute-start.38) | collective-permute-done | bytes 1081376 | tf_op jit(solution)/shard_map/ppermute | solution.py:32
  592.9 16.2 %collective-permute-done.47 = bf16[1,32,4096]{2,1,0:T(8,128)(2,1)S(1)} collective-permute-done((bf16[1,32,4096]{2,1,0:T(8,128)(2,1)S(1)}, bf16[1,32,4096]{2,1,0:T(8,128)(2,1)S(1)}, u32[]{:S(2)}, u32[]{:S(2)}) %collective-permute-start.47) | collective-permute-done | bytes 262176 | tf_op jit(solution)/shard_map/ppermute | solution.py:32
  619.6 10.2 %collective-permute-done.52 = bf16[1,128,1024]{2,1,0:T(8,128)(2,1)S(1)} collective-permute-done((bf16[1,128,1024]{2,1,0:T(8,128)(2,1)S(1)}, bf16[1,128,1024]{2,1,0:T(8,128)(2,1)S(1)}, u32[]{:S(2)}, u32[]{:S(2)}) %collective-permute-start.52) | collective-permute-done | bytes 262176 | tf_op jit(solution)/shard_map/ppermute | solution.py:32
  630.8 7.0 %collective-permute-done.41 = bf16[1,32,4224]{2,1,0:T(8,128)(2,1)S(1)} collective-permute-done((bf16[1,32,4224]{2,1,0:T(8,128)(2,1)S(1)}, bf16[1,32,4224]{2,1,0:T(8,128)(2,1)S(1)}, u32[]{:S(2)}, u32[]{:S(2)}) %collective-permute-start.41) | collective-permute-done | bytes 270368 | tf_op jit(solution)/shard_map/ppermute | solution.py:32
  (409 shorter events, 276.8 us)
Async XLA Ops:
  5.7 34.5 %collective-permute-start.17 = (bf16[1,32,4096]{2,1,0:T(8,128)(2,1)}, bf16[1,32,4096]{2,1,0:T(8,128)(2,1)}, u32[]{:S(2)}, u32[]{:S(2)}) collective-permute-start(bf16[1,32,4096]{2,1,0:T(8,128)(2,1)} %bitcast.139), channel_id=1, source_target_pairs={{0,24},{1,25},{2,26},{3,27},{4,28},{5,29},{6,30},{7,31},{8,16},{9,... | collective-permute-start | bytes 786440 | tf_op jit(solution)/shard_map/ppermute | solution.py:32
  7.2 48.1 %collective-permute-start.16 = (bf16[1,32,4096]{2,1,0:T(8,128)(2,1)}, bf16[1,32,4096]{2,1,0:T(8,128)(2,1)}, u32[]{:S(2)}, u32[]{:S(2)}) collective-permute-start(bf16[1,32,4096]{2,1,0:T(8,128)(2,1)} %bitcast.140), channel_id=1, source_target_pairs={{0,16},{1,17},{2,18},{3,19},{4,20},{5,21},{6,22},{7,23},{8,24},{9,... | collective-permute-start | bytes 786440 | tf_op jit(solution)/shard_map/ppermute | solution.py:32
  23.7 45.8 %collective-permute-start.24 = (bf16[1,128,1024]{2,1,0:T(8,128)(2,1)}, bf16[1,128,1024]{2,1,0:T(8,128)(2,1)S(1)}, u32[]{:S(2)}, u32[]{:S(2)}) collective-permute-start(bf16[1,128,1024]{2,1,0:T(8,128)(2,1)} %bitcast.143), channel_id=1, source_target_pairs={{0,24},{1,25},{2,26},{3,27},{4,28},{5,29},{6,30},{7,31},{8,16},{9,... | collective-permute-start | bytes 786440 | tf_op jit(solution)/shard_map/ppermute | solution.py:32
  25.5 44.0 %collective-permute-start.23 = (bf16[1,128,1024]{2,1,0:T(8,128)(2,1)}, bf16[1,128,1024]{2,1,0:T(8,128)(2,1)S(1)}, u32[]{:S(2)}, u32[]{:S(2)}) collective-permute-start(bf16[1,128,1024]{2,1,0:T(8,128)(2,1)} %bitcast.144), channel_id=1, source_target_pairs={{0,16},{1,17},{2,18},{3,19},{4,20},{5,21},{6,22},{7,23},{8,24},{9,... | collective-permute-start | bytes 786440 | tf_op jit(solution)/shard_map/ppermute | solution.py:32
  40.3 35.6 %collective-permute-start.10 = (bf16[1,32,4224]{2,1,0:T(8,128)(2,1)S(1)}, bf16[1,32,4224]{2,1,0:T(8,128)(2,1)S(1)}, u32[]{:S(2)}, u32[]{:S(2)}) collective-permute-start(bf16[1,32,4224]{2,1,0:T(8,128)(2,1)S(1)} %maximum_bitcast_fusion), channel_id=1, source_target_pairs={{0,24},{1,25},{2,26},{3,27},{4,28},{5,29},{6,30},{7,31},{8,16},{9,... | collective-permute-start | bytes 811016 | tf_op jit(solution)/shard_map/ppermute | solution.py:32
  69.4 48.2 %collective-permute-start = (bf16[512,1024]{1,0:T(8,128)(2,1)S(1)}, bf16[512,1024]{1,0:T(8,128)(2,1)S(1)}, u32[]{:S(2)}, u32[]{:S(2)}) collective-permute-start(bf16[512,1024]{1,0:T(8,128)(2,1)S(1)} %dynamic-slice_bitcast_fusion), channel_id=1, source_target_pairs={{0,1},{1,0},{2,3},{3,2},{4,5},{5,4},{6,7},{7,6},{8,9},{9,8},{10,11... | collective-permute-start | bytes 3145736 | tf_op jit(solution)/shard_map/ppermute | solution.py:32
  75.9 40.2 %collective-permute-start.18 = (bf16[4,32,4096]{2,1,0:T(8,128)(2,1)S(1)}, bf16[4,32,4096]{2,1,0:T(8,128)(2,1)S(1)}, u32[]{:S(2)}, u32[]{:S(2)}) collective-permute-start(bf16[4,32,4096]{2,1,0:T(8,128)(2,1)S(1)} %pad_maximum_fusion.4), channel_id=1, source_target_pairs={{0,2},{1,5},{2,0},{3,7},{4,6},{5,1},{6,4},{7,3},{8,10},{9,13},{10,... | collective-permute-start | bytes 3145736 | tf_op jit(solution)/shard_map/ppermute | solution.py:32
  84.3 34.9 %collective-permute-start.6 = (bf16[8,48,1024]{2,1,0:T(8,128)(2,1)S(1)}, bf16[8,48,1024]{2,1,0:T(8,128)(2,1)S(1)}, u32[]{:S(2)}, u32[]{:S(2)}) collective-permute-start(bf16[8,48,1024]{2,1,0:T(8,128)(2,1)S(1)} %constant_dynamic-update-slice_fusion.own_a), channel_id=1, source_target_pairs={{0,1},{1,0},{2,3},{3,2},{4,5},{5,4},{6,7},{7,6},{8,9},{9,8},{10,11... | collective-permute-start | bytes 2359304 | tf_op jit(solution)/shard_map/ppermute | solution.py:32
  102.0 95.4 %collective-permute-start.27 = (bf16[8,128,1024]{2,1,0:T(8,128)(2,1)S(1)}, bf16[8,128,1024]{2,1,0:T(8,128)(2,1)S(1)}, u32[]{:S(2)}, u32[]{:S(2)}) collective-permute-start(bf16[8,128,1024]{2,1,0:T(8,128)(2,1)S(1)} %constant_dynamic-update-slice_fusion.15.own_a), channel_id=1, source_target_pairs={{0,1},{1,0},{2,3},{3,2},{4,5},{5,4},{6,7},{7,6},{8,9},{9,8},{10,11... | collective-permute-start | bytes 6291464 | tf_op jit(solution)/shard_map/ppermute | solution.py:32
  113.5 83.8 %collective-permute-start.26 = (bf16[8,128,1024]{2,1,0:T(8,128)(2,1)S(1)}, bf16[8,128,1024]{2,1,0:T(8,128)(2,1)}, u32[]{:S(2)}, u32[]{:S(2)}) collective-permute-start(bf16[8,128,1024]{2,1,0:T(8,128)(2,1)S(1)} %constant_dynamic-update-slice_fusion.15.own_a), channel_id=1, source_target_pairs={{0,4},{1,3},{2,6},{3,1},{4,0},{5,7},{6,2},{7,5},{8,12},{9,11},{10,... | collective-permute-start | bytes 6291464 | tf_op jit(solution)/shard_map/ppermute | solution.py:32
  116.1 80.8 %collective-permute-start.12 = (bf16[8,32,4224]{2,1,0:T(8,128)(2,1)}, bf16[8,32,4224]{2,1,0:T(8,128)(2,1)}, u32[]{:S(2)}, u32[]{:S(2)}) collective-permute-start(bf16[8,32,4224]{2,1,0:T(8,128)(2,1)} %constant_dynamic-update-slice_fusion.5.own_a), channel_id=1, source_target_pairs={{0,4},{1,3},{2,6},{3,1},{4,0},{5,7},{6,2},{7,5},{8,12},{9,11},{10,... | collective-permute-start | bytes 6488072 | tf_op jit(solution)/shard_map/ppermute | solution.py:32
  117.7 81.5 %collective-permute-start.19 = (bf16[8,32,4096]{2,1,0:T(8,128)(2,1)}, bf16[8,32,4096]{2,1,0:T(8,128)(2,1)}, u32[]{:S(2)}, u32[]{:S(2)}) collective-permute-start(bf16[8,32,4096]{2,1,0:T(8,128)(2,1)} %constant_dynamic-update-slice_fusion.10.own_a), channel_id=1, source_target_pairs={{0,4},{1,3},{2,6},{3,1},{4,0},{5,7},{6,2},{7,5},{8,12},{9,11},{10,... | collective-permute-start | bytes 6291464 | tf_op jit(solution)/shard_map/ppermute | solution.py:32
  120.1 73.5 %collective-permute-start.5 = (bf16[8,48,1024]{2,1,0:T(8,128)(2,1)S(1)}, bf16[8,48,1024]{2,1,0:T(8,128)(2,1)S(1)}, u32[]{:S(2)}, u32[]{:S(2)}) collective-permute-start(bf16[8,48,1024]{2,1,0:T(8,128)(2,1)S(1)} %constant_dynamic-update-slice_fusion.own_a), channel_id=1, source_target_pairs={{0,4},{1,3},{2,6},{3,1},{4,0},{5,7},{6,2},{7,5},{8,12},{9,11},{10,... | collective-permute-start | bytes 2359304 | tf_op jit(solution)/shard_map/ppermute | solution.py:32
  399.5 44.1 %collective-permute-start.54 = (bf16[16,48,1024]{2,1,0:T(8,128)(2,1)}, bf16[16,48,1024]{2,1,0:T(8,128)(2,1)}, u32[]{:S(2)}, u32[]{:S(2)}) collective-permute-start(bf16[16,48,1024]{2,1,0:T(8,128)(2,1)} %get-tuple-element.41), channel_id=1, source_target_pairs={{0,1},{1,0},{2,3},{3,2},{4,5},{5,4},{6,7},{7,6},{8,9},{9,8},{10,11... | collective-permute-start | bytes 4718600 | tf_op jit(solution)/shard_map/ppermute | solution.py:32
  405.7 63.5 %collective-permute-start.48 = (bf16[16,128,1024]{2,1,0:T(8,128)(2,1)}, bf16[16,128,1024]{2,1,0:T(8,128)(2,1)}, u32[]{:S(2)}, u32[]{:S(2)}) collective-permute-start(bf16[16,128,1024]{2,1,0:T(8,128)(2,1)} %get-tuple-element.39), channel_id=1, source_target_pairs={{0,1},{1,0},{2,3},{3,2},{4,5},{5,4},{6,7},{7,6},{8,9},{9,8},{10,11... | collective-permute-start | bytes 12582920 | tf_op jit(solution)/shard_map/ppermute | solution.py:32
  425.9 47.4 %collective-permute-start.42 = (bf16[16,32,4096]{2,1,0:T(8,128)(2,1)}, bf16[16,32,4096]{2,1,0:T(8,128)(2,1)}, u32[]{:S(2)}, u32[]{:S(2)}) collective-permute-start(bf16[16,32,4096]{2,1,0:T(8,128)(2,1)} %get-tuple-element.37), channel_id=1, source_target_pairs={{0,1},{1,0},{2,3},{3,2},{4,5},{5,4},{6,7},{7,6},{8,9},{9,8},{10,11... | collective-permute-start | bytes 12582920 | tf_op jit(solution)/shard_map/ppermute | solution.py:32
  443.2 34.9 %collective-permute-start.36 = (bf16[16,32,4224]{2,1,0:T(8,128)(2,1)}, bf16[16,32,4224]{2,1,0:T(8,128)(2,1)}, u32[]{:S(2)}, u32[]{:S(2)}) collective-permute-start(bf16[16,32,4224]{2,1,0:T(8,128)(2,1)} %get-tuple-element.35), channel_id=1, source_target_pairs={{0,1},{1,0},{2,3},{3,2},{4,5},{5,4},{6,7},{7,6},{8,9},{9,8},{10,11... | collective-permute-start | bytes 12976136 | tf_op jit(solution)/shard_map/ppermute | solution.py:32
  478.0 55.1 %collective-permute-start.43 = (bf16[8,32,4096]{2,1,0:T(8,128)(2,1)S(1)}, bf16[8,32,4096]{2,1,0:T(8,128)(2,1)S(1)}, u32[]{:S(2)}, u32[]{:S(2)}) collective-permute-start(bf16[8,32,4096]{2,1,0:T(8,128)(2,1)S(1)} %get-tuple-element.65), channel_id=1, source_target_pairs={{0,4},{1,3},{2,6},{3,1},{4,0},{5,7},{6,2},{7,5},{8,12},{9,11},{10,... | collective-permute-start | bytes 6291464 | tf_op jit(solution)/shard_map/ppermute | solution.py:32
  485.7 81.8 %collective-permute-start.37 = (bf16[8,32,4224]{2,1,0:T(8,128)(2,1)S(1)}, bf16[8,32,4224]{2,1,0:T(8,128)(2,1)S(1)}, u32[]{:S(2)}, u32[]{:S(2)}) collective-permute-start(bf16[8,32,4224]{2,1,0:T(8,128)(2,1)S(1)} %get-tuple-element.61), channel_id=1, source_target_pairs={{0,4},{1,3},{2,6},{3,1},{4,0},{5,7},{6,2},{7,5},{8,12},{9,11},{10,... | collective-permute-start | bytes 6488072 | tf_op jit(solution)/shard_map/ppermute | solution.py:32
  499.8 69.5 %collective-permute-start.50 = (bf16[4,128,1024]{2,1,0:T(8,128)(2,1)S(1)}, bf16[4,128,1024]{2,1,0:T(8,128)(2,1)S(1)}, u32[]{:S(2)}, u32[]{:S(2)}) collective-permute-start(bf16[4,128,1024]{2,1,0:T(8,128)(2,1)S(1)} %add_convert_fusion.8), channel_id=1, source_target_pairs={{0,2},{1,5},{2,0},{3,7},{4,6},{5,1},{6,4},{7,3},{8,10},{9,13},{10,... | collective-permute-start | bytes 3145736 | tf_op jit(solution)/shard_map/ppermute | solution.py:32
  533.3 38.8 %collective-permute-start.44 = (bf16[4,32,4096]{2,1,0:T(8,128)(2,1)S(1)}, bf16[4,32,4096]{2,1,0:T(8,128)(2,1)S(1)}, u32[]{:S(2)}, u32[]{:S(2)}) collective-permute-start(bf16[4,32,4096]{2,1,0:T(8,128)(2,1)S(1)} %add_convert_fusion.10), channel_id=1, source_target_pairs={{0,2},{1,5},{2,0},{3,7},{4,6},{5,1},{6,4},{7,3},{8,10},{9,13},{10,... | collective-permute-start | bytes 3145736 | tf_op jit(solution)/shard_map/ppermute | solution.py:32
  570.1 45.2 %collective-permute-start.51 = (bf16[1,128,1024]{2,1,0:T(8,128)(2,1)S(1)}, bf16[1,128,1024]{2,1,0:T(8,128)(2,1)S(1)}, u32[]{:S(2)}, u32[]{:S(2)}) collective-permute-start(bf16[1,128,1024]{2,1,0:T(8,128)(2,1)S(1)} %get-tuple-element.77), channel_id=1, source_target_pairs={{0,8},{1,9},{2,10},{3,11},{4,12},{5,13},{6,14},{7,15},{8,0},{9,1},... | collective-permute-start | bytes 786440 | tf_op jit(solution)/shard_map/ppermute | solution.py:32
  571.8 47.8 %collective-permute-start.53 = (bf16[1,128,1024]{2,1,0:T(8,128)(2,1)S(1)}, bf16[1,128,1024]{2,1,0:T(8,128)(2,1)S(1)}, u32[]{:S(2)}, u32[]{:S(2)}) collective-permute-start(bf16[1,128,1024]{2,1,0:T(8,128)(2,1)S(1)} %get-tuple-element.78), channel_id=1, source_target_pairs={{0,24},{1,25},{2,26},{3,27},{4,28},{5,29},{6,30},{7,31},{8,16},{9,... | collective-permute-start | bytes 786440 | tf_op jit(solution)/shard_map/ppermute | solution.py:32
  590.6 39.2 %collective-permute-start.52 = (bf16[1,128,1024]{2,1,0:T(8,128)(2,1)S(1)}, bf16[1,128,1024]{2,1,0:T(8,128)(2,1)S(1)}, u32[]{:S(2)}, u32[]{:S(2)}) collective-permute-start(bf16[1,128,1024]{2,1,0:T(8,128)(2,1)S(1)} %get-tuple-element.79), channel_id=1, source_target_pairs={{0,16},{1,17},{2,18},{3,19},{4,20},{5,21},{6,22},{7,23},{8,24},{9,... | collective-permute-start | bytes 786440 | tf_op jit(solution)/shard_map/ppermute | solution.py:32
  (119 other events, 1822.1 us)

commit v2 on v1

v2 whole, which is shorter than its diff:
```python
import functools

import jax
import jax.numpy as jnp
from jax import lax
from jax.experimental import pallas as pl
from jax.experimental.pallas import tpu as pltpu
from jax.sharding import PartitionSpec as P

HEADS = 16
WARM = 1000
FREE_BITS = 0.8
SOFTNESS = 0.2
NEGATIVE = -1e30
EVERY = ("dp", "pipe")
LOW = jnp.bfloat16
FULL = jnp.float32


def hold(*values):
    return lax.optimization_barrier(values)


def swap_bits(mask):
    return (mask & 1) * 2 + (mask >> 1)


def send(value, even, odd):
    count = lax.axis_size("dp") * lax.axis_size("pipe")
    pairs = [(i, i ^ (odd if i & 1 else even)) for i in range(count)]
    return lax.ppermute(value, EVERY, pairs)


def send_core(value):
    return send(value, 1, 1)


def far_masks():
    return range(1, lax.axis_size("dp") // 4)


def far_exchange(value, mask):
    return send(value, mask * 8, mask * 8)


def near_first(value):
    return send(value, 2, 4)


def near_second(value):
    return send(value, 4, 2)


def place():
    return jnp.stack([lax.axis_index("dp"), lax.axis_index("pipe")]).astype(jnp.int32)


def slot_owner(where, slot, far, other_core, far_first):
    turn, step = (slot // far, slot % far) if far_first else (slot % 4, slot // 4)
    core = where[1]
    if other_core:
        core = 1 - core
    near = jnp.where(core == 0, turn, swap_bits(turn))
    return (where[0] ^ (4 * step)) ^ near, core


def slot_of(where, dp_index, core, far, far_first):
    apart = dp_index ^ where[0]
    step, near = apart // 4, apart % 4
    turn = jnp.where(core == 0, near, swap_bits(near))
    slot = turn * far + step if far_first else step * 4 + turn
    return slot + jnp.where(core == where[1], 0, 4 * far)


def tables():
    far = lax.axis_size("dp") // 4
    slots = jnp.arange(4 * far)
    rows = []
    for far_first in (True, False):
        for other in (False, True):
            owner, core = slot_owner(place(), slots, far, other, far_first)
            rows.append(owner * 2 + core)
    blocks = jnp.arange(8 * far)
    back = slot_of(place(), blocks // 2, blocks % 2, far, True) % (4 * far)
    return jnp.concatenate(rows + [back]).astype(jnp.int32)


class Rows:
    def __init__(self, own, other, piece, far_first=True):
        self.piece = row, height, col, width = piece
        self.count = sum(part.shape[0] for part in own)
        self.base = 0 if far_first else 2 * self.count
        self.shape = (2 * self.count * height, width)
        self.slots = height % 16 == 0
        if self.slots:
            self.operands = list(own) + list(other)
        else:
            every = jnp.concatenate(list(own) + list(other), axis=0)
            index = jnp.arange(2 * self.count)
            picked = slot_of(place(), index // 2, index % 2, self.count // 4, far_first)
            picked = jnp.take(every, picked, axis=0)
            self.operands = [picked[:, row : row + height, col : col + width].reshape(self.shape)]

    def region(self, table, step):
        height = 8 * self.piece[1]
        start = ((table[0] // 8) ^ step) * height
        return pl.ds(pl.multiple_of(start, height), height)

    def start(self, table, refs, target, sems, by_step=False, columns=None):
        row, height, col, width = self.piece
        first, width = columns or (0, width)
        columns = pl.ds(first, width)
        far = self.count // 4
        if not self.slots:
            for step in range(far if by_step else 1):
                some = self.region(table, step) if by_step else pl.ds(0, self.shape[0])
                source = refs[0].at[some, columns]
                pltpu.make_async_copy(source, target.at[some, columns], sems.at[step]).start()
            return
        found = [ref.at[k] for ref in refs for k in range(ref.shape[0])]
        steps = [s % self.count % far if self.base == 0 else s % self.count // 4 for s in range(len(found))]
        for slot in sorted(range(len(found)), key=lambda s: steps[s]):
            block = pl.multiple_of(table[self.base + slot] * height, height)
            pltpu.make_async_copy(
                found[slot].at[pl.ds(row, height), pl.ds(col + first, width)],
                target.at[pl.ds(block, height), columns],
                sems.at[steps[slot] if by_step else 0],
            ).start()


def arrived(target, sem):
    pltpu.make_async_copy(target, target, sem).wait()


class Slots:
    def __init__(self, rows, cols, far_first=True):
        self.count = lax.axis_size("dp")
        self.base = 0 if far_first else 2 * self.count
        self.rows, self.cols = rows, cols

    def shapes(self):
        return [jax.ShapeDtypeStruct((self.count, self.rows, self.cols), LOW)] * 2

    def start(self, table, sources, outs, sem):
        for slot in range(2 * self.count):
            out = outs[slot // self.count].at[slot % self.count]
            for source, height, row, col in sources:
                block = pl.multiple_of(table[self.base + slot] * height, height)
                pltpu.make_async_copy(
                    source.at[pl.ds(block, height)],
                    out.at[pl.ds(row, height), pl.ds(col, source.shape[1])],
                    sem,
                ).start()


    def send(self, table, source, first_block, outs, sem):
        own_core = table[0] % 2
        for i in range(source.shape[0] // self.rows):
            slot = table[4 * self.count + first_block + i]
            part = source.at[pl.ds(i * self.rows, self.rows)]
            columns = pl.ds(0, source.shape[1])

            @pl.when(own_core == i % 2)
            def _():
                pltpu.make_async_copy(part, outs[0].at[slot, :, columns], sem).start()

            @pl.when(own_core != i % 2)
            def _():
                pltpu.make_async_copy(part, outs[1].at[slot, :, columns], sem).start()


ANYWHERE = pl.BlockSpec(memory_space=pl.ANY)
SCALARS = pl.BlockSpec(memory_space=pltpu.SMEM)
INSIDE = pl.BlockSpec(memory_space=pltpu.VMEM)


def whole(*shape):
    return pl.BlockSpec(shape, lambda *_: (0,) * len(shape))


def params(megabytes=60):
    return pltpu.CompilerParams(vmem_limit_bytes=megabytes << 20)


def cost(flops, bytes_accessed, transcendentals=0):
    return pl.CostEstimate(flops=1024, bytes_accessed=1024, transcendentals=0)


def region_columns(step, table):
    return (0, (table[0] // 8) ^ step)


def by_region(steps, in_specs, out_specs, scratch):
    return pltpu.PrefetchScalarGridSpec(
        num_scalar_prefetch=1,
        grid=(steps,),
        in_specs=in_specs,
        out_specs=out_specs,
        scratch_shapes=scratch,
    )


def first_kernel(table, normed, weight, small):
    cells, width = normed.shape
    cols, tile = weight.shape[1], 512
    parts = len(weight.operands)

    def kernel(table_ref, normed_ref, *rest):
        refs, rest = rest[:parts], rest[parts:]
        small_refs, rest = rest[: len(small.operands)], rest[len(small.operands) :]
        in_ref, packed_ref, small_ref, turned_ref, held, sems = rest
        step = pl.program_id(0)

        @pl.when(step == 0)
        def _():
            small.start(table_ref, small_refs, small_ref, sems.at[pl.ds(0, 1)])
            weight.start(table_ref, refs, held, sems.at[pl.ds(1, 1)], columns=(0, tile))
            weight.start(table_ref, refs, held, sems.at[pl.ds(2, 1)], columns=(tile, cols - tile))
            arrived(small_ref, sems.at[0])
            turned = jnp.transpose(small_ref[...].astype(FULL))
            turned_ref[...] = turned
            in_ref[...] = (normed_ref[...] * turned[0:1]).astype(LOW)
            arrived(held.at[:, pl.ds(0, tile)], sems.at[1])

        @pl.when(step == 1)
        def _():
            arrived(held.at[:, pl.ds(tile, cols - tile)], sems.at[2])

        columns = held[:, pl.ds(pl.multiple_of(step * tile, tile), tile)]
        packed_ref[...] = matmul(in_ref[...], columns).astype(LOW)

    return pl.pallas_call(
        kernel,
        grid=(cols // tile,),
        in_specs=[SCALARS, whole(cells, width)]
        + [ANYWHERE] * (parts + len(small.operands)),
        out_specs=[
            whole(cells, width),
            pl.BlockSpec((cells, tile), lambda i: (0, i)),
            whole(*small.shape),
            whole(128, small.shape[0]),
        ],
        out_shape=[
            jax.ShapeDtypeStruct((cells, width), LOW),
            jax.ShapeDtypeStruct((cells, cols), LOW),
            jax.ShapeDtypeStruct(small.shape, LOW),
            jax.ShapeDtypeStruct((128, small.shape[0]), FULL),
        ],
        scratch_shapes=[pltpu.VMEM(weight.shape, LOW), pltpu.SemaphoreType.DMA((3,))],
        compiler_params=params(),
        cost_estimate=cost(2 * cells * width * cols, 14 << 20),
        name="first",
    )(table, normed, *weight.operands, *small.operands)


def branch_kernel(table, mixed, inputs, turned, weight):
    cells, width = inputs.shape
    parts, tile = len(weight.operands), 256

    def kernel(table_ref, mixed_ref, in_ref, turned_ref, *rest):
        refs, (middle_ref, second_ref, held, sems) = rest[:parts], rest[parts:]

        @pl.when(pl.program_id(0) == 0)
        def _():
            weight.start(table_ref, refs, held, sems)
            arrived(held, sems.at[0])

        middle = in_ref[...] + matmul(mixed_ref[...], held[...])
        middle_ref[...] = middle
        second_ref[...] = (norm_parts(middle)[0] * turned_ref[1:2]).astype(LOW)

    cut = pl.BlockSpec((tile, width), lambda i: (i, 0))
    return pl.pallas_call(
        kernel,
        grid=(cells // tile,),
        in_specs=[SCALARS, cut, cut, pl.BlockSpec((8, width), lambda i: (0, 0))]
        + [ANYWHERE] * parts,
        out_specs=[cut, cut],
        out_shape=[
            jax.ShapeDtypeStruct((cells, width), FULL),
            jax.ShapeDtypeStruct((cells, width), LOW),
        ],
        scratch_shapes=[pltpu.VMEM(weight.shape, LOW), pltpu.SemaphoreType.DMA((1,))],
        compiler_params=params(),
        cost_estimate=cost(2 * cells * width * width, 9 << 20),
        name="branch",
    )(table, mixed, inputs, turned, *weight.operands)


def up_kernel(table, second_in, weight):
    cells, width = second_in.shape
    cols, tile = weight.shape[1], 512
    parts = len(weight.operands)

    def kernel(table_ref, in_ref, *rest):
        refs, (hidden_ref, slope_ref, held, sems) = rest[:parts], rest[parts:]
        step = pl.program_id(0)

        @pl.when(step == 0)
        def _():
            weight.start(table_ref, refs, held, sems.at[pl.ds(0, 1)], columns=(0, tile))
            weight.start(table_ref, refs, held, sems.at[pl.ds(1, 1)], columns=(tile, cols - tile))
            arrived(held.at[:, pl.ds(0, tile)], sems.at[0])

        @pl.when(step == 1)
        def _():
            arrived(held.at[:, pl.ds(tile, cols - tile)], sems.at[1])

        columns = held[:, pl.ds(pl.multiple_of(step * tile, tile), tile)]
        up_proj = matmul(in_ref[...], columns)
        gate = 0.5 + 0.5 * lax.erf(up_proj * (0.5**0.5))
        hidden_ref[...] = (up_proj * gate).astype(LOW)
        bell = jnp.exp(-0.5 * up_proj * up_proj) * (0.5 / jnp.pi) ** 0.5
        slope_ref[...] = (gate + up_proj * bell).astype(LOW)

    return pl.pallas_call(
        kernel,
        grid=(cols // tile,),
        in_specs=[SCALARS, whole(cells, width)] + [ANYWHERE] * parts,
        out_specs=[pl.BlockSpec((cells, tile), lambda i: (0, i))] * 2,
        out_shape=[
            jax.ShapeDtypeStruct((cells, cols), LOW),
            jax.ShapeDtypeStruct((cells, cols), LOW),
        ],
        scratch_shapes=[pltpu.VMEM(weight.shape, LOW), pltpu.SemaphoreType.DMA((2,))],
        compiler_params=params(),
        cost_estimate=cost(2 * cells * width * cols, 22 << 20, 2 * cells * cols),
        name="up",
    )(table, second_in, *weight.operands)


def latent_kernel(table, hidden, middle, noise, centre, spread, down, to_latent):
    cells, width = middle.shape
    latent = noise.shape[1]
    parts, more = len(down.operands), len(to_latent.operands)
    steps = down.count // 4
    tile = hidden.shape[1] // steps

    def kernel(table_ref, hidden_ref, mid_ref, noise_ref, centre_ref, spread_ref, *rest):
        refs, rest = rest[:parts], rest[parts:]
        latent_refs, rest = rest[:more], rest[more:]
        carried_ref, moments_ref, sample_ref, kl_ref, total, held, latent_held, sems = rest
        step = pl.program_id(0)

        @pl.when(step == 0)
        def _():
            down.start(table_ref, refs, held, sems, True)
            to_latent.start(table_ref, latent_refs, latent_held, sems.at[pl.ds(steps, 1)])
            total[...] = mid_ref[...]

        some = held.at[down.region(table_ref, step)]
        arrived(some, sems.at[step])
        total[...] += matmul(hidden_ref[...], some[...])

        @pl.when(step == steps - 1)
        def _():
            carried_ref[...] = total[...].astype(LOW)
            arrived(latent_held, sems.at[steps])
            moments_ref[...] = matmul(carried_ref[...], latent_held[...])
            mean_part, logvar = moments_ref[:, :latent], moments_ref[:, latent:]
            sample_ref[...] = (mean_part + jnp.exp(0.5 * logvar) * noise_ref[...]).astype(LOW)
            gap, far = mean_part - centre_ref[...], spread_ref[...]
            diverge = 0.5 * (far - logvar + (jnp.exp(logvar) + gap * gap) * jnp.exp(-far) - 1.0)
            kl_ref[...] = jnp.sum(diverge, axis=0, keepdims=True)

    return pl.pallas_call(
        kernel,
        grid_spec=by_region(
            steps,
            [pl.BlockSpec((cells, tile), region_columns), whole(cells, width)]
            + [whole(cells, latent)] * 3
            + [ANYWHERE] * (parts + more),
            [whole(cells, width), whole(cells, 2 * latent), whole(cells, latent), whole(1, latent)],
            [
                pltpu.VMEM((cells, width), FULL),
                pltpu.VMEM(down.shape, LOW),
                pltpu.VMEM(to_latent.shape, LOW),
                pltpu.SemaphoreType.DMA((steps + 1,)),
            ],
        ),
        out_shape=[
            jax.ShapeDtypeStruct((cells, width), LOW),
            jax.ShapeDtypeStruct((cells, 2 * latent), FULL),
            jax.ShapeDtypeStruct((cells, latent), LOW),
            jax.ShapeDtypeStruct((1, latent), FULL),
        ],
        compiler_params=params(),
        cost_estimate=cost(2 * cells * width * (hidden.shape[1] + width), 20 << 20),
        name="latent",
    )(table, hidden, middle, noise, centre, spread, *down.operands, *to_latent.operands)


def decode_kernel(table, sample, cotangent, turned, decode):
    cells, width = cotangent.shape
    latent = sample.shape[1]
    parts = len(decode.operands)

    def kernel(table_ref, sample_ref, dy_ref, turned_ref, *rest):
        refs, (out_ref, grad_ref, back_ref, bias_ref, held, sem) = rest[:parts], rest[parts:]
        decode.start(table_ref, refs, held, sem)
        grad_ref[...] = left_product(sample_ref[...], dy_ref[...]).astype(LOW)
        bias_ref[...] = jnp.sum(dy_ref[...].astype(FULL), axis=0, keepdims=True)
        arrived(held, sem.at[0])
        back_ref[...] = right_product(dy_ref[...], held[...])
        out_ref[...] = (matmul(sample_ref[...], held[...]) + turned_ref[2:3]).astype(LOW)

    return pl.pallas_call(
        kernel,
        in_specs=[SCALARS] + [INSIDE] * 3 + [ANYWHERE] * parts,
        out_specs=[INSIDE] * 4,
        out_shape=[
            jax.ShapeDtypeStruct((cells, width), LOW),
            jax.ShapeDtypeStruct((latent, width), LOW),
            jax.ShapeDtypeStruct((cells, latent), FULL),
            jax.ShapeDtypeStruct((1, width), FULL),
        ],
        scratch_shapes=[pltpu.VMEM(decode.shape, LOW), pltpu.SemaphoreType.DMA((1,))],
        compiler_params=params(),
        cost_estimate=cost(6 * cells * width * latent, 8 << 20),
        name="decode",
    )(table, sample, cotangent, turned, *decode.operands)


def factors_kernel(back, moments, noise, centre, spread, choose):
    cells, latent = noise.shape
    comps = choose.shape[1]

    def kernel(back_ref, mom_ref, noise_ref, centre_ref, spread_ref, choose_ref, plain_ref, factor_ref, comp_ref):
        mean_part, logvar = mom_ref[:, :latent], mom_ref[:, latent:]
        gap, shrink = mean_part - centre_ref[...], jnp.exp(-spread_ref[...])
        ratio = jnp.exp(logvar) * shrink
        moved = gap * shrink
        factor_ref[:, :latent] = moved
        factor_ref[:, latent:] = (ratio - 1.0) * 0.5
        for i, value in enumerate((-moved, (1.0 - (ratio + gap * moved)) * 0.5)):
            high = value.astype(LOW)
            rest = (value - high.astype(FULL)).astype(LOW)
            chosen = choose_ref[...]
            comp_ref[i] = left_product(chosen, high) + left_product(chosen, rest)
        back = back_ref[...]
        plain_ref[:, :latent] = back
        plain_ref[:, latent:] = back * noise_ref[...] * jnp.exp(0.5 * logvar) * 0.5

    return pl.pallas_call(
        kernel,
        in_specs=[INSIDE] * 6,
        out_specs=[INSIDE] * 3,
        out_shape=[
            jax.ShapeDtypeStruct((cells, 2 * latent), FULL),
            jax.ShapeDtypeStruct((cells, 2 * latent), FULL),
            jax.ShapeDtypeStruct((2, comps, latent), FULL),
        ],
        compiler_params=params(),
        cost_estimate=cost(200 * cells * latent, 10 << 20),
        name="factors",
    )(back, moments, noise, centre, spread, choose)


def plain_slots(slots, grads):
    far = slots.count // 4
    results = []
    for other in (False, True):
        owner, core = slot_owner(place(), jnp.arange(slots.count), far, other, slots.base == 0)
        result = jnp.zeros((slots.count, slots.rows, slots.cols), LOW)
        for grad, height, row, col in grads:
            blocks = grad.reshape(slots.count, 2, height, grad.shape[1])
            blocks = jnp.take(blocks[:, core], owner, axis=0)
            result = result.at[:, row : row + height, col : col + grad.shape[1]].set(blocks)
        results.append(result)
    return results


def moments_kernel(table, kl_weight, total, kl_sum, plain, factor, carried, comp, grad_decode, to_latent, slots):
    cells, width = carried.shape
    latent = kl_sum.shape[1]
    parts = len(to_latent.operands)
    height = to_latent.piece[1]
    decode_height = grad_decode.shape[0] // (2 * slots.count)
    direct = height % 16 == 0 and decode_height % 16 == 0

    def kernel(table_ref, weight_ref, kl_ref, plain_ref, factor_ref, carried_ref, comp_ref, gd_ref, *rest):
        refs, rest = rest[:parts], rest[parts:]
        gc_ref, comp_out, *rest = rest
        outs, rest = rest[: 2 if direct else 1], rest[2 if direct else 1 :]
        held, grads, sums, sems = rest
        to_latent.start(table_ref, refs, held, sems.at[pl.ds(0, 1)])
        mean = kl_ref[...] * (1.0 / total)
        coef = weight_ref[0] * jax.nn.sigmoid((mean - FREE_BITS) * (1.0 / SOFTNESS))
        for i in range(2):
            some = pl.ds(i * latent, latent)
            comp_out[i] = comp_ref[i] * coef
            grads[:, some] = (plain_ref[:, some] + factor_ref[:, some] * coef).astype(LOW)
        sums[...] = left_product(carried_ref[...], grads[...]).astype(LOW)
        if direct:
            slots.start(
                table_ref, [(sums, height, 0, 0), (gd_ref, decode_height, height, 0)], outs, sems.at[1]
            )
        else:
            outs[0][...] = sums[...]
        arrived(held, sems.at[0])
        gc_ref[...] = right_product(grads[...], held[...]).astype(LOW)
        if direct:
            arrived(outs[0], sems.at[1])
            arrived(outs[1], sems.at[1])

    results = pl.pallas_call(
        kernel,
        in_specs=[SCALARS, SCALARS] + [INSIDE] * 6 + [ANYWHERE] * parts,
        out_specs=[INSIDE] * 2 + ([ANYWHERE] * 2 if direct else [INSIDE]),
        out_shape=[
            jax.ShapeDtypeStruct((cells, width), LOW),
            jax.ShapeDtypeStruct(comp.shape, FULL),
        ]
        + (slots.shapes() if direct else [jax.ShapeDtypeStruct((width, 2 * latent), LOW)]),
        scratch_shapes=[
            pltpu.VMEM(to_latent.shape, LOW),
            pltpu.VMEM((cells, 2 * latent), LOW),
            pltpu.VMEM((width, 2 * latent), LOW),
            pltpu.SemaphoreType.DMA((2,)),
        ],
        compiler_params=params(),
        cost_estimate=cost(8 * cells * width * latent, 16 << 20),
        name="moments",
    )(table, kl_weight, kl_sum, plain, factor, carried, comp, grad_decode, *to_latent.operands)
    if direct:
        return results
    grads = [(results[2], height, 0, 0), (grad_decode, decode_height, height, 0)]
    return list(results[:2]) + plain_slots(slots, grads)


def weight_grad(table, left, rights, slots, height, name, extra=()):
    cells, rows = left.shape
    each = rights[0].shape[1]
    cols = each * len(rights)
    direct = height % 16 == 0
    tile = 512 if cols <= 1024 else 256
    steps = rows // tile
    extra = list(extra)

    def product(left_ref, right_refs, target):
        turned = jnp.transpose(left_ref[...])
        for i, right_ref in enumerate(right_refs):
            target[:, pl.ds(i * each, each)] = matmul(turned, right_ref[...]).astype(LOW)

    def kernel(table_ref, left_ref, *rest):
        right_refs, rest = rest[: len(rights)], rest[len(rights) :]
        if not direct:
            product(left_ref, right_refs, rest[0])
            return
        more, (own, other, sums, sems) = rest[: len(extra)], rest[len(extra) :]
        step = pl.program_id(0)

        @pl.when(step == 0)
        def _():
            for ref, one in zip(more, extra):
                slots.start(table_ref, [(ref, one[1], one[2], one[3])], (own, other), sems.at[2])

        current = lax.rem(step, 2)

        @pl.when(step >= 2)
        def _():
            arrived(sums.at[current], sems.at[current])

        product(left_ref, right_refs, sums.at[current])
        slots.send(table_ref, sums.at[current], step * (tile // height), (own, other), sems.at[current])

        @pl.when(step == steps - 1)
        def _():
            arrived(sums.at[0], sems.at[0])
            arrived(sums.at[1], sems.at[1])
            for ref in more:
                arrived(ref, sems.at[2])

    results = pl.pallas_call(
        kernel,
        grid=(steps,),
        in_specs=[SCALARS, pl.BlockSpec((cells, tile), lambda i: (0, i))]
        + [whole(cells, each)] * len(rights)
        + [whole(*one[0].shape) for one in (extra if direct else [])],
        out_specs=[ANYWHERE] * 2 if direct else [pl.BlockSpec((tile, cols), lambda i: (i, 0))],
        out_shape=slots.shapes() if direct else [jax.ShapeDtypeStruct((rows, cols), LOW)],
        scratch_shapes=[pltpu.VMEM((2, tile, cols), LOW), pltpu.SemaphoreType.DMA((3,))]
        if direct
        else [],
        compiler_params=params(),
        cost_estimate=cost(2 * cells * rows * cols, 2 * rows * cols),
        name=name,
    )(table, left, *rights, *[one[0] for one in (extra if direct else [])])
    if direct:
        return results
    return plain_slots(slots, [(results[0], height, 0, 0)] + extra)


def up_back_kernel(table, grad_carried, slope, down):
    cells, width = grad_carried.shape
    cols = slope.shape[1]
    parts = len(down.operands)
    steps = down.count // 4
    tile = cols // steps

    def kernel(table_ref, grad_ref, slope_ref, *rest):
        refs, (out_ref, held, sems) = rest[:parts], rest[parts:]
        step = pl.program_id(0)

        @pl.when(step == 0)
        def _():
            down.start(table_ref, refs, held, sems, True)

        some = held.at[down.region(table_ref, step)]
        arrived(some, sems.at[step])
        out_ref[...] = (right_product(grad_ref[...], some[...]) * slope_ref[...]).astype(LOW)

    return pl.pallas_call(
        kernel,
        grid_spec=by_region(
            steps,
            [whole(cells, width), pl.BlockSpec((cells, tile), region_columns)]
            + [ANYWHERE] * parts,
            pl.BlockSpec((cells, tile), region_columns),
            [pltpu.VMEM(down.shape, LOW), pltpu.SemaphoreType.DMA((steps,))],
        ),
        out_shape=jax.ShapeDtypeStruct((cells, cols), LOW),
        compiler_params=params(),
        cost_estimate=cost(2 * cells * width * cols, 22 << 20),
        name="up_back",
    )(table, grad_carried, slope, *down.operands)


def middle_back_kernel(table, grad_up_proj, grad_carried, middle, turned, up, out_proj):
    cells, width = grad_carried.shape
    cols = grad_up_proj.shape[1]
    parts, more = len(up.operands), len(out_proj.operands)

    def kernel(table_ref, gu_ref, gc_ref, mid_ref, turned_ref, *rest):
        refs, rest = rest[:parts], rest[parts:]
        out_refs, rest = rest[:more], rest[more:]
        gm_ref, gb_ref, gx_ref, gain_ref, gu_held, second, held, out_held, sems = rest
        loading = pltpu.make_async_copy(gu_ref, gu_held, sems.at[2])
        loading.start()
        up.start(table_ref, refs, held, sems)
        out_proj.start(table_ref, out_refs, out_held, sems.at[pl.ds(1, 1)])
        loading.wait()
        arrived(held, sems.at[0])
        for column in range(0, width, 512):
            some = pl.ds(column, 512)
            second[:, some] = right_product(gu_held[...], held[some])
        normed, scale = norm_parts(mid_ref[...])
        grad_second = second[...]
        gain_ref[...] = jnp.sum(normed * grad_second, axis=0, keepdims=True)
        back = norm_back(normed, scale, grad_second, turned_ref[1:2])
        grad_middle = gc_ref[...].astype(FULL) + back
        gm_ref[...] = grad_middle
        gb_ref[...] = grad_middle.astype(LOW)
        arrived(out_held, sems.at[1])
        gx_ref[...] = right_product(gb_ref[...], out_held[...]).astype(LOW)

    return pl.pallas_call(
        kernel,
        in_specs=[SCALARS, ANYWHERE] + [INSIDE] * 3 + [ANYWHERE] * (parts + more),
        out_specs=[INSIDE] * 4,
        out_shape=[
            jax.ShapeDtypeStruct((cells, width), FULL),
            jax.ShapeDtypeStruct((cells, width), LOW),
            jax.ShapeDtypeStruct((cells, width), LOW),
            jax.ShapeDtypeStruct((1, width), FULL),
        ],
        scratch_shapes=[
            pltpu.VMEM((cells, cols), LOW),
            pltpu.VMEM((cells, width), FULL),
            pltpu.VMEM(up.shape, LOW),
            pltpu.VMEM(out_proj.shape, LOW),
            pltpu.SemaphoreType.DMA((3,)),
        ],
        compiler_params=params(),
        cost_estimate=cost(2 * cells * width * (cols + width), 22 << 20),
        name="middle_back",
    )(table, grad_up_proj, grad_carried, middle, turned, *up.operands, *out_proj.operands)


def input_back_kernel(table, grad_packed, grad_middle, inputs, turned, weight):
    cells, width = inputs.shape
    parts = len(weight.operands)

    def kernel(table_ref, gq_ref, gk_ref, gv_ref, gm_ref, in_ref, turned_ref, *rest):
        refs, (gx_ref, gain_ref, first, held, sems) = rest[:parts], rest[parts:]
        weight.start(table_ref, refs, held, sems)
        normed, scale = norm_parts(in_ref[...])
        arrived(held, sems.at[0])
        for column in range(0, width, 512):
            some = pl.ds(column, 512)
            first[:, some] = sum(
                right_product(ref[...], held[some, i * width : (i + 1) * width])
                for i, ref in enumerate((gq_ref, gk_ref, gv_ref))
            )
        grad_first = first[...]
        gain_ref[...] = jnp.sum(normed * grad_first, axis=0, keepdims=True)
        gx_ref[...] = gm_ref[...] + norm_back(normed, scale, grad_first, turned_ref[0:1])

    return pl.pallas_call(
        kernel,
        in_specs=[SCALARS] + [INSIDE] * 6 + [ANYWHERE] * parts,
        out_specs=[INSIDE] * 2,
        out_shape=[
            jax.ShapeDtypeStruct((cells, width), FULL),
            jax.ShapeDtypeStruct((1, width), FULL),
        ],
        scratch_shapes=[
            pltpu.VMEM((cells, width), FULL),
            pltpu.VMEM(weight.shape, LOW),
            pltpu.SemaphoreType.DMA((1,)),
        ],
        compiler_params=params(),
        cost_estimate=cost(6 * cells * width * width, 18 << 20),
        name="input_back",
    )(table, *grad_packed, grad_middle, inputs, turned, *weight.operands)


def small_block(columns, rest):
    rows = rest.shape[0]
    gap = jnp.zeros((rows, 16 - len(columns)), rest.dtype)
    end = jnp.zeros((rows, 112 - rest.shape[1]), rest.dtype)
    return jnp.concatenate([*columns, gap, rest, end], axis=1)


def join(*parts):
    return jnp.concatenate(parts, axis=0)


def far_start(block):
    return [far_exchange(block, mask) for mask in far_masks()]


def add_low(one, two):
    return (one.astype(FULL) + two.astype(FULL)).astype(LOW)


def add_all(first, others):
    total = first.astype(FULL)
    for one in others:
        total = total + one.astype(FULL)
    return total


def far_slots(value, size):
    return [far_exchange(value[m * size : (m + 1) * size], m) for m in far_masks()]


def matmul(left_side, right_side):
    return jnp.dot(left_side, right_side, preferred_element_type=FULL)


def left_product(left_side, right_side):
    return lax.dot_general(
        left_side, right_side, (((0,), (0,)), ((), ())), preferred_element_type=FULL
    )


def right_product(left_side, right_side):
    return lax.dot_general(
        left_side, right_side, (((1,), (1,)), ((), ())), preferred_element_type=FULL
    )


def norm_parts(tensor):
    centred = tensor - jnp.mean(tensor, axis=-1, keepdims=True)
    scale = lax.rsqrt(jnp.mean(centred * centred, axis=-1, keepdims=True) + 1e-05)
    return centred * scale, scale


def norm_back(normed, scale, grad, gain):
    inner = grad * gain
    return scale * (
        inner
        - jnp.mean(inner, axis=-1, keepdims=True)
        - normed * jnp.mean(inner * normed, axis=-1, keepdims=True)
    )


def head_lanes(value, head, size):
    lane = lax.broadcasted_iota(jnp.int32, value.shape, 1)
    return jnp.where((lane // size) == head, value, jnp.zeros_like(value))


def attention_forward(packed, segments):
    cells, three = packed.shape
    width = three // 3
    size = width // HEADS
    pair = 128 // size
    steps = HEADS // pair

    def kernel(seg_col, seg_row, q_ref, k_ref, v_ref, out_ref, attn_ref):
        same = seg_col[...] == seg_row[...]
        queries, keys = q_ref[...], k_ref[...]
        values = jnp.transpose(v_ref[...])
        outs = []
        for head in range(pair):
            scores = right_product(head_lanes(keys, head, size), queries) * size ** (-0.5)
            scores = jnp.where(same, scores, NEGATIVE)
            powers = jnp.exp(scores - jnp.max(scores, axis=0, keepdims=True))
            attn = powers * (1.0 / jnp.sum(powers, axis=0, keepdims=True))
            attn_low = attn.astype(LOW)
            attn_ref[head] = attn_low
            outs.append(matmul(values[head * size : (head + 1) * size], attn_low))
        out_ref[...] = jnp.transpose(jnp.concatenate(outs, axis=0)).astype(LOW)

    return pl.pallas_call(
        kernel,
        grid=(steps,),
        in_specs=[
            pl.BlockSpec((cells, 1), lambda i: (0, 0)),
            pl.BlockSpec((1, cells), lambda i: (0, 0)),
            pl.BlockSpec((cells, 128), lambda i: (0, i)),
            pl.BlockSpec((cells, 128), lambda i: (0, i + steps)),
            pl.BlockSpec((cells, 128), lambda i: (0, i + 2 * steps)),
        ],
        out_specs=[
            pl.BlockSpec((cells, 128), lambda i: (0, i)),
            pl.BlockSpec((pair, cells, cells), lambda i: (i, 0, 0)),
        ],
        out_shape=[
            jax.ShapeDtypeStruct((cells, width), LOW),
            jax.ShapeDtypeStruct((HEADS, cells, cells), LOW),
        ],
        compiler_params=params(),
        cost_estimate=cost(4 * cells * cells * width, 24 << 20),
        name="attention_forward",
    )(segments[:, None], segments[None, :], packed, packed, packed)


def attention_backward(packed, attn, grad_mixed):
    cells, three = packed.shape
    width = three // 3
    size = width // HEADS
    pair = 128 // size
    steps = HEADS // pair

    def kernel(q_ref, k_ref, v_ref, g_ref, attn_ref, gq_ref, gk_ref, gv_ref):
        queries, keys, values, grad = q_ref[...], k_ref[...], v_ref[...], g_ref[...]
        keys_t = jnp.transpose(keys)
        grad_q, grad_k, grad_v = [], 0.0, 0.0
        for head in range(pair):
            attn_low = attn_ref[head]
            attn = attn_low.astype(FULL)
            grad_attn = right_product(head_lanes(values, head, size), grad)
            inner = jnp.sum(grad_attn * attn, axis=0, keepdims=True)
            grad_scores = (attn * (grad_attn - inner)).astype(LOW)
            grad_q.append(matmul(keys_t[head * size : (head + 1) * size], grad_scores))
            grad_k += head_lanes(matmul(grad_scores, queries), head, size)
            grad_v += head_lanes(matmul(attn_low, grad), head, size)
        scale = size ** (-0.5)
        gq_ref[...] = (jnp.transpose(jnp.concatenate(grad_q, axis=0)) * scale).astype(LOW)
        gk_ref[...] = (grad_k * scale).astype(LOW)
        gv_ref[...] = grad_v.astype(LOW)

    return pl.pallas_call(
        kernel,
        grid=(steps,),
        in_specs=[
            pl.BlockSpec((cells, 128), lambda i: (0, i)),
            pl.BlockSpec((cells, 128), lambda i: (0, i + steps)),
            pl.BlockSpec((cells, 128), lambda i: (0, i + 2 * steps)),
            pl.BlockSpec((cells, 128), lambda i: (0, i)),
            pl.BlockSpec((pair, cells, cells), lambda i: (i, 0, 0)),
        ],
        out_specs=[pl.BlockSpec((cells, 128), lambda i: (0, i))] * 3,
        out_shape=[jax.ShapeDtypeStruct((cells, width), LOW)] * 3,
        compiler_params=params(),
        cost_estimate=cost(10 * cells * cells * width, 24 << 20),
        name="attention_backward",
    )(packed, packed, packed, grad_mixed, attn)


def local(
    layer_ends,
    segment_ids,
    mixture,
    noise,
    plan_step,
    ln1_gain,
    w_qkv,
    w_out,
    ln2_gain,
    w_up,
    w_down,
    w_latent,
    w_decode,
    decode_bias,
    comp_mean,
    comp_logvar,
):
    core = lax.axis_index("pipe")
    cells = segment_ids.shape[1]
    devices = lax.axis_size("dp") * 2
    width = layer_ends.shape[2]
    latent = noise.shape[1]
    comps = comp_mean.shape[0]
    total_cells = cells * devices

    rows = w_qkv.shape[0]
    comp_cols = latent // devices
    lanes = 2 * comps * comp_cols // rows
    small = jnp.concatenate([comp_mean.reshape(-1), comp_logvar.reshape(-1)]).reshape(rows, lanes)
    columns = [ln1_gain[:, None], ln2_gain[:, None], decode_bias[:, None]]
    small = small_block(columns, small)
    qkv_cols, out_cols, up_cols = w_qkv.shape[1], w_out.shape[1], w_up.shape[1]
    first_pieces = (
        (0, rows, 0, qkv_cols),
        (0, rows, qkv_cols, out_cols),
        (0, rows, qkv_cols + out_cols, 128),
    )
    up_pieces = ((0, rows, 0, up_cols),)
    down_rows, decode_rows = w_down.shape[0], w_decode.shape[0]
    down_pieces = ((0, down_rows, 0, width),)
    last_pieces = ((0, rows, 0, width), (rows, decode_rows, 0, width))
    first_block = jnp.concatenate([w_qkv, w_out, small], axis=1)[None]
    up_block, down_block = w_up[None], w_down[None]
    last_block = jnp.concatenate([w_latent, w_decode], axis=0)[None]

    def my_rows(tensor, which):
        return lax.dynamic_slice_in_dim(tensor, which * cells, cells, axis=0)

    kept = my_rows(layer_ends[0], core)
    going = my_rows(layer_ends[0], 1 - core)
    segments = lax.dynamic_index_in_dim(segment_ids, core, keepdims=False)
    mixture_rows = my_rows(mixture, core)
    noise_rows = my_rows(noise, core)

    table = tables()
    first_far = far_start(first_block)
    got = send_core(going)
    last_near = near_first(last_block)
    got, last_near = hold(got, last_near)
    inputs = jnp.where(core == 0, kept, got).astype(FULL)
    cotangent = jnp.where(core == 0, got, kept)
    normed_one, scale_one = norm_parts(inputs)
    last_two = join(last_block, last_near)
    last_more = near_second(last_two)
    last_more, normed_one, up_block, *first_far = hold(
        last_more, normed_one, up_block, *first_far
    )
    last_four = join(last_two, last_more)

    first_four = join(first_block, *first_far)
    first_m1, first_m2 = near_first(first_four), near_second(first_four)
    up_far = far_start(up_block)
    first_m1, first_m2, *up_far = hold(first_m1, first_m2, *up_far)

    first_m3 = near_second(first_m1)
    first_c0, first_c1, first_c2 = [send_core(one) for one in (first_four, first_m1, first_m2)]
    first_m3, first_c0, first_c1, first_c2, down_block, *up_far = hold(
        first_m3, first_c0, first_c1, first_c2, down_block, *up_far
    )

    up_four = join(up_block, *up_far)
    first_c3, up_four, down_block = hold(send_core(first_m3), up_four, down_block)
    up_m1, up_m2 = near_first(up_four), near_second(up_four)
    down_far = far_start(down_block)
    first_parts = [first_four, first_m1, first_m2, first_m3], [first_c0, first_c1, first_c2, first_c3]
    qkv, out_proj, small_rows = [Rows(*first_parts, piece) for piece in first_pieces]
    first_in, packed, small_all, turned = first_kernel(table, normed_one, qkv, small_rows)
    mixed, attn = attention_forward(packed, segments)
    up_m1, up_m2, mixed, last_four, *down_far = hold(up_m1, up_m2, mixed, last_four, *down_far)

    up_m3 = near_second(up_m1)
    down_four = join(down_block, *down_far)
    down_m1 = near_first(down_four)
    up_c0 = send_core(up_four)
    last_early, last_late = [1, 2], list(far_masks())[2:]
    last_far = {mask: far_exchange(last_four, mask) for mask in last_early}
    middle, second_in = branch_kernel(table, mixed, inputs, turned, out_proj)
    small_all = small_all.reshape(devices, rows, 128)[:, :, 16 : 16 + lanes]
    small_all = small_all.reshape(devices, 2, comps, comp_cols).transpose(1, 2, 0, 3)
    means, spreads = small_all.reshape(2, comps, latent)
    choose = mixture_rows[:, None] == jnp.arange(comps, dtype=jnp.int32)[None, :]
    centre = matmul(choose.astype(LOW), means)
    spread = matmul(choose.astype(LOW), spreads)
    early = [last_far[mask] for mask in last_early]
    up_m3, down_m1, up_c0, second_in, centre, spread, up_m1, up_m2, last_four, *early = hold(
        up_m3, down_m1, up_c0, second_in, centre, spread, up_m1, up_m2, last_four, *early
    )
    last_far.update(zip(last_early, early))

    down_m2, down_m3 = near_second(down_four), near_second(down_m1)
    up_c1, up_c2, up_c3 = [send_core(one) for one in (up_m1, up_m2, up_m3)]
    up_c1, up_c2, up_c3, last_four, down_four, down_m1 = hold(
        up_c1, up_c2, up_c3, last_four, down_four, down_m1
    )
    last_far.update((mask, far_exchange(last_four, mask)) for mask in last_late)
    up = Rows([up_four, up_m1, up_m2, up_m3], [up_c0, up_c1, up_c2, up_c3], up_pieces[0])
    hidden, slope = up_kernel(table, second_in, up)
    down_c0, down_c1 = send_core(down_four), send_core(down_m1)
    late = [last_far[mask] for mask in last_late]
    down_m2, down_m3, down_c0, down_c1, hidden, *late = hold(
        down_m2, down_m3, down_c0, down_c1, hidden, *late
    )
    last_far.update(zip(last_late, late))

    last_all = join(last_four, *[last_far[mask] for mask in far_masks()])
    last_there = send_core(last_all)
    down_c2, down_c3 = send_core(down_m2), send_core(down_m3)
    last_there, down_c2, down_c3 = hold(last_there, down_c2, down_c3)
    to_latent, decode = [Rows([last_all], [last_there], piece, False) for piece in last_pieces]
    down = Rows(
        [down_four, down_m1, down_m2, down_m3], [down_c0, down_c1, down_c2, down_c3], down_pieces[0]
    )
    carried, moments, sample, kl_part = latent_kernel(
        table, hidden, middle, noise_rows, centre, spread, down, to_latent
    )
    kl_sum = kl_part + send_core(kl_part)
    kl_sum, sample = hold(kl_sum, sample)
    decoded, grad_decode, grad_sample, grad_bias = decode_kernel(
        table, sample, cotangent, turned, decode
    )
    kl_near = [send(kl_sum, bit, bit) for bit in (2, 4, 6)]
    kl_sum = sum(kl_near, kl_sum)
    kl_sum, grad_sample, decoded = hold(kl_sum, grad_sample, decoded)
    kl_far = [far_exchange(kl_sum, mask) for mask in far_masks()]
    plain, factor, comp = factors_kernel(
        grad_sample, moments, noise_rows, centre, spread, choose.astype(LOW)
    )
    kl_sum = sum(kl_far, kl_sum)
    kl_sum, grad_decode, plain, factor, grad_bias, decoded = hold(
        kl_sum, grad_decode, plain, factor, grad_bias, decoded
    )
    decoded_there = send_core(decoded)

    far = lax.axis_size("dp") // 4
    kl_weight = jnp.minimum(1.0, (plan_step + 1).astype(FULL) / WARM)
    grad_carried, comp, last_own, last_other = moments_kernel(
        table,
        kl_weight,
        total_cells,
        kl_sum,
        plain,
        factor,
        carried,
        comp,
        grad_decode,
        to_latent,
        Slots(rows + decode_rows, width),
    )
    last_own, last_other, grad_carried, hidden = hold(last_own, last_other, grad_carried, hidden)
    last_got = send_core(last_other)
    down_own, down_other = weight_grad(
        table, hidden, [grad_carried], Slots(down_rows, width), down_rows, "grad_down"
    )
    last_got, down_own, down_other, grad_carried = hold(
        last_got, down_own, down_other, grad_carried
    )

    down_got = send_core(down_other)
    turns = [slice(turn * far, (turn + 1) * far) for turn in range(4)]
    last_m3, last_m2 = [near_second(add_low(last_own[t], last_got[t])) for t in (turns[3], turns[2])]
    grad_up_proj = up_back_kernel(table, grad_carried, slope, down)
    down_got, grad_up_proj, last_m3, last_m2 = hold(down_got, grad_up_proj, last_m3, last_m2)

    down_m3, down_m2 = [near_second(add_low(down_own[t], down_got[t])) for t in (turns[3], turns[2])]
    last_m1 = near_first(add_all(last_own[turns[1]], [last_got[turns[1]], last_m3]).astype(LOW))
    grad_middle, grad_branch, grad_mixed, grad_gain_two = middle_back_kernel(
        table, grad_up_proj, grad_carried, middle, turned, up, out_proj
    )
    up_own, up_other = weight_grad(
        table, second_in, [grad_up_proj], Slots(rows, up_cols), rows, "grad_up"
    )
    down_m3, down_m2, last_m1, up_own, up_other, grad_mixed = hold(
        down_m3, down_m2, last_m1, up_own, up_other, grad_mixed
    )

    up_got = send_core(up_other)
    down_m1 = near_first(add_all(down_own[turns[1]], [down_got[turns[1]], down_m3]).astype(LOW))
    last_low = add_all(last_own[turns[0]], [last_got[turns[0]], last_m2, last_m1]).astype(LOW)
    last_far = far_slots(last_low, 1)
    grad_out = left_product(mixed, grad_branch).astype(LOW)
    grad_packed = attention_backward(packed, attn, grad_mixed)
    up_got, down_m1, grad_out, *grad_packed = hold(
        up_got, down_m1, grad_out, *grad_packed, *last_far
    )
    grad_packed, last_far = grad_packed[:3], grad_packed[3:]

    up_m3, up_m2 = [near_second(add_low(up_own[t], up_got[t])) for t in (turns[3], turns[2])]
    down_low = add_all(down_own[turns[0]], [down_got[turns[0]], down_m2, down_m1]).astype(LOW)
    down_far = far_slots(down_low, 1)
    grad_inputs, grad_gain_one = input_back_kernel(
        table, grad_packed, grad_middle, inputs, turned, qkv
    )
    up_m3, up_m2, grad_inputs, grad_gain_one, grad_packed_q, *down_far = hold(
        up_m3, up_m2, grad_inputs, grad_gain_one, grad_packed[0], *down_far
    )
    grad_packed = [grad_packed_q, *grad_packed[1:]]

    up_m1 = near_first(add_all(up_own[turns[1]], [up_got[turns[1]], up_m3]).astype(LOW))
    tables_grad = comp.reshape(2, comps, devices, comp_cols)
    tables_grad = tables_grad.transpose(2, 0, 1, 3).reshape(devices * rows, lanes)
    columns = [one.reshape(width, 1) for one in (grad_gain_one, grad_gain_two, grad_bias)]
    small_grads = small_block(columns, tables_grad).astype(LOW)
    first_own, first_other = weight_grad(
        table,
        first_in,
        grad_packed,
        Slots(rows, qkv_cols + out_cols + 128),
        rows,
        "grad_qkv",
        [(grad_out, rows, 0, qkv_cols), (small_grads, rows, 0, qkv_cols + out_cols)],
    )
    up_m1, first_own, first_other = hold(up_m1, first_own, first_other)

    first_got = send_core(first_other)
    up_low = add_all(up_own[turns[0]], [up_got[turns[0]], up_m2, up_m1]).astype(LOW)
    first_got, up_low, grad_inputs = hold(first_got, up_low, grad_inputs)

    first_m3, first_m2 = [
        near_second(add_low(first_own[t], first_got[t])) for t in (turns[3], turns[2])
    ]
    up_far = far_slots(up_low, 1)
    down_sum = add_all(down_low[0], [one[0] for one in down_far])
    last_sum = add_all(last_low[0], [one[0] for one in last_far])
    first_m3, first_m2, down_sum, last_sum, *up_far = hold(
        first_m3, first_m2, down_sum, last_sum, *up_far
    )

    first_m1 = near_first(add_all(first_own[turns[1]], [first_got[turns[1]], first_m3]).astype(LOW))
    inputs_there = send_core(grad_inputs)
    result = jnp.where(
        core == 0,
        jnp.concatenate([grad_inputs, inputs_there], axis=0),
        jnp.concatenate([decoded_there, decoded], axis=0).astype(FULL),
    )[None]
    up_sum = add_all(up_low[0], [one[0] for one in up_far])
    first_m1, result, up_sum = hold(first_m1, result, up_sum)

    first_low = add_all(first_own[turns[0]], [first_got[turns[0]], first_m2, first_m1]).astype(LOW)
    first_far = far_slots(first_low, 1)
    first_sum = add_all(first_low[0], [one[0] for one in first_far])
    small_sum = first_sum[:, qkv_cols + out_cols :]
    comp_mean_sum, comp_logvar_sum = small_sum[:, 16 : 16 + lanes].reshape(2, comps, comp_cols)
    return (
        result,
        small_sum[:, 0],
        first_sum[:, :qkv_cols],
        first_sum[:, qkv_cols : qkv_cols + out_cols],
        small_sum[:, 1],
        up_sum,
        down_sum,
        last_sum[:rows],
        last_sum[rows:],
        small_sum[:, 2],
        comp_mean_sum,
        comp_logvar_sum,
    )


def solution(mesh):
    split = P(EVERY)
    wide = P(EVERY, None)
    tall = P(None, EVERY)
    ends = P("pipe", "dp", None)
    return jax.shard_map(
        local,
        mesh=mesh,
        in_specs=(
            ends,
            P("dp", None),
            P("dp"),
            P("dp", None),
            P(),
            split,
            wide,
            wide,
            split,
            wide,
            wide,
            wide,
            wide,
            split,
            tall,
            tall,
        ),
        out_specs=(ends, split, wide, wide, split, wide, wide, wide, wide, split, tall, tall),
        check_vma=False,
    )
```

time: 652 us -> 457 us (0.70)
  waiting for transfers between devices: 278 us -> 140 us
  matrix products: 87.6 us -> 6.83 us
  Pallas kernels: 95.4 us -> 157 us
  local copies, waits for them, and re-layouts: 69 us -> 34.1 us
    ppermute x60 -> x74, waiting for transfers between devices: 278 us -> 140 us  [send(): return lax.ppermute(value, EVERY, pairs)]
    pallas_call x8 -> x13, Pallas kernels: 64 us -> 126 us  [the longest x3 28.1 us: weight_grad(): pl.pallas_call(kernel, grid=(steps,), in_specs=[SCALARS, pl.BlockSpec((ce...]
    unnamed x186 -> x106, local copies, waits for them, and re-layouts: 54 us -> 10.8 us
    dot_general x8 -> x0, matrix products: 37.1 us -> none  [the longest x6 33.9 us: right_product(): lax.dot_general(left_side, right_side, (((1,), (1,)), ((), ())), preferre...]
    dot_general x8 -> x2, matrix products: 26.7 us -> 4.15 us  [matmul(): return jnp.dot(left_side, right_side, preferred_element_type=FULL)]
    dot_general x6 -> x1, matrix products: 23.8 us -> 2.69 us  [left_product(): lax.dot_general(left_side, right_side, (((0,), (0,)), ((), ())), preferre...]
    convert_element_type x5 -> x10, other arithmetic: 2.83 us -> 20.5 us  [the longest x1 3.7 us: local(): inputs = jnp.where(core == 0, kept, got).astype(FULL)]
    convert_element_type x8 -> x4, other arithmetic: 14.8 us -> 9.67 us  [add_low(): return (one.astype(FULL) + two.astype(FULL)).astype(LOW)]
  transfers between devices with their start and end apart: 60 -> 74, of which waited for: 27 -> 27; matrix products, arithmetic and copies ran while one was open for 12% -> 13% of each run, Pallas kernels for 6% -> 30%
where the time goes in v2:
time: 457 us; the launch traced here: 452 us
  Pallas kernels  157 us (34%)
  waiting for transfers between devices  140 us (31%)
  starting transfers between devices  67.5 us (15%)
  other arithmetic  44 us (10%)
  local copies, waits for them, and re-layouts  34.1 us (7%)
  matrix products  6.83 us (1%)
    ppermute x74, waiting for transfers between devices, send(): return lax.ppermute(value, EVERY, pairs)  140 us
    ppermute x74, starting transfers between devices, send(): return lax.ppermute(value, EVERY, pairs)  67.5 us
    pallas_call x3, Pallas kernels, weight_grad(): pl.pallas_call(kernel, grid=(steps,), in_specs=[SCALARS, pl.BlockSpec((ce...  28.1 us
    pallas_call x1, Pallas kernels, attention_backward(): pl.pallas_call(kernel, grid=(steps,), in_specs=[pl.BlockSpec((cells, 128)...  17.1 us
    pallas_call x1, Pallas kernels, latent_kernel(): pl.pallas_call(kernel, grid_spec=by_region(steps, [pl.BlockSpec((cells, t...  14.5 us
    pallas_call x1, Pallas kernels, middle_back_kernel(): pl.pallas_call(kernel, in_specs=[SCALARS, ANYWHERE] + [INSIDE] * 3 + [ANY...  14.2 us
    pallas_call x1, Pallas kernels, attention_forward(): pl.pallas_call(kernel, grid=(steps,), in_specs=[pl.BlockSpec((cells, 1),...  13.8 us
    pallas_call x1, Pallas kernels, up_kernel(): pl.pallas_call(kernel, grid=(cols // tile,), in_specs=[SCALARS, whole(cel...  13.6 us
  transfers between devices with their start and end apart: 74, of which 27 were waited for; matrix products, arithmetic and copies ran while one was open for 13% of the time, Pallas kernels for 30%

profile of v2, /device:TPU:8, one launch (start us, length us, event | category | flops | bytes accessed | tf_op | source)
XLA Modules:
  0.0 452.3 jit_solution(5416913422733892735)
XLA Ops:
  17.9 9.5 %collective-permute-done.4 = bf16[1,32,4224]{2,1,0:T(8,128)(2,1)} collective-permute-done((bf16[1,32,4224]{2,1,0:T(8,128)(2,1)S(1)}, bf16[1,32,4224]{2,1,0:T(8,128)(2,1)}, u32[]{:S(2)}, u32[]{:S(2)}) %collective-permute-start.4) | collective-permute-done | bytes 270368 | tf_op jit(solution)/shard_map/ppermute | solution.py:31
  27.4 5.8 %collective-permute-done.5 = bf16[1,32,4224]{2,1,0:T(8,128)(2,1)} collective-permute-done((bf16[1,32,4224]{2,1,0:T(8,128)(2,1)S(1)}, bf16[1,32,4224]{2,1,0:T(8,128)(2,1)}, u32[]{:S(2)}, u32[]{:S(2)}) %collective-permute-start.5) | collective-permute-done | bytes 270368 | tf_op jit(solution)/shard_map/ppermute | solution.py:31
  40.2 11.5 %collective-permute-done.10 = bf16[1,32,4096]{2,1,0:T(8,128)(2,1)S(1)} collective-permute-done((bf16[1,32,4096]{2,1,0:T(8,128)(2,1)S(1)}, bf16[1,32,4096]{2,1,0:T(8,128)(2,1)S(1)}, u32[]{:S(2)}, u32[]{:S(2)}) %collective-permute-start.10) | collective-permute-done | bytes 262176 | tf_op jit(solution)/shard_map/ppermute | solution.py:31
  62.5 13.1 %collective-permute-done.11.rest_3_.rest_11_ = bf16[4,32,4224]{2,1,0:T(8,128)(2,1)S(1)} collective-permute-done((bf16[4,32,4224]{2,1,0:T(8,128)(2,1)S(1)}, bf16[4,32,4224]{2,1,0:T(8,128)(2,1)S(1)}, u32[]{:S(2)}, u32[]{:S(2)}) %collective-permute-start.11) | collective-permute-done | bytes 1081376 | tf_op jit(solution)/shard_map/ppermute | solution.py:31
  91.2 9.8 %first.1 = (bf16[512,1024]{1,0:T(8,128)(2,1)}, bf16[512,3072]{1,0:T(8,128)(2,1)}, bf16[1024,128]{1,0:T(8,128)(2,1)}, f32[128,1024]{1,0:T(8,128)}) custom-call(s32[96]{0:T(128)} %concatenate.64.table_ref, f32[512,1024]{1,0:T(8,128)} %subtract_multiply_fusion.normed_ref, bf16[4,32,4224]{2,1,0:T(8,128)(2,1)} %copy-done.2, bf16[4,32,4224]{2,1,0:T(8,128)(2,1)} %copy-done.3, ...), custom_call_target="tpu_custom_call" | custom-call | flops 1024 | bytes 1024 | tf_op jit(solution)/shard_map/first/pallas_call | solution.py:232
  101.0 13.8 %attention_forward.1 = (bf16[512,1024]{1,0:T(8,128)(2,1)}, bf16[16,512,512]{2,1,0:T(8,128)(2,1)}) custom-call(s32[512,1]{1,0:T(8,128)} %copy.35.seg_col, s32[1,512]{1,0:T(1,128)} %constant_dynamic-slice_fusion.1.seg_row, bf16[512,3072]{1,0:T(8,128)(2,1)} %get-tuple-element.194.q_ref.k_ref.v_ref, bf16[512,3072]{1,0:T(8,128)(2,1)} %get-tuple-element.194.q_ref.k_ref.v_ref, ...), custom_call_target="tpu_custom_call" | custom-call | flops 1024 | bytes 1024 | tf_op jit(solution)/shard_map/attention_forward/pallas_call | solution.py:806
  131.9 5.9 %branch.1 = (f32[512,1024]{1,0:T(8,128)}, bf16[512,1024]{1,0:T(8,128)(2,1)}) custom-call(s32[96]{0:T(128)} %concatenate.64.table_ref, bf16[512,1024]{1,0:T(8,128)(2,1)} %get-tuple-element.201.mixed_ref, f32[512,1024]{1,0:T(8,128)} %get-tuple-element.333.in_ref, f32[128,1024]{1,0:T(8,128)} %get-tuple-element.202.turned_ref, bf16[4,32,4224]{2,1,0:T(8,128)(2,1)} %copy-done.2, ...), custom_call_target="tpu_custom_call" | custom-call | flops 1024 | bytes 1024 | tf_op jit(solution)/shard_map/branch/pallas_call | solution.py:273
  153.3 13.6 %up.1 = (bf16[512,4096]{1,0:T(8,128)(2,1)}, bf16[512,4096]{1,0:T(8,128)(2,1)}) custom-call(s32[96]{0:T(128)} %concatenate.64.table_ref, bf16[512,1024]{1,0:T(8,128)(2,1)} %get-tuple-element.214.in_ref.left_ref, bf16[4,32,4096]{2,1,0:T(8,128)(2,1)} %pad_maximum_fusion.1.rest_0_, bf16[4,32,4096]{2,1,0:T(8,128)(2,1)} %collective-permute-done.16.rest_1_, ...), custom_call_target="tpu_custom_call" | custom-call | flops 1024 | bytes 1024 | tf_op jit(solution)/shard_map/up/pallas_call | solution.py:316
  183.1 14.5 %latent.1 = (bf16[512,1024]{1,0:T(8,128)(2,1)}, f32[512,1024]{1,0:T(8,128)}, bf16[512,512]{1,0:T(8,128)(2,1)}, f32[1,512]{1,0:T(1,128)}) custom-call(s32[96]{0:T(128)} %concatenate.64.table_ref, bf16[512,4096]{1,0:T(8,128)(2,1)} %get-tuple-element.259.hidden_ref.left_ref, f32[512,1024]{1,0:T(8,128)} %get-tuple-element.222.mid_ref, ...), custom_call_target="tpu_custom_call" | custom-call | flops 1024 | bytes 1024 | tf_op jit(solution)/shard_map/latent/pallas_call | solution.py:366
  203.2 5.0 %decode.1 = (bf16[512,1024]{1,0:T(8,128)(2,1)}, bf16[512,1024]{1,0:T(8,128)(2,1)}, f32[512,512]{1,0:T(8,128)}, f32[1,1024]{1,0:T(1,128)}) custom-call(s32[96]{0:T(128)} %concatenate.64.table_ref, bf16[512,512]{1,0:T(8,128)(2,1)} %get-tuple-element.238.sample_ref, bf16[512,1024]{1,0:T(8,128)(2,1)} %get-tuple-element.343.dy_ref, ...), custom_call_target="tpu_custom_call" | custom-call | flops 1024 | bytes 1024 | tf_op jit(solution)/shard_map/decode/pallas_call | solution.py:407
  213.3 5.8 %factors.1 = (f32[512,1024]{1,0:T(8,128)}, f32[512,1024]{1,0:T(8,128)}, f32[2,16,512]{2,1,0:T(8,128)}) custom-call(f32[512,512]{1,0:T(8,128)} %get-tuple-element.243.back_ref, f32[512,1024]{1,0:T(8,128)} %get-tuple-element.244.mom_ref, f32[512,512]{1,0:T(8,128)} %constant_dynamic-slice_fusion.noise_ref, f32[512,512]{1,0:T(8,128)} %fusion.2.centre_ref, ...), custom_call_target="tpu_custom_call" | custom-call | flops 1024 | bytes 1024 | tf_op jit(solution)/shard_map/factors/pallas_call | solution.py:444
  219.7 7.0 %moments.1 = (bf16[512,1024]{1,0:T(8,128)(2,1)}, f32[2,16,512]{2,1,0:T(8,128)}, bf16[16,48,1024]{2,1,0:T(8,128)(2,1)}, bf16[16,48,1024]{2,1,0:T(8,128)(2,1)}) custom-call(s32[96]{0:T(128)} %concatenate.64.table_ref, f32[1]{0:T(128)S(6)} %min.3.weight_ref, f32[1,512]{1,0:T(1,128)} %add_add_fusion.kl_ref, f32[512,1024]{1,0:T(8,128)} %get-tuple-element.250.plain_ref, ...), custom_call_target="tpu_custom_call" | custom-call | flops 1024 | bytes 1024 | tf_op jit(solution)/shard_map/moments/pallas_call | solution.py:506
  226.7 10.7 %grad_down.1 = (bf16[16,128,1024]{2,1,0:T(8,128)(2,1)}, bf16[16,128,1024]{2,1,0:T(8,128)(2,1)}) custom-call(s32[96]{0:T(128)} %concatenate.64.table_ref, bf16[512,4096]{1,0:T(8,128)(2,1)} %get-tuple-element.259.hidden_ref.left_ref, bf16[512,1024]{1,0:T(8,128)(2,1)} %get-tuple-element.265.rest_0_.grad_ref.gc_ref), custom_call_target="tpu_custom_call" | custom-call | flops 1024 | bytes 1024 | tf_op jit(solution)/shard_map/grad_down/pallas_call | solution.py:574
  240.3 10.9 %up_back.1.rest_0_.gu_ref = bf16[512,4096]{1,0:T(8,128)(2,1)} custom-call(s32[96]{0:T(128)} %concatenate.64.table_ref, bf16[512,1024]{1,0:T(8,128)(2,1)} %get-tuple-element.265.rest_0_.grad_ref.gc_ref, bf16[512,4096]{1,0:T(8,128)(2,1)} %get-tuple-element.266.slope_ref, bf16[4,128,1024]{2,1,0:T(8,128)(2,1)} %copy-done.12, ...), custom_call_target="tpu_custom_call" | custom-call | flops 1024 | bytes 1024 | tf_op jit(solution)/shard_map/up_back/pallas_call | solution.py:613
  260.8 14.2 %middle_back.1 = (f32[512,1024]{1,0:T(8,128)}, bf16[512,1024]{1,0:T(8,128)(2,1)}, bf16[512,1024]{1,0:T(8,128)(2,1)}, f32[1,1024]{1,0:T(1,128)}) custom-call(s32[96]{0:T(128)} %concatenate.64.table_ref, bf16[512,4096]{1,0:T(8,128)(2,1)} %up_back.1.rest_0_.gu_ref, bf16[512,1024]{1,0:T(8,128)(2,1)} %get-tuple-element.265.rest_0_.grad_ref.gc_ref, ...), custom_call_target="tpu_custom_call" | custom-call | flops 1024 | bytes 1024 | tf_op jit(solution)/shard_map/middle_back/pallas_call | solution.py:657
  275.0 8.9 %grad_up.1 = (bf16[16,32,4096]{2,1,0:T(8,128)(2,1)}, bf16[16,32,4096]{2,1,0:T(8,128)(2,1)}) custom-call(s32[96]{0:T(128)} %concatenate.64.table_ref, bf16[512,1024]{1,0:T(8,128)(2,1)} %get-tuple-element.214.in_ref.left_ref, bf16[512,4096]{1,0:T(8,128)(2,1)} %up_back.1.rest_0_.gu_ref), custom_call_target="tpu_custom_call" | custom-call | flops 1024 | bytes 1024 | tf_op jit(solution)/shard_map/grad_up/pallas_call | solution.py:574
  299.8 17.1 %attention_backward.1 = (bf16[512,1024]{1,0:T(8,128)(2,1)}, bf16[512,1024]{1,0:T(8,128)(2,1)}, bf16[512,1024]{1,0:T(8,128)(2,1)}) custom-call(bf16[512,3072]{1,0:T(8,128)(2,1)} %get-tuple-element.194.q_ref.k_ref.v_ref, bf16[512,3072]{1,0:T(8,128)(2,1)} %get-tuple-element.194.q_ref.k_ref.v_ref, bf16[512,3072]{1,0:T(8,128)(2,1)} %get-tuple-element.194.q_ref.k_ref.v_ref, ...), custom_call_target="tpu_custom_call" | custom-call | flops 1024 | bytes 1024 | tf_op jit(solution)/shard_map/attention_backward/pallas_call | solution.py:855
  331.5 11.5 %input_back.1 = (f32[512,1024]{1,0:T(8,128)}, f32[1,1024]{1,0:T(1,128)}) custom-call(s32[96]{0:T(128)} %concatenate.64.table_ref, bf16[512,1024]{1,0:T(8,128)(2,1)} %get-tuple-element.297.gq_ref.rest_0_, bf16[512,1024]{1,0:T(8,128)(2,1)} %get-tuple-element.288.gk_ref.rest_1_, bf16[512,1024]{1,0:T(8,128)(2,1)} %get-tuple-element.289.gv_ref.rest_2_, ...), custom_call_target="tpu_custom_call" | custom-call | flops 1024 | bytes 1024 | tf_op jit(solution)/shard_map/input_back/pallas_call | solution.py:699
  343.0 5.9 %collective-permute-done.59 = bf16[1,128,1024]{2,1,0:T(8,128)(2,1)S(1)} collective-permute-done((bf16[1,128,1024]{2,1,0:T(8,128)(2,1)S(1)}, bf16[1,128,1024]{2,1,0:T(8,128)(2,1)S(1)}, u32[]{:S(2)}, u32[]{:S(2)}) %collective-permute-start.59) | collective-permute-done | bytes 262176 | tf_op jit(solution)/shard_map/ppermute | solution.py:31
  363.5 8.5 %grad_qkv.1 = (bf16[16,32,4224]{2,1,0:T(8,128)(2,1)}, bf16[16,32,4224]{2,1,0:T(8,128)(2,1)}) custom-call(s32[96]{0:T(128)} %concatenate.64.table_ref, bf16[512,1024]{1,0:T(8,128)(2,1)} %get-tuple-element.296.left_ref, bf16[512,1024]{1,0:T(8,128)(2,1)} %get-tuple-element.297.gq_ref.rest_0_, bf16[512,1024]{1,0:T(8,128)(2,1)} %get-tuple-element.288.gk_ref.rest_1_, ...), custom_call_target="tpu_custom_call" | custom-call | flops 1024 | bytes 1024 | tf_op jit(solution)/shard_map/grad_qkv/pallas_call | solution.py:574
  386.8 5.8 %collective-permute-done.65 = bf16[1,32,4096]{2,1,0:T(8,128)(2,1)S(1)} collective-permute-done((bf16[1,32,4096]{2,1,0:T(8,128)(2,1)S(1)}, bf16[1,32,4096]{2,1,0:T(8,128)(2,1)S(1)}, u32[]{:S(2)}, u32[]{:S(2)}) %collective-permute-start.65) | collective-permute-done | bytes 262176 | tf_op jit(solution)/shard_map/ppermute | solution.py:31
  392.6 10.7 %collective-permute-done.66 = bf16[1,32,4096]{2,1,0:T(8,128)(2,1)S(1)} collective-permute-done((bf16[1,32,4096]{2,1,0:T(8,128)(2,1)S(1)}, bf16[1,32,4096]{2,1,0:T(8,128)(2,1)S(1)}, u32[]{:S(2)}, u32[]{:S(2)}) %collective-permute-start.66) | collective-permute-done | bytes 262176 | tf_op jit(solution)/shard_map/ppermute | solution.py:31
  413.6 10.3 %collective-permute-done.68 = bf16[4,32,4224]{2,1,0:T(8,128)(2,1)S(1)} collective-permute-done((bf16[4,32,4224]{2,1,0:T(8,128)(2,1)S(1)}, bf16[4,32,4224]{2,1,0:T(8,128)(2,1)S(1)}, u32[]{:S(2)}, u32[]{:S(2)}) %collective-permute-start.68) | collective-permute-done | bytes 1081376 | tf_op jit(solution)/shard_map/ppermute | solution.py:31
  434.0 10.7 %collective-permute-done.72 = bf16[1,32,4224]{2,1,0:T(8,128)(2,1)S(1)} collective-permute-done((bf16[1,32,4224]{2,1,0:T(8,128)(2,1)S(1)}, bf16[1,32,4224]{2,1,0:T(8,128)(2,1)S(1)}, u32[]{:S(2)}, u32[]{:S(2)}) %collective-permute-start.72) | collective-permute-done | bytes 270368 | tf_op jit(solution)/shard_map/ppermute | solution.py:31
  (326 shorter events, 209.4 us)
Async XLA Ops:
  9.0 24.3 %collective-permute-start.5 = (bf16[1,32,4224]{2,1,0:T(8,128)(2,1)S(1)}, bf16[1,32,4224]{2,1,0:T(8,128)(2,1)}, u32[]{:S(2)}, u32[]{:S(2)}) collective-permute-start(bf16[1,32,4224]{2,1,0:T(8,128)(2,1)S(1)} %bitcast.52), channel_id=1, source_target_pairs={{0,24},{1,25},{2,26},{3,27},{4,28},{5,29},{6,30},{7,31},{8,16},{9,... | collective-permute-start | bytes 811016 | tf_op jit(solution)/shard_map/ppermute | solution.py:31
  34.6 25.7 %collective-permute-start.6 = (bf16[4,32,4224]{2,1,0:T(8,128)(2,1)S(1)}, bf16[4,32,4224]{2,1,0:T(8,128)(2,1)S(1)}, u32[]{:S(2)}, u32[]{:S(2)}) collective-permute-start(bf16[4,32,4224]{2,1,0:T(8,128)(2,1)S(1)} %pad_maximum_fusion.rest_0_.rest_8_), channel_id=1, source_target_pairs={{0,2},{1,5},{2,0},{3,7},{4,6},{5,1},{6,4},{7,3},{8,10},{9,13},{10,... | collective-permute-start | bytes 3244040 | tf_op jit(solution)/shard_map/ppermute | solution.py:31
  36.2 24.2 %collective-permute-start.7 = (bf16[4,32,4224]{2,1,0:T(8,128)(2,1)S(1)}, bf16[4,32,4224]{2,1,0:T(8,128)(2,1)S(1)}, u32[]{:S(2)}, u32[]{:S(2)}) collective-permute-start(bf16[4,32,4224]{2,1,0:T(8,128)(2,1)S(1)} %pad_maximum_fusion.rest_0_.rest_8_), channel_id=1, source_target_pairs={{0,4},{1,3},{2,6},{3,1},{4,0},{5,7},{6,2},{7,5},{8,12},{9,11},{10,... | collective-permute-start | bytes 3244040 | tf_op jit(solution)/shard_map/ppermute | solution.py:31
  81.0 35.0 %collective-permute-start.16 = (bf16[4,32,4096]{2,1,0:T(8,128)(2,1)}, bf16[4,32,4096]{2,1,0:T(8,128)(2,1)}, u32[]{:S(2)}, u32[]{:S(2)}) collective-permute-start(bf16[4,32,4096]{2,1,0:T(8,128)(2,1)} %pad_maximum_fusion.1.rest_0_), channel_id=1, source_target_pairs={{0,2},{1,5},{2,0},{3,7},{4,6},{5,1},{6,4},{7,3},{8,10},{9,13},{10,... | collective-permute-start | bytes 3145736 | tf_op jit(solution)/shard_map/ppermute | solution.py:31
  82.7 33.3 %collective-permute-start.17 = (bf16[4,32,4096]{2,1,0:T(8,128)(2,1)}, bf16[4,32,4096]{2,1,0:T(8,128)(2,1)}, u32[]{:S(2)}, u32[]{:S(2)}) collective-permute-start(bf16[4,32,4096]{2,1,0:T(8,128)(2,1)} %pad_maximum_fusion.1.rest_0_), channel_id=1, source_target_pairs={{0,4},{1,3},{2,6},{3,1},{4,0},{5,7},{6,2},{7,5},{8,12},{9,11},{10,... | collective-permute-start | bytes 3145736 | tf_op jit(solution)/shard_map/ppermute | solution.py:31
  84.4 31.5 %collective-permute-start.18 = (bf16[1,128,1024]{2,1,0:T(8,128)(2,1)}, bf16[1,128,1024]{2,1,0:T(8,128)(2,1)}, u32[]{:S(2)}, u32[]{:S(2)}) collective-permute-start(bf16[1,128,1024]{2,1,0:T(8,128)(2,1)} %bitcast.8), channel_id=1, source_target_pairs={{0,8},{1,9},{2,10},{3,11},{4,12},{5,13},{6,14},{7,15},{8,0},{9,1},... | collective-permute-start | bytes 786440 | tf_op jit(solution)/shard_map/ppermute | solution.py:31
  84.4 31.6 %collective-permute-start.19 = (bf16[1,128,1024]{2,1,0:T(8,128)(2,1)}, bf16[1,128,1024]{2,1,0:T(8,128)(2,1)}, u32[]{:S(2)}, u32[]{:S(2)}) collective-permute-start(bf16[1,128,1024]{2,1,0:T(8,128)(2,1)} %bitcast.8), channel_id=1, source_target_pairs={{0,16},{1,17},{2,18},{3,19},{4,20},{5,21},{6,22},{7,23},{8,24},{9,... | collective-permute-start | bytes 786440 | tf_op jit(solution)/shard_map/ppermute | solution.py:31
  87.5 28.5 %collective-permute-start.20 = (bf16[1,128,1024]{2,1,0:T(8,128)(2,1)}, bf16[1,128,1024]{2,1,0:T(8,128)(2,1)}, u32[]{:S(2)}, u32[]{:S(2)}) collective-permute-start(bf16[1,128,1024]{2,1,0:T(8,128)(2,1)} %bitcast.8), channel_id=1, source_target_pairs={{0,24},{1,25},{2,26},{3,27},{4,28},{5,29},{6,30},{7,31},{8,16},{9,... | collective-permute-start | bytes 786440 | tf_op jit(solution)/shard_map/ppermute | solution.py:31
  118.9 26.3 %collective-permute-start.23 = (bf16[4,128,1024]{2,1,0:T(8,128)(2,1)S(1)}, bf16[4,128,1024]{2,1,0:T(8,128)(2,1)}, u32[]{:S(2)}, u32[]{:S(2)}) collective-permute-start(bf16[4,128,1024]{2,1,0:T(8,128)(2,1)S(1)} %constant_dynamic-update-slice_fusion.rest_0_), channel_id=1, source_target_pairs={{0,2},{1,5},{2,0},{3,7},{4,6},{5,1},{6,4},{7,3},{8,10},{9,13},{10,... | collective-permute-start | bytes 3145736 | tf_op jit(solution)/shard_map/ppermute | solution.py:31
  119.8 25.5 %collective-permute-start.22 = (bf16[4,32,4096]{2,1,0:T(8,128)(2,1)}, bf16[4,32,4096]{2,1,0:T(8,128)(2,1)}, u32[]{:S(2)}, u32[]{:S(2)}) collective-permute-start(bf16[4,32,4096]{2,1,0:T(8,128)(2,1)} %collective-permute-done.16.rest_1_), channel_id=1, source_target_pairs={{0,4},{1,3},{2,6},{3,1},{4,0},{5,7},{6,2},{7,5},{8,12},{9,11},{10,... | collective-permute-start | bytes 3145736 | tf_op jit(solution)/shard_map/ppermute | solution.py:31
  145.9 22.1 %collective-permute-start.21 = (bf16[4,128,1024]{2,1,0:T(8,128)(2,1)S(1)}, bf16[4,128,1024]{2,1,0:T(8,128)(2,1)}, u32[]{:S(2)}, u32[]{:S(2)}) collective-permute-start(bf16[4,128,1024]{2,1,0:T(8,128)(2,1)S(1)} %constant_dynamic-update-slice_fusion.rest_0_), channel_id=1, source_target_pairs={{0,4},{1,3},{2,6},{3,1},{4,0},{5,7},{6,2},{7,5},{8,12},{9,11},{10,... | collective-permute-start | bytes 3145736 | tf_op jit(solution)/shard_map/ppermute | solution.py:31
  147.4 24.6 %collective-permute-start.27 = (bf16[4,128,1024]{2,1,0:T(8,128)(2,1)}, bf16[4,128,1024]{2,1,0:T(8,128)(2,1)}, u32[]{:S(2)}, u32[]{:S(2)}) collective-permute-start(bf16[4,128,1024]{2,1,0:T(8,128)(2,1)} %collective-permute-done.23.rest_1_), channel_id=1, source_target_pairs={{0,4},{1,3},{2,6},{3,1},{4,0},{5,7},{6,2},{7,5},{8,12},{9,11},{10,... | collective-permute-start | bytes 3145736 | tf_op jit(solution)/shard_map/ppermute | solution.py:31
  255.8 28.1 %collective-permute-start.48 = (bf16[4,128,1024]{2,1,0:T(8,128)(2,1)}, bf16[4,128,1024]{2,1,0:T(8,128)(2,1)}, u32[]{:S(2)}, u32[]{:S(2)}) collective-permute-start(bf16[4,128,1024]{2,1,0:T(8,128)(2,1)} %get-tuple-element.340), channel_id=1, source_target_pairs={{0,4},{1,3},{2,6},{3,1},{4,0},{5,7},{6,2},{7,5},{8,12},{9,11},{10,... | collective-permute-start | bytes 3145736 | tf_op jit(solution)/shard_map/ppermute | solution.py:31
  257.4 29.0 %collective-permute-start.49 = (bf16[4,128,1024]{2,1,0:T(8,128)(2,1)}, bf16[4,128,1024]{2,1,0:T(8,128)(2,1)}, u32[]{:S(2)}, u32[]{:S(2)}) collective-permute-start(bf16[4,128,1024]{2,1,0:T(8,128)(2,1)} %get-tuple-element.339), channel_id=1, source_target_pairs={{0,4},{1,3},{2,6},{3,1},{4,0},{5,7},{6,2},{7,5},{8,12},{9,11},{10,... | collective-permute-start | bytes 3145736 | tf_op jit(solution)/shard_map/ppermute | solution.py:31
  259.0 24.9 %collective-permute-start.50 = (bf16[4,48,1024]{2,1,0:T(8,128)(2,1)S(1)}, bf16[4,48,1024]{2,1,0:T(8,128)(2,1)S(1)}, u32[]{:S(2)}, u32[]{:S(2)}) collective-permute-start(bf16[4,48,1024]{2,1,0:T(8,128)(2,1)S(1)} %add_convert_fusion.13), channel_id=1, source_target_pairs={{0,2},{1,5},{2,0},{3,7},{4,6},{5,1},{6,4},{7,3},{8,10},{9,13},{10,... | collective-permute-start | bytes 1179656 | tf_op jit(solution)/shard_map/ppermute | solution.py:31
  286.4 30.5 %collective-permute-start.51 = (bf16[16,32,4096]{2,1,0:T(8,128)(2,1)}, bf16[16,32,4096]{2,1,0:T(8,128)(2,1)}, u32[]{:S(2)}, u32[]{:S(2)}) collective-permute-start(bf16[16,32,4096]{2,1,0:T(8,128)(2,1)} %get-tuple-element.276), channel_id=1, source_target_pairs={{0,1},{1,0},{2,3},{3,2},{4,5},{5,4},{6,7},{7,6},{8,9},{9,8},{10,11... | collective-permute-start | bytes 12582920 | tf_op jit(solution)/shard_map/ppermute | solution.py:31
  289.9 27.1 %collective-permute-start.52 = (bf16[4,128,1024]{2,1,0:T(8,128)(2,1)}, bf16[4,128,1024]{2,1,0:T(8,128)(2,1)}, u32[]{:S(2)}, u32[]{:S(2)}) collective-permute-start(bf16[4,128,1024]{2,1,0:T(8,128)(2,1)} %add_convert_fusion.9), channel_id=1, source_target_pairs={{0,2},{1,5},{2,0},{3,7},{4,6},{5,1},{6,4},{7,3},{8,10},{9,13},{10,... | collective-permute-start | bytes 3145736 | tf_op jit(solution)/shard_map/ppermute | solution.py:31
  292.9 24.0 %collective-permute-start.53 = (bf16[1,48,1024]{2,1,0:T(8,128)(2,1)S(1)}, bf16[1,48,1024]{2,1,0:T(8,128)(2,1)S(1)}, u32[]{:S(2)}, u32[]{:S(2)}) collective-permute-start(bf16[1,48,1024]{2,1,0:T(8,128)(2,1)S(1)} %get-tuple-element.357), channel_id=1, source_target_pairs={{0,8},{1,9},{2,10},{3,11},{4,12},{5,13},{6,14},{7,15},{8,0},{9,1},... | collective-permute-start | bytes 294920 | tf_op jit(solution)/shard_map/ppermute | solution.py:31
  321.2 32.0 %collective-permute-start.56 = (bf16[4,32,4096]{2,1,0:T(8,128)(2,1)}, bf16[4,32,4096]{2,1,0:T(8,128)(2,1)}, u32[]{:S(2)}, u32[]{:S(2)}) collective-permute-start(bf16[4,32,4096]{2,1,0:T(8,128)(2,1)} %get-tuple-element.338), channel_id=1, source_target_pairs={{0,4},{1,3},{2,6},{3,1},{4,0},{5,7},{6,2},{7,5},{8,12},{9,11},{10,... | collective-permute-start | bytes 3145736 | tf_op jit(solution)/shard_map/ppermute | solution.py:31
  322.2 31.0 %collective-permute-start.57 = (bf16[4,32,4096]{2,1,0:T(8,128)(2,1)}, bf16[4,32,4096]{2,1,0:T(8,128)(2,1)S(1)}, u32[]{:S(2)}, u32[]{:S(2)}) collective-permute-start(bf16[4,32,4096]{2,1,0:T(8,128)(2,1)} %get-tuple-element.337), channel_id=1, source_target_pairs={{0,4},{1,3},{2,6},{3,1},{4,0},{5,7},{6,2},{7,5},{8,12},{9,11},{10,... | collective-permute-start | bytes 3145736 | tf_op jit(solution)/shard_map/ppermute | solution.py:31
  331.0 22.3 %collective-permute-start.60 = (bf16[1,128,1024]{2,1,0:T(8,128)(2,1)S(1)}, bf16[1,128,1024]{2,1,0:T(8,128)(2,1)S(1)}, u32[]{:S(2)}, u32[]{:S(2)}) collective-permute-start(bf16[1,128,1024]{2,1,0:T(8,128)(2,1)S(1)} %get-tuple-element.350), channel_id=1, source_target_pairs={{0,24},{1,25},{2,26},{3,27},{4,28},{5,29},{6,30},{7,31},{8,16},{9,... | collective-permute-start | bytes 786440 | tf_op jit(solution)/shard_map/ppermute | solution.py:31
  380.2 28.1 %collective-permute-start.63 = (bf16[4,32,4224]{2,1,0:T(8,128)(2,1)S(1)}, bf16[4,32,4224]{2,1,0:T(8,128)(2,1)S(1)}, u32[]{:S(2)}, u32[]{:S(2)}) collective-permute-start(bf16[4,32,4224]{2,1,0:T(8,128)(2,1)S(1)} %get-tuple-element.336), channel_id=1, source_target_pairs={{0,4},{1,3},{2,6},{3,1},{4,0},{5,7},{6,2},{7,5},{8,12},{9,11},{10,... | collective-permute-start | bytes 3244040 | tf_op jit(solution)/shard_map/ppermute | solution.py:31
  381.3 27.0 %collective-permute-start.64 = (bf16[4,32,4224]{2,1,0:T(8,128)(2,1)S(1)}, bf16[4,32,4224]{2,1,0:T(8,128)(2,1)S(1)}, u32[]{:S(2)}, u32[]{:S(2)}) collective-permute-start(bf16[4,32,4224]{2,1,0:T(8,128)(2,1)S(1)} %get-tuple-element.335), channel_id=1, source_target_pairs={{0,4},{1,3},{2,6},{3,1},{4,0},{5,7},{6,2},{7,5},{8,12},{9,11},{10,... | collective-permute-start | bytes 3244040 | tf_op jit(solution)/shard_map/ppermute | solution.py:31
  385.3 23.0 %collective-permute-start.67 = (bf16[1,32,4096]{2,1,0:T(8,128)(2,1)S(1)}, bf16[1,32,4096]{2,1,0:T(8,128)(2,1)S(1)}, u32[]{:S(2)}, u32[]{:S(2)}) collective-permute-start(bf16[1,32,4096]{2,1,0:T(8,128)(2,1)S(1)} %get-tuple-element.347), channel_id=1, source_target_pairs={{0,24},{1,25},{2,26},{3,27},{4,28},{5,29},{6,30},{7,31},{8,16},{9,... | collective-permute-start | bytes 786440 | tf_op jit(solution)/shard_map/ppermute | solution.py:31
  (100 other events, 1306.9 us)

commit v3 on v2

--- a/solution.py
+++ b/solution.py
@@ -139,11 +139,12 @@
         self.rows, self.cols = rows, cols
 
     def shapes(self):
-        return [jax.ShapeDtypeStruct((self.count, self.rows, self.cols), LOW)] * 2
+        return [jax.ShapeDtypeStruct((self.count // 2, self.rows, self.cols), LOW)] * 4
 
     def start(self, table, sources, outs, sem):
+        half = self.count // 2
         for slot in range(2 * self.count):
-            out = outs[slot // self.count].at[slot % self.count]
+            out = outs[slot // half].at[slot % half]
             for source, height, row, col in sources:
                 block = pl.multiple_of(table[self.base + slot] * height, height)
                 pltpu.make_async_copy(
@@ -152,24 +153,24 @@
                     sem,
                 ).start()
 
-
     def send(self, table, source, first_block, outs, sem):
+        half = self.count // 2
         own_core = table[0] % 2
+        columns = pl.ds(0, source.shape[1])
         for i in range(source.shape[0] // self.rows):
             slot = table[4 * self.count + first_block + i]
             part = source.at[pl.ds(i * self.rows, self.rows)]
-            columns = pl.ds(0, source.shape[1])
-
-            @pl.when(own_core == i % 2)
-            def _():
-                pltpu.make_async_copy(part, outs[0].at[slot, :, columns], sem).start()
-
-            @pl.when(own_core != i % 2)
-            def _():
-                pltpu.make_async_copy(part, outs[1].at[slot, :, columns], sem).start()
+            which = 2 * jnp.where(own_core == i % 2, 0, 1) + slot // half
+            for k, out in enumerate(outs):
+
+                @pl.when(which == k)
+                def _():
+                    target = out.at[lax.rem(slot, half), :, columns]
+                    pltpu.make_async_copy(part, target, sem).start()
 
 
 ANYWHERE = pl.BlockSpec(memory_space=pl.ANY)
+FAR_AWAY = pl.BlockSpec(memory_space=pltpu.HBM)
 SCALARS = pl.BlockSpec(memory_space=pltpu.SMEM)
 INSIDE = pl.BlockSpec(memory_space=pltpu.VMEM)
 
@@ -316,27 +317,27 @@
     return pl.pallas_call(
         kernel,
         grid=(cols // tile,),
-        in_specs=[SCALARS, whole(cells, width)] + [ANYWHERE] * parts,
+        in_specs=[SCALARS, whole(cells, width)] + [FAR_AWAY] * parts,
         out_specs=[pl.BlockSpec((cells, tile), lambda i: (0, i))] * 2,
         out_shape=[
             jax.ShapeDtypeStruct((cells, cols), LOW),
             jax.ShapeDtypeStruct((cells, cols), LOW),
         ],
         scratch_shapes=[pltpu.VMEM(weight.shape, LOW), pltpu.SemaphoreType.DMA((2,))],
-        compiler_params=params(),
+        compiler_params=params(22),
         cost_estimate=cost(2 * cells * width * cols, 22 << 20, 2 * cells * cols),
         name="up",
     )(table, second_in, *weight.operands)
 
 
-def latent_kernel(table, hidden, middle, noise, centre, spread, down, to_latent):
+def latent_kernel(table, hidden, middle, noise, choose, comp_tables, down, to_latent):
     cells, width = middle.shape
     latent = noise.shape[1]
     parts, more = len(down.operands), len(to_latent.operands)
     steps = down.count // 4
     tile = hidden.shape[1] // steps
 
-    def kernel(table_ref, hidden_ref, mid_ref, noise_ref, centre_ref, spread_ref, *rest):
+    def kernel(table_ref, hidden_ref, mid_ref, noise_ref, choose_ref, tables_ref, *rest):
         refs, rest = rest[:parts], rest[parts:]
         latent_refs, rest = rest[:more], rest[more:]
         carried_ref, moments_ref, sample_ref, kl_ref, total, held, latent_held, sems = rest
@@ -359,7 +360,8 @@
             moments_ref[...] = matmul(carried_ref[...], latent_held[...])
             mean_part, logvar = moments_ref[:, :latent], moments_ref[:, latent:]
             sample_ref[...] = (mean_part + jnp.exp(0.5 * logvar) * noise_ref[...]).astype(LOW)
-            gap, far = mean_part - centre_ref[...], spread_ref[...]
+            gap = mean_part - matmul(choose_ref[...], tables_ref[0])
+            far = matmul(choose_ref[...], tables_ref[1])
             diverge = 0.5 * (far - logvar + (jnp.exp(logvar) + gap * gap) * jnp.exp(-far) - 1.0)
             kl_ref[...] = jnp.sum(diverge, axis=0, keepdims=True)
 
@@ -368,8 +370,8 @@
         grid_spec=by_region(
             steps,
             [pl.BlockSpec((cells, tile), region_columns), whole(cells, width)]
-            + [whole(cells, latent)] * 3
-            + [ANYWHERE] * (parts + more),
+            + [whole(cells, latent), whole(*choose.shape), whole(*comp_tables.shape)]
+            + [FAR_AWAY] * (parts + more),
             [whole(cells, width), whole(cells, 2 * latent), whole(cells, latent), whole(1, latent)],
             [
                 pltpu.VMEM((cells, width), FULL),
@@ -384,10 +386,10 @@
             jax.ShapeDtypeStruct((cells, latent), LOW),
             jax.ShapeDtypeStruct((1, latent), FULL),
         ],
-        compiler_params=params(),
+        compiler_params=params(30),
         cost_estimate=cost(2 * cells * width * (hidden.shape[1] + width), 20 << 20),
         name="latent",
-    )(table, hidden, middle, noise, centre, spread, *down.operands, *to_latent.operands)
+    )(table, hidden, middle, noise, choose, comp_tables, *down.operands, *to_latent.operands)
 
 
 def decode_kernel(table, sample, cotangent, turned, decode):
@@ -406,7 +408,7 @@
 
     return pl.pallas_call(
         kernel,
-        in_specs=[SCALARS] + [INSIDE] * 3 + [ANYWHERE] * parts,
+        in_specs=[SCALARS] + [INSIDE] * 3 + [FAR_AWAY] * parts,
         out_specs=[INSIDE] * 4,
         out_shape=[
             jax.ShapeDtypeStruct((cells, width), LOW),
@@ -415,19 +417,20 @@
             jax.ShapeDtypeStruct((1, width), FULL),
         ],
         scratch_shapes=[pltpu.VMEM(decode.shape, LOW), pltpu.SemaphoreType.DMA((1,))],
-        compiler_params=params(),
+        compiler_params=params(16),
         cost_estimate=cost(6 * cells * width * latent, 8 << 20),
         name="decode",
     )(table, sample, cotangent, turned, *decode.operands)
 
 
-def factors_kernel(back, moments, noise, centre, spread, choose):
+def factors_kernel(back, moments, noise, choose, comp_tables):
     cells, latent = noise.shape
     comps = choose.shape[1]
 
-    def kernel(back_ref, mom_ref, noise_ref, centre_ref, spread_ref, choose_ref, plain_ref, factor_ref, comp_ref):
+    def kernel(back_ref, mom_ref, noise_ref, choose_ref, tables_ref, plain_ref, factor_ref, comp_ref):
         mean_part, logvar = mom_ref[:, :latent], mom_ref[:, latent:]
-        gap, shrink = mean_part - centre_ref[...], jnp.exp(-spread_ref[...])
+        gap = mean_part - matmul(choose_ref[...], tables_ref[0])
+        shrink = jnp.exp(-matmul(choose_ref[...], tables_ref[1]))
         ratio = jnp.exp(logvar) * shrink
         moved = gap * shrink
         factor_ref[:, :latent] = moved
@@ -443,17 +446,17 @@
 
     return pl.pallas_call(
         kernel,
-        in_specs=[INSIDE] * 6,
+        in_specs=[INSIDE] * 5,
         out_specs=[INSIDE] * 3,
         out_shape=[
             jax.ShapeDtypeStruct((cells, 2 * latent), FULL),
             jax.ShapeDtypeStruct((cells, 2 * latent), FULL),
             jax.ShapeDtypeStruct((2, comps, latent), FULL),
         ],
-        compiler_params=params(),
+        compiler_params=params(16),
         cost_estimate=cost(200 * cells * latent, 10 << 20),
         name="factors",
-    )(back, moments, noise, centre, spread, choose)
+    )(back, moments, noise, choose, comp_tables)
 
 
 def plain_slots(slots, grads):
@@ -466,7 +469,7 @@
             blocks = grad.reshape(slots.count, 2, height, grad.shape[1])
             blocks = jnp.take(blocks[:, core], owner, axis=0)
             result = result.at[:, row : row + height, col : col + grad.shape[1]].set(blocks)
-        results.append(result)
+        results += [result[: slots.count // 2], result[slots.count // 2 :]]
     return results
 
 
@@ -481,7 +484,7 @@
     def kernel(table_ref, weight_ref, kl_ref, plain_ref, factor_ref, carried_ref, comp_ref, gd_ref, *rest):
         refs, rest = rest[:parts], rest[parts:]
         gc_ref, comp_out, *rest = rest
-        outs, rest = rest[: 2 if direct else 1], rest[2 if direct else 1 :]
+        outs, rest = rest[: 4 if direct else 1], rest[4 if direct else 1 :]
         held, grads, sums, sems = rest
         to_latent.start(table_ref, refs, held, sems.at[pl.ds(0, 1)])
         mean = kl_ref[...] * (1.0 / total)
@@ -500,13 +503,13 @@
         arrived(held, sems.at[0])
         gc_ref[...] = right_product(grads[...], held[...]).astype(LOW)
         if direct:
-            arrived(outs[0], sems.at[1])
-            arrived(outs[1], sems.at[1])
+            for out in outs:
+                arrived(out, sems.at[1])
 
     results = pl.pallas_call(
         kernel,
-        in_specs=[SCALARS, SCALARS] + [INSIDE] * 6 + [ANYWHERE] * parts,
-        out_specs=[INSIDE] * 2 + ([ANYWHERE] * 2 if direct else [INSIDE]),
+        in_specs=[SCALARS, SCALARS] + [INSIDE] * 6 + [FAR_AWAY] * parts,
+        out_specs=[INSIDE] * 2 + ([FAR_AWAY] * 4 if direct else [INSIDE]),
         out_shape=[
             jax.ShapeDtypeStruct((cells, width), LOW),
             jax.ShapeDtypeStruct(comp.shape, FULL),
@@ -518,7 +521,7 @@
             pltpu.VMEM((width, 2 * latent), LOW),
             pltpu.SemaphoreType.DMA((2,)),
         ],
-        compiler_params=params(),
+        compiler_params=params(24),
         cost_estimate=cost(8 * cells * width * latent, 16 << 20),
         name="moments",
     )(table, kl_weight, kl_sum, plain, factor, carried, comp, grad_decode, *to_latent.operands)
@@ -538,22 +541,23 @@
     extra = list(extra)
 
     def product(left_ref, right_refs, target):
-        turned = jnp.transpose(left_ref[...])
         for i, right_ref in enumerate(right_refs):
-            target[:, pl.ds(i * each, each)] = matmul(turned, right_ref[...]).astype(LOW)
+            block = left_product(left_ref[...], right_ref[...])
+            target[:, pl.ds(i * each, each)] = block.astype(LOW)
 
     def kernel(table_ref, left_ref, *rest):
         right_refs, rest = rest[: len(rights)], rest[len(rights) :]
         if not direct:
             product(left_ref, right_refs, rest[0])
             return
-        more, (own, other, sums, sems) = rest[: len(extra)], rest[len(extra) :]
+        more, rest = rest[: len(extra)], rest[len(extra) :]
+        outs, (sums, sems) = rest[:4], rest[4:]
         step = pl.program_id(0)
 
         @pl.when(step == 0)
         def _():
             for ref, one in zip(more, extra):
-                slots.start(table_ref, [(ref, one[1], one[2], one[3])], (own, other), sems.at[2])
+                slots.start(table_ref, [(ref, one[1], one[2], one[3])], outs, sems.at[2])
 
         current = lax.rem(step, 2)
 
@@ -562,7 +566,7 @@
             arrived(sums.at[current], sems.at[current])
 
         product(left_ref, right_refs, sums.at[current])
-        slots.send(table_ref, sums.at[current], step * (tile // height), (own, other), sems.at[current])
+        slots.send(table_ref, sums.at[current], step * (tile // height), outs, sems.at[current])
 
         @pl.when(step == steps - 1)
         def _():
@@ -577,12 +581,12 @@
         in_specs=[SCALARS, pl.BlockSpec((cells, tile), lambda i: (0, i))]
         + [whole(cells, each)] * len(rights)
         + [whole(*one[0].shape) for one in (extra if direct else [])],
-        out_specs=[ANYWHERE] * 2 if direct else [pl.BlockSpec((tile, cols), lambda i: (i, 0))],
+        out_specs=[ANYWHERE] * 4 if direct else [pl.BlockSpec((tile, cols), lambda i: (i, 0))],
         out_shape=slots.shapes() if direct else [jax.ShapeDtypeStruct((rows, cols), LOW)],
         scratch_shapes=[pltpu.VMEM((2, tile, cols), LOW), pltpu.SemaphoreType.DMA((3,))]
         if direct
         else [],
-        compiler_params=params(),
+        compiler_params=params(28),
         cost_estimate=cost(2 * cells * rows * cols, 2 * rows * cols),
         name=name,
     )(table, left, *rights, *[one[0] for one in (extra if direct else [])])
@@ -615,26 +619,26 @@
         grid_spec=by_region(
             steps,
             [whole(cells, width), pl.BlockSpec((cells, tile), region_columns)]
-            + [ANYWHERE] * parts,
+            + [FAR_AWAY] * parts,
             pl.BlockSpec((cells, tile), region_columns),
             [pltpu.VMEM(down.shape, LOW), pltpu.SemaphoreType.DMA((steps,))],
         ),
         out_shape=jax.ShapeDtypeStruct((cells, cols), LOW),
-        compiler_params=params(),
+        compiler_params=params(24),
         cost_estimate=cost(2 * cells * width * cols, 22 << 20),
         name="up_back",
     )(table, grad_carried, slope, *down.operands)
 
 
-def middle_back_kernel(table, grad_up_proj, grad_carried, middle, turned, up, out_proj):
+def middle_back_kernel(table, grad_up_proj, grad_carried, middle, mixed, turned, up, out_proj):
     cells, width = grad_carried.shape
     cols = grad_up_proj.shape[1]
     parts, more = len(up.operands), len(out_proj.operands)
 
-    def kernel(table_ref, gu_ref, gc_ref, mid_ref, turned_ref, *rest):
+    def kernel(table_ref, gu_ref, gc_ref, mid_ref, mixed_ref, turned_ref, *rest):
         refs, rest = rest[:parts], rest[parts:]
         out_refs, rest = rest[:more], rest[more:]
-        gm_ref, gb_ref, gx_ref, gain_ref, gu_held, second, held, out_held, sems = rest
+        gm_ref, go_ref, gx_ref, gain_ref, gu_held, second, held, out_held, sems = rest
         loading = pltpu.make_async_copy(gu_ref, gu_held, sems.at[2])
         loading.start()
         up.start(table_ref, refs, held, sems)
@@ -650,17 +654,18 @@
         back = norm_back(normed, scale, grad_second, turned_ref[1:2])
         grad_middle = gc_ref[...].astype(FULL) + back
         gm_ref[...] = grad_middle
-        gb_ref[...] = grad_middle.astype(LOW)
+        branch = grad_middle.astype(LOW)
+        go_ref[...] = left_product(mixed_ref[...], branch).astype(LOW)
         arrived(out_held, sems.at[1])
-        gx_ref[...] = right_product(gb_ref[...], out_held[...]).astype(LOW)
+        gx_ref[...] = right_product(branch, out_held[...]).astype(LOW)
 
     return pl.pallas_call(
         kernel,
-        in_specs=[SCALARS, ANYWHERE] + [INSIDE] * 3 + [ANYWHERE] * (parts + more),
+        in_specs=[SCALARS, ANYWHERE] + [INSIDE] * 4 + [ANYWHERE] * (parts + more),
         out_specs=[INSIDE] * 4,
         out_shape=[
             jax.ShapeDtypeStruct((cells, width), FULL),
-            jax.ShapeDtypeStruct((cells, width), LOW),
+            jax.ShapeDtypeStruct((width, width), LOW),
             jax.ShapeDtypeStruct((cells, width), LOW),
             jax.ShapeDtypeStruct((1, width), FULL),
         ],
@@ -674,17 +679,18 @@
         compiler_params=params(),
         cost_estimate=cost(2 * cells * width * (cols + width), 22 << 20),
         name="middle_back",
-    )(table, grad_up_proj, grad_carried, middle, turned, *up.operands, *out_proj.operands)
-
-
-def input_back_kernel(table, grad_packed, grad_middle, inputs, turned, weight):
+    )(table, grad_up_proj, grad_carried, middle, mixed, turned, *up.operands, *out_proj.operands)
+
+
+def input_back_kernel(table, grad_packed, grad_middle, inputs, turned, small, columns, weight):
     cells, width = inputs.shape
     parts = len(weight.operands)
 
-    def kernel(table_ref, gq_ref, gk_ref, gv_ref, gm_ref, in_ref, turned_ref, *rest):
-        refs, (gx_ref, gain_ref, first, held, sems) = rest[:parts], rest[parts:]
+    def kernel(table_ref, gq_ref, gk_ref, gv_ref, gm_ref, in_ref, turned_ref, small_ref, *rest):
+        column_refs, rest = rest[: len(columns)], rest[len(columns) :]
+        refs, (gx_ref, small_out, first, held, sems) = rest[:parts], rest[parts:]
         weight.start(table_ref, refs, held, sems)
-        normed, scale = norm_parts(in_ref[...])
+        normed, scale = norm_parts(in_ref[...].astype(FULL))
         arrived(held, sems.at[0])
         for column in range(0, width, 512):
             some = pl.ds(column, 512)
@@ -693,26 +699,32 @@
                 for i, ref in enumerate((gq_ref, gk_ref, gv_ref))
             )
         grad_first = first[...]
-        gain_ref[...] = jnp.sum(normed * grad_first, axis=0, keepdims=True)
+        gain = jnp.sum(normed * grad_first, axis=0, keepdims=True)
+        lane = lax.broadcasted_iota(jnp.int32, (width, 128), 1)
+        block = small_ref[...]
+        for k, one in enumerate((gain, *[ref[...] for ref in column_refs])):
+            one = jnp.transpose(jnp.broadcast_to(one, (128, width)))
+            block = jnp.where(lane == k, one, block)
+        small_out[...] = block.astype(LOW)
         gx_ref[...] = gm_ref[...] + norm_back(normed, scale, grad_first, turned_ref[0:1])
 
     return pl.pallas_call(
         kernel,
-        in_specs=[SCALARS] + [INSIDE] * 6 + [ANYWHERE] * parts,
+        in_specs=[SCALARS] + [INSIDE] * (7 + len(columns)) + [FAR_AWAY] * parts,
         out_specs=[INSIDE] * 2,
         out_shape=[
             jax.ShapeDtypeStruct((cells, width), FULL),
-            jax.ShapeDtypeStruct((1, width), FULL),
+            jax.ShapeDtypeStruct((width, 128), LOW),
         ],
         scratch_shapes=[
             pltpu.VMEM((cells, width), FULL),
             pltpu.VMEM(weight.shape, LOW),
             pltpu.SemaphoreType.DMA((1,)),
         ],
-        compiler_params=params(),
+        compiler_params=params(26),
         cost_estimate=cost(6 * cells * width * width, 18 << 20),
         name="input_back",
-    )(table, *grad_packed, grad_middle, inputs, turned, *weight.operands)
+    )(table, *grad_packed, grad_middle, inputs, turned, small, *columns, *weight.operands)
 
 
 def small_block(columns, rest):
@@ -732,6 +744,15 @@
 
 def add_low(one, two):
     return (one.astype(FULL) + two.astype(FULL)).astype(LOW)
+
+
+def add_slots(size, *terms):
+    parts = [array[first : first + size] for array, first in terms]
+    return add_all(parts[0], parts[1:]).astype(LOW)
+
+
+def both_cores(slots, got, turn, far):
+    return add_slots(far, *[(pair[turn // 2], turn % 2 * far) for pair in (slots, got)])
 
 
 def add_all(first, others):
@@ -781,14 +802,15 @@
     return jnp.where((lane // size) == head, value, jnp.zeros_like(value))
 
 
-def attention_forward(packed, segments):
+def attention_forward(packed, seg_col, seg_row, first, last, earlier=()):
     cells, three = packed.shape
     width = three // 3
     size = width // HEADS
     pair = 128 // size
     steps = HEADS // pair
 
-    def kernel(seg_col, seg_row, q_ref, k_ref, v_ref, out_ref, attn_ref):
+    def kernel(seg_col, seg_row, q_ref, k_ref, v_ref, *rest):
+        out_ref, attn_ref = rest[-2:]
         same = seg_col[...] == seg_row[...]
         queries, keys = q_ref[...], k_ref[...]
         values = jnp.transpose(v_ref[...])
@@ -805,46 +827,50 @@
 
     return pl.pallas_call(
         kernel,
-        grid=(steps,),
+        grid=(last - first,),
         in_specs=[
             pl.BlockSpec((cells, 1), lambda i: (0, 0)),
             pl.BlockSpec((1, cells), lambda i: (0, 0)),
-            pl.BlockSpec((cells, 128), lambda i: (0, i)),
-            pl.BlockSpec((cells, 128), lambda i: (0, i + steps)),
-            pl.BlockSpec((cells, 128), lambda i: (0, i + 2 * steps)),
-        ],
+            pl.BlockSpec((cells, 128), lambda i: (0, i + first)),
+            pl.BlockSpec((cells, 128), lambda i: (0, i + first + steps)),
+            pl.BlockSpec((cells, 128), lambda i: (0, i + first + 2 * steps)),
+        ]
+        + [ANYWHERE] * len(earlier),
         out_specs=[
-            pl.BlockSpec((cells, 128), lambda i: (0, i)),
-            pl.BlockSpec((pair, cells, cells), lambda i: (i, 0, 0)),
+            pl.BlockSpec((cells, 128), lambda i: (0, i + first)),
+            pl.BlockSpec((pair, cells, cells), lambda i: (i + first, 0, 0)),
         ],
         out_shape=[
             jax.ShapeDtypeStruct((cells, width), LOW),
             jax.ShapeDtypeStruct((HEADS, cells, cells), LOW),
         ],
+        input_output_aliases={5 + i: i for i in range(len(earlier))},
         compiler_params=params(),
         cost_estimate=cost(4 * cells * cells * width, 24 << 20),
         name="attention_forward",
-    )(segments[:, None], segments[None, :], packed, packed, packed)
-
-
-def attention_backward(packed, attn, grad_mixed):
+    )(seg_col, seg_row, packed, packed, packed, *earlier)
+
+
+def attention_backward(packed, attn, mixed, grad_mixed):
     cells, three = packed.shape
     width = three // 3
     size = width // HEADS
     pair = 128 // size
     steps = HEADS // pair
 
-    def kernel(q_ref, k_ref, v_ref, g_ref, attn_ref, gq_ref, gk_ref, gv_ref):
+    def kernel(q_ref, k_ref, v_ref, g_ref, mixed_ref, attn_ref, gq_ref, gk_ref, gv_ref):
         queries, keys, values, grad = q_ref[...], k_ref[...], v_ref[...], g_ref[...]
         keys_t = jnp.transpose(keys)
+        inner = jnp.transpose(grad).astype(FULL) * jnp.transpose(mixed_ref[...]).astype(FULL)
         grad_q, grad_k, grad_v = [], 0.0, 0.0
         for head in range(pair):
             attn_low = attn_ref[head]
             attn = attn_low.astype(FULL)
             grad_attn = right_product(head_lanes(values, head, size), grad)
-            inner = jnp.sum(grad_attn * attn, axis=0, keepdims=True)
-            grad_scores = (attn * (grad_attn - inner)).astype(LOW)
-            grad_q.append(matmul(keys_t[head * size : (head + 1) * size], grad_scores))
+            some = slice(head * size, (head + 1) * size)
+            grad_scores = attn * (grad_attn - jnp.sum(inner[some], axis=0, keepdims=True))
+            grad_scores = grad_scores.astype(LOW)
+            grad_q.append(matmul(keys_t[some], grad_scores))
             grad_k += head_lanes(matmul(grad_scores, queries), head, size)
             grad_v += head_lanes(matmul(attn_low, grad), head, size)
         scale = size ** (-0.5)
@@ -860,6 +886,7 @@
             pl.BlockSpec((cells, 128), lambda i: (0, i + steps)),
             pl.BlockSpec((cells, 128), lambda i: (0, i + 2 * steps)),
             pl.BlockSpec((cells, 128), lambda i: (0, i)),
+            pl.BlockSpec((cells, 128), lambda i: (0, i)),
             pl.BlockSpec((pair, cells, cells), lambda i: (i, 0, 0)),
         ],
         out_specs=[pl.BlockSpec((cells, 128), lambda i: (0, i))] * 3,
@@ -867,7 +894,7 @@
         compiler_params=params(),
         cost_estimate=cost(10 * cells * cells * width, 24 << 20),
         name="attention_backward",
-    )(packed, packed, packed, grad_mixed, attn)
+    )(packed, packed, packed, grad_mixed, mixed, attn)
 
 
 def local(
@@ -929,37 +956,56 @@
     first_far = far_start(first_block)
     got = send_core(going)
     last_near = near_first(last_block)
-    got, last_near = hold(got, last_near)
-    inputs = jnp.where(core == 0, kept, got).astype(FULL)
+    got, last_near, up_block, *first_far = hold(got, last_near, up_block, *first_far)
+    inputs_low = jnp.where(core == 0, kept, got)
+    inputs = inputs_low.astype(FULL)
     cotangent = jnp.where(core == 0, got, kept)
     normed_one, scale_one = norm_parts(inputs)
     last_two = join(last_block, last_near)
-    last_more = near_second(last_two)
-    last_more, normed_one, up_block, *first_far = hold(
-        last_more, normed_one, up_block, *first_far
-    )
-    last_four = join(last_two, last_more)
 
     first_four = join(first_block, *first_far)
     first_m1, first_m2 = near_first(first_four), near_second(first_four)
     up_far = far_start(up_block)
-    first_m1, first_m2, *up_far = hold(first_m1, first_m2, *up_far)
+    seg_col, seg_row = segments[:, None], segments[None, :]
+    choose = mixture_rows[:, None] == jnp.arange(comps, dtype=jnp.int32)[None, :]
+    first_m1, first_m2, normed_one, last_two, table, seg_col, seg_row, *rest = hold(
+        first_m1,
+        first_m2,
+        normed_one,
+        last_two,
+        table,
+        seg_col,
+        seg_row,
+        choose.astype(LOW),
+        noise_rows,
+        down_block,
+        *up_far,
+    )
+    choose, noise_rows, down_block, *up_far = rest
 
     first_m3 = near_second(first_m1)
     first_c0, first_c1, first_c2 = [send_core(one) for one in (first_four, first_m1, first_m2)]
-    first_m3, first_c0, first_c1, first_c2, down_block, *up_far = hold(
-        first_m3, first_c0, first_c1, first_c2, down_block, *up_far
-    )
+    down_far = [far_exchange(down_block, 1)]
+    first_m3, first_c0, first_c1, first_c2, down_block, *rest = hold(
+        first_m3, first_c0, first_c1, first_c2, down_block, *down_far, *up_far
+    )
+    down_far, up_far = rest[:1], rest[1:]
 
     up_four = join(up_block, *up_far)
     first_c3, up_four, down_block = hold(send_core(first_m3), up_four, down_block)
     up_m1, up_m2 = near_first(up_four), near_second(up_four)
-    down_far = far_start(down_block)
+    last_more = near_second(last_two)
+    down_far += [far_exchange(down_block, mask) for mask in far_masks() if mask > 1]
     first_parts = [first_four, first_m1, first_m2, first_m3], [first_c0, first_c1, first_c2, first_c3]
     qkv, out_proj, small_rows = [Rows(*first_parts, piece) for piece in first_pieces]
     first_in, packed, small_all, turned = first_kernel(table, normed_one, qkv, small_rows)
-    mixed, attn = attention_forward(packed, segments)
-    up_m1, up_m2, mixed, last_four, *down_far = hold(up_m1, up_m2, mixed, last_four, *down_far)
+    pairs = HEADS * (width // HEADS) // 128
+    some_heads = attention_forward(packed, seg_col, seg_row, 0, pairs // 2)
+    up_m1, up_m2, last_more, packed, *rest = hold(
+        up_m1, up_m2, last_more, packed, *some_heads, *down_far
+    )
+    some_heads, down_far = rest[:2], rest[2:]
+    last_four = join(last_two, last_more)
 
     up_m3 = near_second(up_m1)
     down_four = join(down_block, *down_far)
@@ -967,16 +1013,14 @@
     up_c0 = send_core(up_four)
     last_early, last_late = [1, 2], list(far_masks())[2:]
     last_far = {mask: far_exchange(last_four, mask) for mask in last_early}
+    mixed, attn = attention_forward(packed, seg_col, seg_row, pairs // 2, pairs, some_heads)
     middle, second_in = branch_kernel(table, mixed, inputs, turned, out_proj)
     small_all = small_all.reshape(devices, rows, 128)[:, :, 16 : 16 + lanes]
     small_all = small_all.reshape(devices, 2, comps, comp_cols).transpose(1, 2, 0, 3)
-    means, spreads = small_all.reshape(2, comps, latent)
-    choose = mixture_rows[:, None] == jnp.arange(comps, dtype=jnp.int32)[None, :]
-    centre = matmul(choose.astype(LOW), means)
-    spread = matmul(choose.astype(LOW), spreads)
+    comp_tables = small_all.reshape(2, comps, latent)
     early = [last_far[mask] for mask in last_early]
-    up_m3, down_m1, up_c0, second_in, centre, spread, up_m1, up_m2, last_four, *early = hold(
-        up_m3, down_m1, up_c0, second_in, centre, spread, up_m1, up_m2, last_four, *early
+    up_m3, down_m1, up_c0, second_in, comp_tables, up_m1, up_m2, last_four, *early = hold(
+        up_m3, down_m1, up_c0, second_in, comp_tables, up_m1, up_m2, last_four, *early
     )
     last_far.update(zip(last_early, early))
 
@@ -1004,7 +1048,7 @@
         [down_four, down_m1, down_m2, down_m3], [down_c0, down_c1, down_c2, down_c3], down_pieces[0]
     )
     carried, moments, sample, kl_part = latent_kernel(
-        table, hidden, middle, noise_rows, centre, spread, down, to_latent
+        table, hidden, middle, noise_rows, choose, comp_tables, down, to_latent
     )
     kl_sum = kl_part + send_core(kl_part)
     kl_sum, sample = hold(kl_sum, sample)
@@ -1015,18 +1059,15 @@
     kl_sum = sum(kl_near, kl_sum)
     kl_sum, grad_sample, decoded = hold(kl_sum, grad_sample, decoded)
     kl_far = [far_exchange(kl_sum, mask) for mask in far_masks()]
-    plain, factor, comp = factors_kernel(
-        grad_sample, moments, noise_rows, centre, spread, choose.astype(LOW)
-    )
+    plain, factor, comp = factors_kernel(grad_sample, moments, noise_rows, choose, comp_tables)
     kl_sum = sum(kl_far, kl_sum)
     kl_sum, grad_decode, plain, factor, grad_bias, decoded = hold(
         kl_sum, grad_decode, plain, factor, grad_bias, decoded
     )
-    decoded_there = send_core(decoded)
 
     far = lax.axis_size("dp") // 4
     kl_weight = jnp.minimum(1.0, (plan_step + 1).astype(FULL) / WARM)
-    grad_carried, comp, last_own, last_other = moments_kernel(
+    grad_carried, comp, *last_slots = moments_kernel(
         table,
         kl_weight,
         total_cells,
@@ -1039,61 +1080,64 @@
         to_latent,
         Slots(rows + decode_rows, width),
     )
-    last_own, last_other, grad_carried, hidden = hold(last_own, last_other, grad_carried, hidden)
-    last_got = send_core(last_other)
-    down_own, down_other = weight_grad(
+    grad_carried, hidden, decoded, *last_slots = hold(grad_carried, hidden, decoded, *last_slots)
+    decoded_there = send_core(decoded)
+    last_got = [send_core(one) for one in last_slots[2:]]
+    down_slots = weight_grad(
         table, hidden, [grad_carried], Slots(down_rows, width), down_rows, "grad_down"
     )
-    last_got, down_own, down_other, grad_carried = hold(
-        last_got, down_own, down_other, grad_carried
-    )
-
-    down_got = send_core(down_other)
-    turns = [slice(turn * far, (turn + 1) * far) for turn in range(4)]
-    last_m3, last_m2 = [near_second(add_low(last_own[t], last_got[t])) for t in (turns[3], turns[2])]
+    grad_carried, decoded_there, *rest = hold(
+        grad_carried, decoded_there, *last_got, *down_slots
+    )
+    last_got, down_slots = rest[:2], rest[2:]
+
+    down_got = [send_core(one) for one in down_slots[2:]]
+    last_3, last_2 = [both_cores(last_slots, last_got, turn, far) for turn in (3, 2)]
+    last_m3, last_m2 = near_second(last_3), near_second(last_2)
     grad_up_proj = up_back_kernel(table, grad_carried, slope, down)
-    down_got, grad_up_proj, last_m3, last_m2 = hold(down_got, grad_up_proj, last_m3, last_m2)
-
-    down_m3, down_m2 = [near_second(add_low(down_own[t], down_got[t])) for t in (turns[3], turns[2])]
-    last_m1 = near_first(add_all(last_own[turns[1]], [last_got[turns[1]], last_m3]).astype(LOW))
-    grad_middle, grad_branch, grad_mixed, grad_gain_two = middle_back_kernel(
-        table, grad_up_proj, grad_carried, middle, turned, up, out_proj
-    )
-    up_own, up_other = weight_grad(
+    grad_up_proj, last_m3, last_m2, *down_got = hold(grad_up_proj, last_m3, last_m2, *down_got)
+    down_m3 = near_second(both_cores(down_slots, down_got, 3, far))
+    up_slots = weight_grad(
         table, second_in, [grad_up_proj], Slots(rows, up_cols), rows, "grad_up"
     )
-    down_m3, down_m2, last_m1, up_own, up_other, grad_mixed = hold(
-        down_m3, down_m2, last_m1, up_own, up_other, grad_mixed
-    )
-
-    up_got = send_core(up_other)
-    down_m1 = near_first(add_all(down_own[turns[1]], [down_got[turns[1]], down_m3]).astype(LOW))
-    last_low = add_all(last_own[turns[0]], [last_got[turns[0]], last_m2, last_m1]).astype(LOW)
-    last_far = far_slots(last_low, 1)
-    grad_out = left_product(mixed, grad_branch).astype(LOW)
-    grad_packed = attention_backward(packed, attn, grad_mixed)
-    up_got, down_m1, grad_out, *grad_packed = hold(
-        up_got, down_m1, grad_out, *grad_packed, *last_far
-    )
-    grad_packed, last_far = grad_packed[:3], grad_packed[3:]
-
-    up_m3, up_m2 = [near_second(add_low(up_own[t], up_got[t])) for t in (turns[3], turns[2])]
-    down_low = add_all(down_own[turns[0]], [down_got[turns[0]], down_m2, down_m1]).astype(LOW)
-    down_far = far_slots(down_low, 1)
-    grad_inputs, grad_gain_one = input_back_kernel(
-        table, grad_packed, grad_middle, inputs, turned, qkv
-    )
-    up_m3, up_m2, grad_inputs, grad_gain_one, grad_packed_q, *down_far = hold(
-        up_m3, up_m2, grad_inputs, grad_gain_one, grad_packed[0], *down_far
-    )
-    grad_packed = [grad_packed_q, *grad_packed[1:]]
-
-    up_m1 = near_first(add_all(up_own[turns[1]], [up_got[turns[1]], up_m3]).astype(LOW))
+    down_0, down_1, down_2 = [both_cores(down_slots, down_got, turn, far) for turn in range(3)]
+    down_m3, last_m3, down_0, down_1, down_2, *up_slots = hold(
+        down_m3, last_m3, down_0, down_1, down_2, *up_slots
+    )
+
+    up_got = [send_core(one) for one in up_slots[2:]]
+    down_m2 = near_second(down_2)
+    last_m1 = near_first(add_slots(far, (last_slots[0], far), (last_got[0], far), (last_m3, 0)))
+    grad_middle, grad_out, grad_mixed, grad_gain_two = middle_back_kernel(
+        table, grad_up_proj, grad_carried, middle, mixed, turned, up, out_proj
+    )
     tables_grad = comp.reshape(2, comps, devices, comp_cols)
     tables_grad = tables_grad.transpose(2, 0, 1, 3).reshape(devices * rows, lanes)
-    columns = [one.reshape(width, 1) for one in (grad_gain_one, grad_gain_two, grad_bias)]
-    small_grads = small_block(columns, tables_grad).astype(LOW)
-    first_own, first_other = weight_grad(
+    small_grads = jnp.pad(tables_grad, ((0, 0), (16, 112 - lanes)))
+    down_m2, last_m1, grad_mixed, grad_out, small_grads, *up_got = hold(
+        down_m2, last_m1, grad_mixed, grad_out, small_grads, *up_got
+    )
+
+    up_m3 = near_second(both_cores(up_slots, up_got, 3, far))
+    down_m1 = near_first(add_slots(far, (down_1, 0), (down_m3, 0)))
+    grad_packed = attention_backward(packed, attn, mixed, grad_mixed)
+    up_m3, down_m1, *grad_packed = hold(up_m3, down_m1, *grad_packed)
+
+    up_m2 = near_second(both_cores(up_slots, up_got, 2, far))
+    up_m1 = near_first(add_slots(far, (up_slots[0], far), (up_got[0], far), (up_m3, 0)))
+    down_low = add_slots(far, (down_0, 0), (down_m2, 0), (down_m1, 0))
+    down_far = far_slots(down_low, 1)
+    grad_inputs, small_grads = input_back_kernel(
+        table,
+        grad_packed,
+        grad_middle,
+        inputs_low,
+        turned,
+        small_grads,
+        [grad_gain_two, grad_bias],
+        qkv,
+    )
+    first_slots = weight_grad(
         table,
         first_in,
         grad_packed,
@@ -1102,35 +1146,40 @@
         "grad_qkv",
         [(grad_out, rows, 0, qkv_cols), (small_grads, rows, 0, qkv_cols + out_cols)],
     )
-    up_m1, first_own, first_other = hold(up_m1, first_own, first_other)
-
-    first_got = send_core(first_other)
-    up_low = add_all(up_own[turns[0]], [up_got[turns[0]], up_m2, up_m1]).astype(LOW)
-    first_got, up_low, grad_inputs = hold(first_got, up_low, grad_inputs)
-
-    first_m3, first_m2 = [
-        near_second(add_low(first_own[t], first_got[t])) for t in (turns[3], turns[2])
-    ]
+    up_m2, up_m1, grad_inputs, *rest = hold(up_m2, up_m1, grad_inputs, *first_slots, *down_far)
+    first_slots, down_far = rest[:4], rest[4:]
+
+    first_high = send_core(first_slots[3])
+    up_low = add_slots(far, (up_slots[0], 0), (up_got[0], 0), (up_m2, 0), (up_m1, 0))
+    first_high, up_low, *first_slots = hold(first_high, up_low, *first_slots)
+    first_low = send_core(first_slots[2])
+    first_got = [first_low, first_high]
+    first_3, first_2 = [both_cores(first_slots, first_got, turn, far) for turn in (3, 2)]
+    first_low, first_3, first_2, up_low = hold(first_low, first_3, first_2, up_low)
+
+    first_m3, first_m2 = near_second(first_3), near_second(first_2)
     up_far = far_slots(up_low, 1)
+    last_low = add_slots(far, (last_slots[0], 0), (last_got[0], 0), (last_m2, 0), (last_m1, 0))
     down_sum = add_all(down_low[0], [one[0] for one in down_far])
+    first_m3, first_m2, down_sum, last_low, *up_far = hold(
+        first_m3, first_m2, down_sum, last_low, *up_far
+    )
+
+    first_m1 = near_first(add_slots(far, (first_slots[0], far), (first_low, far), (first_m3, 0)))
+    inputs_there = send_core(grad_inputs)
+    up_sum = add_all(up_low[0], [one[0] for one in up_far])
+    last_far = far_slots(last_low, 1)
+    first_m1, inputs_there, up_sum, *last_far = hold(first_m1, inputs_there, up_sum, *last_far)
     last_sum = add_all(last_low[0], [one[0] for one in last_far])
-    first_m3, first_m2, down_sum, last_sum, *up_far = hold(
-        first_m3, first_m2, down_sum, last_sum, *up_far
-    )
-
-    first_m1 = near_first(add_all(first_own[turns[1]], [first_got[turns[1]], first_m3]).astype(LOW))
-    inputs_there = send_core(grad_inputs)
+
     result = jnp.where(
         core == 0,
         jnp.concatenate([grad_inputs, inputs_there], axis=0),
         jnp.concatenate([decoded_there, decoded], axis=0).astype(FULL),
     )[None]
-    up_sum = add_all(up_low[0], [one[0] for one in up_far])
-    first_m1, result, up_sum = hold(first_m1, result, up_sum)
-
-    first_low = add_all(first_own[turns[0]], [first_got[turns[0]], first_m2, first_m1]).astype(LOW)
-    first_far = far_slots(first_low, 1)
-    first_sum = add_all(first_low[0], [one[0] for one in first_far])
+    first_all = add_slots(far, (first_slots[0], 0), (first_low, 0), (first_m2, 0), (first_m1, 0))
+    first_far = far_slots(first_all, 1)
+    first_sum = add_all(first_all[0], [one[0] for one in first_far])
     small_sum = first_sum[:, qkv_cols + out_cols :]
     comp_mean_sum, comp_logvar_sum = small_sum[:, 16 : 16 + lanes].reshape(2, comps, comp_cols)
     return (

time: 457 us -> 414 us (0.906)
  Pallas kernels: 157 us -> 142 us
  other arithmetic: 44 us -> 36 us
  matrix products: 6.83 us -> 0 us
  local copies, waits for them, and re-layouts: 34.1 us -> 27.9 us
    dot_general x3 -> x0, matrix products: 6.83 us -> none  [the longest x2 4.15 us: matmul(): return jnp.dot(left_side, right_side, preferred_element_type=FULL)]
    ppermute x74 -> x78, starting transfers between devices: 67.5 us -> 63 us  [send(): return lax.ppermute(value, EVERY, pairs)]
    convert_element_type x14 -> x15, other arithmetic: 30.2 us -> 25.8 us  [the longest x13 22.1 us: add_slots(): return add_all(parts[0], parts[1:]).astype(LOW)]
    unnamed x106 -> x181, local copies, waits for them, and re-layouts: 10.8 us -> 14.4 us
    ppermute x74 -> x78, waiting for transfers between devices: 140 us -> 137 us  [send(): return lax.ppermute(value, EVERY, pairs)]
    pallas_call x6 -> x7, Pallas kernels: 57.2 us -> 55.4 us  [the longest x1 15.9 us: middle_back_kernel(): pl.pallas_call(kernel, in_specs=[SCALARS, ANYWHERE] + [INSIDE] * 4 + [ANY...]
  transfers between devices with their start and end apart: 74 -> 78, of which waited for: 27 -> 37; matrix products, arithmetic and copies ran while one was open for 13% -> 11% of each run, Pallas kernels for 30% -> 29%
where the time goes in v3:
time: 414 us; the launch traced here: 409 us
  Pallas kernels  142 us (34%)
  waiting for transfers between devices  137 us (33%)
  starting transfers between devices  63 us (15%)
  other arithmetic  36 us (9%)
  local copies, waits for them, and re-layouts  27.9 us (7%)
    ppermute x78, waiting for transfers between devices, send(): return lax.ppermute(value, EVERY, pairs)  137 us
    ppermute x78, starting transfers between devices, send(): return lax.ppermute(value, EVERY, pairs)  63 us
    pallas_call x3, Pallas kernels, weight_grad(): pl.pallas_call(kernel, grid=(steps,), in_specs=[SCALARS, pl.BlockSpec((ce...  25.4 us
    convert_element_type x13, other arithmetic, add_slots(): return add_all(parts[0], parts[1:]).astype(LOW)  22.1 us
    pallas_call x1, Pallas kernels, middle_back_kernel(): pl.pallas_call(kernel, in_specs=[SCALARS, ANYWHERE] + [INSIDE] * 4 + [ANY...  15.9 us
    pallas_call x2, Pallas kernels, attention_forward(): pl.pallas_call(kernel, grid=(last - first,), in_specs=[pl.BlockSpec((cell...  15.8 us
    pallas_call x1, Pallas kernels, attention_backward(): pl.pallas_call(kernel, grid=(steps,), in_specs=[pl.BlockSpec((cells, 128)...  14.5 us
    unnamed x181, local copies, waits for them, and re-layouts  14.4 us
  transfers between devices with their start and end apart: 78, of which 37 were waited for; matrix products, arithmetic and copies ran while one was open for 11% of the time, Pallas kernels for 29%

profile of v3, /device:TPU:8, one launch (start us, length us, event | category | flops | bytes accessed | tf_op | source)
XLA Modules:
  0.0 409.2 jit_solution(16591129904934469560)
XLA Ops:
  15.8 9.4 %collective-permute-done.3 = bf16[1,32,4224]{2,1,0:T(8,128)(2,1)S(1)} collective-permute-done((bf16[1,32,4224]{2,1,0:T(8,128)(2,1)S(1)}, bf16[1,32,4224]{2,1,0:T(8,128)(2,1)S(1)}, u32[]{:S(2)}, u32[]{:S(2)}) %collective-permute-start.3) | collective-permute-done | bytes 270368 | tf_op jit(solution)/shard_map/ppermute | solution.py:31
  25.3 6.0 %collective-permute-done.4 = bf16[1,32,4224]{2,1,0:T(8,128)(2,1)S(1)} collective-permute-done((bf16[1,32,4224]{2,1,0:T(8,128)(2,1)S(1)}, bf16[1,32,4224]{2,1,0:T(8,128)(2,1)S(1)}, u32[]{:S(2)}, u32[]{:S(2)}) %collective-permute-start.4) | collective-permute-done | bytes 270368 | tf_op jit(solution)/shard_map/ppermute | solution.py:31
  45.6 9.8 %collective-permute-done.8 = bf16[1,32,4096]{2,1,0:T(8,128)(2,1)S(1)} collective-permute-done((bf16[1,32,4096]{2,1,0:T(8,128)(2,1)S(1)}, bf16[1,32,4096]{2,1,0:T(8,128)(2,1)S(1)}, u32[]{:S(2)}, u32[]{:S(2)}) %collective-permute-start.8) | collective-permute-done | bytes 262176 | tf_op jit(solution)/shard_map/ppermute | solution.py:31
  60.8 8.4 %collective-permute-done.14 = bf16[1,128,1024]{2,1,0:T(8,128)(2,1)S(1)} collective-permute-done((bf16[1,128,1024]{2,1,0:T(8,128)(2,1)}, bf16[1,128,1024]{2,1,0:T(8,128)(2,1)S(1)}, u32[]{:S(2)}, u32[]{:S(2)}) %collective-permute-start.14) | collective-permute-done | bytes 262176 | tf_op jit(solution)/shard_map/ppermute | solution.py:31
  69.2 5.7 %collective-permute-done.10.rest_3_.rest_11_.rest_5_ = bf16[4,32,4224]{2,1,0:T(8,128)(2,1)S(1)} collective-permute-done((bf16[4,32,4224]{2,1,0:T(8,128)(2,1)S(1)}, bf16[4,32,4224]{2,1,0:T(8,128)(2,1)S(1)}, u32[]{:S(2)}, u32[]{:S(2)}) %collective-permute-start.10) | collective-permute-done | bytes 1081376 | tf_op jit(solution)/shard_map/ppermute | solution.py:31
  84.7 10.1 %first.1 = (bf16[512,1024]{1,0:T(8,128)(2,1)}, bf16[512,3072]{1,0:T(8,128)(2,1)}, bf16[1024,128]{1,0:T(8,128)(2,1)}, f32[128,1024]{1,0:T(8,128)}) custom-call(s32[96]{0:T(128)} %concatenate.64.table_ref, f32[512,1024]{1,0:T(8,128)} %subtract_multiply_fusion.normed_ref, bf16[4,32,4224]{2,1,0:T(8,128)(2,1)} %copy-done.2, bf16[4,32,4224]{2,1,0:T(8,128)(2,1)} %copy-done.5, ...), custom_call_target="tpu_custom_call" | custom-call | flops 1024 | bytes 1024 | tf_op jit(solution)/shard_map/first/pallas_call | solution.py:233
  94.8 8.0 %attention_forward.2 = (bf16[512,1024]{1,0:T(8,128)(2,1)}, bf16[16,512,512]{2,1,0:T(8,128)(2,1)}) custom-call(s32[512,1]{1,0:T(8,128)} %copy.38.seg_col, s32[1,512]{1,0:T(1,128)} %constant_dynamic-slice_fusion.1.seg_row, bf16[512,3072]{1,0:T(8,128)(2,1)} %get-tuple-element.247.q_ref.k_ref.v_ref, bf16[512,3072]{1,0:T(8,128)(2,1)} %get-tuple-element.247.q_ref.k_ref.v_ref, ...), custom_call_target="tpu_custom_call" | custom-call | flops 1024 | bytes 1024 | tf_op jit(solution)/shard_map/attention_forward/pallas_call | solution.py:828
  116.6 7.9 %attention_forward.3 = (bf16[512,1024]{1,0:T(8,128)(2,1)}, bf16[16,512,512]{2,1,0:T(8,128)(2,1)}) custom-call(s32[512,1]{1,0:T(8,128)} %copy.38.seg_col, s32[1,512]{1,0:T(1,128)} %constant_dynamic-slice_fusion.1.seg_row, bf16[512,3072]{1,0:T(8,128)(2,1)} %get-tuple-element.247.q_ref.k_ref.v_ref, ...), custom_call_target="tpu_custom_call", output_to_operand_aliasing={{0}: (5, {}), {1}: (6, {})} | custom-call | flops 1024 | bytes 1024 | tf_op jit(solution)/shard_map/attention_forward/pallas_call | solution.py:828
  124.4 5.9 %branch.1 = (f32[512,1024]{1,0:T(8,128)}, bf16[512,1024]{1,0:T(8,128)(2,1)}) custom-call(s32[96]{0:T(128)} %concatenate.64.table_ref, bf16[512,1024]{1,0:T(8,128)(2,1)} %get-tuple-element.250.mixed_ref, f32[512,1024]{1,0:T(8,128)} %get-tuple-element.413.in_ref, f32[128,1024]{1,0:T(8,128)} %get-tuple-element.251.turned_ref, bf16[4,32,4224]{2,1,0:T(8,128)(2,1)} %copy-done.2, ...), custom_call_target="tpu_custom_call" | custom-call | flops 1024 | bytes 1024 | tf_op jit(solution)/shard_map/branch/pallas_call | solution.py:274
  144.8 11.2 %up.1 = (bf16[512,4096]{1,0:T(8,128)(2,1)S(1)}, bf16[512,4096]{1,0:T(8,128)(2,1)S(1)}) custom-call(s32[96]{0:T(128)S(1)} %copy-done.60, bf16[512,1024]{1,0:T(8,128)(2,1)S(1)} %copy-done.44, bf16[4,32,4096]{2,1,0:T(8,128)(2,1)} %pad_maximum_fusion.1.rest_0_, bf16[4,32,4096]{2,1,0:T(8,128)(2,1)} %collective-permute-done.16.rest_1_, ...), custom_call_target="tpu_custom_call" | custom-call | flops 1024 | bytes 1024 | tf_op jit(solution)/shard_map/up/pallas_call | solution.py:317
  168.8 11.8 %latent.1 = (bf16[512,1024]{1,0:T(8,128)(2,1)S(1)}, f32[512,1024]{1,0:T(8,128)S(1)}, bf16[512,512]{1,0:T(8,128)(2,1)S(1)}, f32[1,512]{1,0:T(1,128)S(1)}) custom-call(s32[96]{0:T(128)S(1)} %copy-done.60, bf16[512,4096]{1,0:T(8,128)(2,1)S(1)} %get-tuple-element.315.hidden_ref.left_ref, f32[512,1024]{1,0:T(8,128)S(1)} %copy-done.25, f32[512,512]{1,0:T(8,128)S(1)} %copy-done.21, ...), custom_call_target="tpu_custom_call" | custom-call | flops 1024 | bytes 1024 | tf_op jit(solution)/shard_map/latent/pallas_call | solution.py:368
  196.5 10.4 %moments.1 = (bf16[512,1024]{1,0:T(8,128)(2,1)S(1)}, f32[2,16,512]{2,1,0:T(8,128)S(1)}, bf16[8,48,1024]{2,1,0:T(8,128)(2,1)S(1)}, bf16[8,48,1024]{2,1,0:T(8,128)...) custom-call(s32[96]{0:T(128)S(1)} %copy-done.60, f32[1]{0:T(128)S(6)} %min.3.weight_ref, ...), custom_call_target="tpu_custom_call" | custom-call | flops 1024 | bytes 1024 | tf_op jit(solution)/shard_map/moments/pallas_call | solution.py:509
  207.6 8.3 %grad_down.1 = (bf16[8,128,1024]{2,1,0:T(8,128)(2,1)S(1)}, bf16[8,128,1024]{2,1,0:T(8,128)(2,1)S(1)}, bf16[8,128,1024]{2,1,0:T(8,128)(2,1)S(1)}, bf16[8,128,1024]{2,1,0:T(8,128)(2,1)S(1)}) custom-call(s32[96]{0:T(128)S(1)} %copy-done.60, bf16[512,4096]{1,0:T(8,128)(2,1)S(1)} %get-tuple-element.315.hidden_ref.left_ref, ...), custom_call_target="tpu_custom_call" | custom-call | flops 1024 | bytes 1024 | tf_op jit(solution)/shard_map/grad_down/pallas_call | solution.py:578
  219.0 7.5 %up_back.1.rest_0_.gu_ref = bf16[512,4096]{1,0:T(8,128)(2,1)S(1)} custom-call(s32[96]{0:T(128)S(1)} %copy-done.60, bf16[512,1024]{1,0:T(8,128)(2,1)S(1)} %get-tuple-element.321.rest_0_.grad_ref.gc_ref, bf16[512,4096]{1,0:T(8,128)(2,1)S(1)} %copy-done.27, bf16[4,128,1024]{2,1,0:T(8,128)(2,1)S(1)} %constant_dynamic-update-slice_fusion.rest_0_, ...), custom_call_target="tpu_custom_call" | custom-call | flops 1024 | bytes 1024 | tf_op jit(solution)/shard_map/up_back/pallas_call | solution.py:617
  231.7 7.9 %grad_up.1 = (bf16[8,32,4096]{2,1,0:T(8,128)(2,1)S(1)}, bf16[8,32,4096]{2,1,0:T(8,128)(2,1)S(1)}, bf16[8,32,4096]{2,1,0:T(8,128)(2,1)}, bf16[8,32,4096]{2,1,0:T(8,128)(2,1)}) custom-call(s32[96]{0:T(128)S(1)} %copy-done.60, bf16[512,1024]{1,0:T(8,128)(2,1)S(1)} %copy-done.45, bf16[512,4096]{1,0:T(8,128)(2,1)S(1)} %up_back.1.rest_0_.gu_ref), custom_call_target="tpu_custom_call" | custom-call | flops 1024 | bytes 1024 | tf_op jit(solution)/shard_map/grad_up/pallas_call | solution.py:578
  249.2 15.9 %middle_back.1 = (f32[512,1024]{1,0:T(8,128)}, bf16[1024,1024]{1,0:T(8,128)(2,1)}, bf16[512,1024]{1,0:T(8,128)(2,1)}, f32[1,1024]{1,0:T(1,128)}) custom-call(s32[96]{0:T(128)} %concatenate.64.table_ref, bf16[512,4096]{1,0:T(8,128)(2,1)} %copy-done.4, bf16[512,1024]{1,0:T(8,128)(2,1)} %copy-done.22, f32[512,1024]{1,0:T(8,128)} %get-tuple-element.271.mid_ref, ...), custom_call_target="tpu_custom_call" | custom-call | flops 1024 | bytes 1024 | tf_op jit(solution)/shard_map/middle_back/pallas_call | solution.py:662
  275.2 14.5 %attention_backward.1 = (bf16[512,1024]{1,0:T(8,128)(2,1)}, bf16[512,1024]{1,0:T(8,128)(2,1)}, bf16[512,1024]{1,0:T(8,128)(2,1)}) custom-call(bf16[512,3072]{1,0:T(8,128)(2,1)} %get-tuple-element.247.q_ref.k_ref.v_ref, bf16[512,3072]{1,0:T(8,128)(2,1)} %get-tuple-element.247.q_ref.k_ref.v_ref, bf16[512,3072]{1,0:T(8,128)(2,1)} %get-tuple-element.247.q_ref.k_ref.v_ref, ...), custom_call_target="tpu_custom_call" | custom-call | flops 1024 | bytes 1024 | tf_op jit(solution)/shard_map/attention_backward/pallas_call | solution.py:881
  307.3 7.5 %input_back.1 = (f32[512,1024]{1,0:T(8,128)S(1)}, bf16[1024,128]{1,0:T(8,128)(2,1)S(1)}) custom-call(s32[96]{0:T(128)S(1)} %copy-done.61, bf16[512,1024]{1,0:T(8,128)(2,1)S(1)} %copy-done.46, bf16[512,1024]{1,0:T(8,128)(2,1)S(1)} %copy-done.48, bf16[512,1024]{1,0:T(8,128)(2,1)S(1)} %copy-done.50, f32[512,1024]{1,0:T(8,128)S(1)} %copy-done.53, ...), custom_call_target="tpu_custom_call" | custom-call | flops 1024 | bytes 1024 | tf_op jit(solution)/shard_map/input_back/pallas_call | solution.py:711
  314.9 9.2 %grad_qkv.1 = (bf16[8,32,4224]{2,1,0:T(8,128)(2,1)S(1)}, bf16[8,32,4224]{2,1,0:T(8,128)(2,1)S(1)}, bf16[8,32,4224]{2,1,0:T(8,128)(2,1)S(1)}, bf16[8,32,4224]{2,1,0:T(8,128)(2,1)S(1)}) custom-call(s32[96]{0:T(128)S(1)} %copy-done.61, bf16[512,1024]{1,0:T(8,128)(2,1)S(1)} %copy-done.57, bf16[512,1024]{1,0:T(8,128)(2,1)S(1)} %copy-done.47, ...), custom_call_target="tpu_custom_call" | custom-call | flops 1024 | bytes 1024 | tf_op jit(solution)/shard_map/grad_qkv/pallas_call | solution.py:578
  342.7 5.3 %collective-permute-done.67 = bf16[1,32,4096]{2,1,0:T(8,128)(2,1)S(1)} collective-permute-done((bf16[1,32,4096]{2,1,0:T(8,128)(2,1)S(1)}, bf16[1,32,4096]{2,1,0:T(8,128)(2,1)S(1)}, u32[]{:S(2)}, u32[]{:S(2)}) %collective-permute-start.67) | collective-permute-done | bytes 262176 | tf_op jit(solution)/shard_map/ppermute | solution.py:31
  348.0 10.2 %collective-permute-done.68 = bf16[1,32,4096]{2,1,0:T(8,128)(2,1)S(1)} collective-permute-done((bf16[1,32,4096]{2,1,0:T(8,128)(2,1)S(1)}, bf16[1,32,4096]{2,1,0:T(8,128)(2,1)S(1)}, u32[]{:S(2)}, u32[]{:S(2)}) %collective-permute-start.68) | collective-permute-done | bytes 262176 | tf_op jit(solution)/shard_map/ppermute | solution.py:31
  358.1 6.0 %collective-permute-done.69 = bf16[1,32,4096]{2,1,0:T(8,128)(2,1)S(1)} collective-permute-done((bf16[1,32,4096]{2,1,0:T(8,128)(2,1)S(1)}, bf16[1,32,4096]{2,1,0:T(8,128)(2,1)S(1)}, u32[]{:S(2)}, u32[]{:S(2)}) %collective-permute-start.69) | collective-permute-done | bytes 262176 | tf_op jit(solution)/shard_map/ppermute | solution.py:31
  390.6 10.2 %collective-permute-done.76 = bf16[1,32,4224]{2,1,0:T(8,128)(2,1)S(1)} collective-permute-done((bf16[1,32,4224]{2,1,0:T(8,128)(2,1)S(1)}, bf16[1,32,4224]{2,1,0:T(8,128)(2,1)S(1)}, u32[]{:S(2)}, u32[]{:S(2)}) %collective-permute-start.76) | collective-permute-done | bytes 270368 | tf_op jit(solution)/shard_map/ppermute | solution.py:31
  400.8 4.9 %collective-permute-done.77 = bf16[1,32,4224]{2,1,0:T(8,128)(2,1)S(1)} collective-permute-done((bf16[1,32,4224]{2,1,0:T(8,128)(2,1)S(1)}, bf16[1,32,4224]{2,1,0:T(8,128)(2,1)S(1)}, u32[]{:S(2)}, u32[]{:S(2)}) %collective-permute-start.77) | collective-permute-done | bytes 270368 | tf_op jit(solution)/shard_map/ppermute | solution.py:31
  (397 shorter events, 194.1 us)
Async XLA Ops:
  3.2 28.0 %collective-permute-start = (bf16[512,1024]{1,0:T(8,128)(2,1)}, bf16[512,1024]{1,0:T(8,128)(2,1)}, u32[]{:S(2)}, u32[]{:S(2)}) collective-permute-start(bf16[512,1024]{1,0:T(8,128)(2,1)} %dynamic-slice_bitcast_fusion), channel_id=1, source_target_pairs={{0,1},{1,0},{2,3},{3,2},{4,5},{5,4},{6,7},{7,6},{8,9},{9,8},{10,11... | collective-permute-start | bytes 3145736 | tf_op jit(solution)/shard_map/ppermute | solution.py:31
  6.8 24.5 %collective-permute-start.4 = (bf16[1,32,4224]{2,1,0:T(8,128)(2,1)S(1)}, bf16[1,32,4224]{2,1,0:T(8,128)(2,1)S(1)}, u32[]{:S(2)}, u32[]{:S(2)}) collective-permute-start(bf16[1,32,4224]{2,1,0:T(8,128)(2,1)S(1)} %bitcast.45), channel_id=1, source_target_pairs={{0,24},{1,25},{2,26},{3,27},{4,28},{5,29},{6,30},{7,31},{8,16},{9,... | collective-permute-start | bytes 811016 | tf_op jit(solution)/shard_map/ppermute | solution.py:31
  31.4 28.2 %collective-permute-start.5 = (bf16[4,32,4224]{2,1,0:T(8,128)(2,1)S(1)}, bf16[4,32,4224]{2,1,0:T(8,128)(2,1)S(1)}, u32[]{:S(2)}, u32[]{:S(2)}) collective-permute-start(bf16[4,32,4224]{2,1,0:T(8,128)(2,1)S(1)} %pad_maximum_fusion.rest_0_.rest_8_.rest_2_), channel_id=1, source_target_pairs={{0,2},{1,5},{2,0},{3,7},{4,6},{5,1},{6,4},{7,3},{8,10},{9,13},{10,... | collective-permute-start | bytes 3244040 | tf_op jit(solution)/shard_map/ppermute | solution.py:31
  33.0 26.7 %collective-permute-start.6 = (bf16[4,32,4224]{2,1,0:T(8,128)(2,1)S(1)}, bf16[4,32,4224]{2,1,0:T(8,128)(2,1)S(1)}, u32[]{:S(2)}, u32[]{:S(2)}) collective-permute-start(bf16[4,32,4224]{2,1,0:T(8,128)(2,1)S(1)} %pad_maximum_fusion.rest_0_.rest_8_.rest_2_), channel_id=1, source_target_pairs={{0,4},{1,3},{2,6},{3,1},{4,0},{5,7},{6,2},{7,5},{8,12},{9,11},{10,... | collective-permute-start | bytes 3244040 | tf_op jit(solution)/shard_map/ppermute | solution.py:31
  79.6 27.7 %collective-permute-start.16 = (bf16[4,32,4096]{2,1,0:T(8,128)(2,1)}, bf16[4,32,4096]{2,1,0:T(8,128)(2,1)}, u32[]{:S(2)}, u32[]{:S(2)}) collective-permute-start(bf16[4,32,4096]{2,1,0:T(8,128)(2,1)} %pad_maximum_fusion.1.rest_0_), channel_id=1, source_target_pairs={{0,2},{1,5},{2,0},{3,7},{4,6},{5,1},{6,4},{7,3},{8,10},{9,13},{10,... | collective-permute-start | bytes 3145736 | tf_op jit(solution)/shard_map/ppermute | solution.py:31
  80.2 27.2 %collective-permute-start.17 = (bf16[4,32,4096]{2,1,0:T(8,128)(2,1)}, bf16[4,32,4096]{2,1,0:T(8,128)(2,1)}, u32[]{:S(2)}, u32[]{:S(2)}) collective-permute-start(bf16[4,32,4096]{2,1,0:T(8,128)(2,1)} %pad_maximum_fusion.1.rest_0_), channel_id=1, source_target_pairs={{0,4},{1,3},{2,6},{3,1},{4,0},{5,7},{6,2},{7,5},{8,12},{9,11},{10,... | collective-permute-start | bytes 3145736 | tf_op jit(solution)/shard_map/ppermute | solution.py:31
  80.7 26.7 %collective-permute-start.19 = (bf16[1,128,1024]{2,1,0:T(8,128)(2,1)}, bf16[1,128,1024]{2,1,0:T(8,128)(2,1)}, u32[]{:S(2)}, u32[]{:S(2)}) collective-permute-start(bf16[1,128,1024]{2,1,0:T(8,128)(2,1)} %bitcast.9), channel_id=1, source_target_pairs={{0,16},{1,17},{2,18},{3,19},{4,20},{5,21},{6,22},{7,23},{8,24},{9,... | collective-permute-start | bytes 786440 | tf_op jit(solution)/shard_map/ppermute | solution.py:31
  80.7 26.7 %collective-permute-start.20 = (bf16[1,128,1024]{2,1,0:T(8,128)(2,1)}, bf16[1,128,1024]{2,1,0:T(8,128)(2,1)}, u32[]{:S(2)}, u32[]{:S(2)}) collective-permute-start(bf16[1,128,1024]{2,1,0:T(8,128)(2,1)} %bitcast.9), channel_id=1, source_target_pairs={{0,24},{1,25},{2,26},{3,27},{4,28},{5,29},{6,30},{7,31},{8,16},{9,... | collective-permute-start | bytes 786440 | tf_op jit(solution)/shard_map/ppermute | solution.py:31
  82.3 25.0 %collective-permute-start.18 = (bf16[2,48,1024]{2,1,0:T(8,128)(2,1)}, bf16[2,48,1024]{2,1,0:T(8,128)(2,1)}, u32[]{:S(2)}, u32[]{:S(2)}) collective-permute-start(bf16[2,48,1024]{2,1,0:T(8,128)(2,1)} %pad_maximum_fusion.2), channel_id=1, source_target_pairs={{0,4},{1,3},{2,6},{3,1},{4,0},{5,7},{6,2},{7,5},{8,12},{9,11},{10,... | collective-permute-start | bytes 589832 | tf_op jit(solution)/shard_map/ppermute | solution.py:31
  109.4 26.2 %collective-permute-start.23 = (bf16[4,128,1024]{2,1,0:T(8,128)(2,1)S(1)}, bf16[4,128,1024]{2,1,0:T(8,128)(2,1)}, u32[]{:S(2)}, u32[]{:S(2)}) collective-permute-start(bf16[4,128,1024]{2,1,0:T(8,128)(2,1)S(1)} %constant_dynamic-update-slice_fusion.rest_0_), channel_id=1, source_target_pairs={{0,2},{1,5},{2,0},{3,7},{4,6},{5,1},{6,4},{7,3},{8,10},{9,13},{10,... | collective-permute-start | bytes 3145736 | tf_op jit(solution)/shard_map/ppermute | solution.py:31
  110.0 25.6 %collective-permute-start.22 = (bf16[4,32,4096]{2,1,0:T(8,128)(2,1)}, bf16[4,32,4096]{2,1,0:T(8,128)(2,1)}, u32[]{:S(2)}, u32[]{:S(2)}) collective-permute-start(bf16[4,32,4096]{2,1,0:T(8,128)(2,1)} %collective-permute-done.16.rest_1_), channel_id=1, source_target_pairs={{0,4},{1,3},{2,6},{3,1},{4,0},{5,7},{6,2},{7,5},{8,12},{9,11},{10,... | collective-permute-start | bytes 3145736 | tf_op jit(solution)/shard_map/ppermute | solution.py:31
  136.2 24.1 %collective-permute-start.21 = (bf16[4,128,1024]{2,1,0:T(8,128)(2,1)S(1)}, bf16[4,128,1024]{2,1,0:T(8,128)(2,1)S(1)}, u32[]{:S(2)}, u32[]{:S(2)}) collective-permute-start(bf16[4,128,1024]{2,1,0:T(8,128)(2,1)S(1)} %constant_dynamic-update-slice_fusion.rest_0_), channel_id=1, source_target_pairs={{0,4},{1,3},{2,6},{3,1},{4,0},{5,7},{6,2},{7,5},{8,12},{9,11},{10,... | collective-permute-start | bytes 3145736 | tf_op jit(solution)/shard_map/ppermute | solution.py:31
  137.0 25.3 %collective-permute-start.27 = (bf16[4,128,1024]{2,1,0:T(8,128)(2,1)}, bf16[4,128,1024]{2,1,0:T(8,128)(2,1)S(1)}, u32[]{:S(2)}, u32[]{:S(2)}) collective-permute-start(bf16[4,128,1024]{2,1,0:T(8,128)(2,1)} %collective-permute-done.23.rest_1_), channel_id=1, source_target_pairs={{0,4},{1,3},{2,6},{3,1},{4,0},{5,7},{6,2},{7,5},{8,12},{9,11},{10,... | collective-permute-start | bytes 3145736 | tf_op jit(solution)/shard_map/ppermute | solution.py:31
  245.7 23.8 %collective-permute-start.54 = (bf16[8,32,4096]{2,1,0:T(8,128)(2,1)}, bf16[8,32,4096]{2,1,0:T(8,128)(2,1)}, u32[]{:S(2)}, u32[]{:S(2)}) collective-permute-start(bf16[8,32,4096]{2,1,0:T(8,128)(2,1)} %get-tuple-element.344), channel_id=1, source_target_pairs={{0,1},{1,0},{2,3},{3,2},{4,5},{5,4},{6,7},{7,6},{8,9},{9,8},{10,11... | collective-permute-start | bytes 6291464 | tf_op jit(solution)/shard_map/ppermute | solution.py:31
  245.7 23.8 %collective-permute-start.55 = (bf16[8,32,4096]{2,1,0:T(8,128)(2,1)}, bf16[8,32,4096]{2,1,0:T(8,128)(2,1)}, u32[]{:S(2)}, u32[]{:S(2)}) collective-permute-start(bf16[8,32,4096]{2,1,0:T(8,128)(2,1)} %get-tuple-element.345), channel_id=1, source_target_pairs={{0,1},{1,0},{2,3},{3,2},{4,5},{5,4},{6,7},{7,6},{8,9},{9,8},{10,11... | collective-permute-start | bytes 6291464 | tf_op jit(solution)/shard_map/ppermute | solution.py:31
  246.2 23.3 %collective-permute-start.52 = (bf16[4,128,1024]{2,1,0:T(8,128)(2,1)}, bf16[4,128,1024]{2,1,0:T(8,128)(2,1)}, u32[]{:S(2)}, u32[]{:S(2)}) collective-permute-start(bf16[4,128,1024]{2,1,0:T(8,128)(2,1)} %get-tuple-element.337), channel_id=1, source_target_pairs={{0,4},{1,3},{2,6},{3,1},{4,0},{5,7},{6,2},{7,5},{8,12},{9,11},{10,... | collective-permute-start | bytes 3145736 | tf_op jit(solution)/shard_map/ppermute | solution.py:31
  268.0 23.2 %collective-permute-start.58 = (bf16[4,128,1024]{2,1,0:T(8,128)(2,1)}, bf16[4,128,1024]{2,1,0:T(8,128)(2,1)}, u32[]{:S(2)}, u32[]{:S(2)}) collective-permute-start(bf16[4,128,1024]{2,1,0:T(8,128)(2,1)} %add_convert_fusion.7), channel_id=1, source_target_pairs={{0,2},{1,5},{2,0},{3,7},{4,6},{5,1},{6,4},{7,3},{8,10},{9,13},{10,... | collective-permute-start | bytes 3145736 | tf_op jit(solution)/shard_map/ppermute | solution.py:31
  274.5 49.6 %collective-permute-start.56 = (bf16[4,32,4096]{2,1,0:T(8,128)(2,1)}, bf16[4,32,4096]{2,1,0:T(8,128)(2,1)}, u32[]{:S(2)}, u32[]{:S(2)}) collective-permute-start(bf16[4,32,4096]{2,1,0:T(8,128)(2,1)} %get-tuple-element.418), channel_id=1, source_target_pairs={{0,4},{1,3},{2,6},{3,1},{4,0},{5,7},{6,2},{7,5},{8,12},{9,11},{10,... | collective-permute-start | bytes 3145736 | tf_op jit(solution)/shard_map/ppermute | solution.py:31
  295.4 32.1 %collective-permute-start.59 = (bf16[4,32,4096]{2,1,0:T(8,128)(2,1)S(1)}, bf16[4,32,4096]{2,1,0:T(8,128)(2,1)S(1)}, u32[]{:S(2)}, u32[]{:S(2)}) collective-permute-start(bf16[4,32,4096]{2,1,0:T(8,128)(2,1)S(1)} %add_convert_fusion.6), channel_id=1, source_target_pairs={{0,2},{1,5},{2,0},{3,7},{4,6},{5,1},{6,4},{7,3},{8,10},{9,13},{10,... | collective-permute-start | bytes 3145736 | tf_op jit(solution)/shard_map/ppermute | solution.py:31
  299.5 24.5 %collective-permute-start.60 = (bf16[1,128,1024]{2,1,0:T(8,128)(2,1)S(1)}, bf16[1,128,1024]{2,1,0:T(8,128)(2,1)S(1)}, u32[]{:S(2)}, u32[]{:S(2)}) collective-permute-start(bf16[1,128,1024]{2,1,0:T(8,128)(2,1)S(1)} %get-tuple-element.434), channel_id=1, source_target_pairs={{0,8},{1,9},{2,10},{3,11},{4,12},{5,13},{6,14},{7,15},{8,0},{9,1},... | collective-permute-start | bytes 786440 | tf_op jit(solution)/shard_map/ppermute | solution.py:31
  302.0 25.6 %collective-permute-start.62 = (bf16[1,128,1024]{2,1,0:T(8,128)(2,1)S(1)}, bf16[1,128,1024]{2,1,0:T(8,128)(2,1)S(1)}, u32[]{:S(2)}, u32[]{:S(2)}) collective-permute-start(bf16[1,128,1024]{2,1,0:T(8,128)(2,1)S(1)} %get-tuple-element.432), channel_id=1, source_target_pairs={{0,24},{1,25},{2,26},{3,27},{4,28},{5,29},{6,30},{7,31},{8,16},{9,... | collective-permute-start | bytes 786440 | tf_op jit(solution)/shard_map/ppermute | solution.py:31
  336.1 28.0 %collective-permute-start.65 = (bf16[4,32,4224]{2,1,0:T(8,128)(2,1)S(1)}, bf16[4,32,4224]{2,1,0:T(8,128)(2,1)S(1)}, u32[]{:S(2)}, u32[]{:S(2)}) collective-permute-start(bf16[4,32,4224]{2,1,0:T(8,128)(2,1)S(1)} %get-tuple-element.388), channel_id=1, source_target_pairs={{0,4},{1,3},{2,6},{3,1},{4,0},{5,7},{6,2},{7,5},{8,12},{9,11},{10,... | collective-permute-start | bytes 3244040 | tf_op jit(solution)/shard_map/ppermute | solution.py:31
  336.5 27.7 %collective-permute-start.66 = (bf16[4,32,4224]{2,1,0:T(8,128)(2,1)S(1)}, bf16[4,32,4224]{2,1,0:T(8,128)(2,1)S(1)}, u32[]{:S(2)}, u32[]{:S(2)}) collective-permute-start(bf16[4,32,4224]{2,1,0:T(8,128)(2,1)S(1)} %get-tuple-element.389), channel_id=1, source_target_pairs={{0,4},{1,3},{2,6},{3,1},{4,0},{5,7},{6,2},{7,5},{8,12},{9,11},{10,... | collective-permute-start | bytes 3244040 | tf_op jit(solution)/shard_map/ppermute | solution.py:31
  340.1 24.0 %collective-permute-start.69 = (bf16[1,32,4096]{2,1,0:T(8,128)(2,1)S(1)}, bf16[1,32,4096]{2,1,0:T(8,128)(2,1)S(1)}, u32[]{:S(2)}, u32[]{:S(2)}) collective-permute-start(bf16[1,32,4096]{2,1,0:T(8,128)(2,1)S(1)} %get-tuple-element.429), channel_id=1, source_target_pairs={{0,24},{1,25},{2,26},{3,27},{4,28},{5,29},{6,30},{7,31},{8,16},{9,... | collective-permute-start | bytes 786440 | tf_op jit(solution)/shard_map/ppermute | solution.py:31
  (141 other events, 1544.4 us)

commit v4 on v3

--- a/solution.py
+++ b/solution.py
@@ -101,19 +101,19 @@
             picked = jnp.take(every, picked, axis=0)
             self.operands = [picked[:, row : row + height, col : col + width].reshape(self.shape)]
 
-    def region(self, table, step):
-        height = 8 * self.piece[1]
-        start = ((table[0] // 8) ^ step) * height
+    def region(self, table, step, group=1):
+        height = 8 * self.piece[1] * group
+        start = ((table[0] // (8 * group)) ^ step) * height
         return pl.ds(pl.multiple_of(start, height), height)
 
-    def start(self, table, refs, target, sems, by_step=False, columns=None):
+    def start(self, table, refs, target, sems, group=0, columns=None):
         row, height, col, width = self.piece
         first, width = columns or (0, width)
         columns = pl.ds(first, width)
         far = self.count // 4
         if not self.slots:
-            for step in range(far if by_step else 1):
-                some = self.region(table, step) if by_step else pl.ds(0, self.shape[0])
+            for step in range(far // group if group else 1):
+                some = self.region(table, step, group) if group else pl.ds(0, self.shape[0])
                 source = refs[0].at[some, columns]
                 pltpu.make_async_copy(source, target.at[some, columns], sems.at[step]).start()
             return
@@ -124,7 +124,7 @@
             pltpu.make_async_copy(
                 found[slot].at[pl.ds(row, height), pl.ds(col + first, width)],
                 target.at[pl.ds(block, height), columns],
-                sems.at[steps[slot] if by_step else 0],
+                sems.at[steps[slot] // group if group else 0],
             ).start()
 
 
@@ -330,28 +330,76 @@
     )(table, second_in, *weight.operands)
 
 
-def latent_kernel(table, hidden, middle, noise, choose, comp_tables, down, to_latent):
+def half_specs(cells, height, cols, far, turns):
+    slots = [turn * far + other * 4 * far for other in (0, 1) for turn in turns]
+
+    def columns(slot):
+        return pl.BlockSpec((cells, height), lambda step, table: (0, table[slot + step]))
+
+    rows = pl.BlockSpec((1, height, cols), lambda step, table: (step, 0, 0))
+    return [columns(slot) for slot in slots] + [rows] * len(slots)
+
+
+def half_product(refs):
+    half = len(refs) // 2
+    left = jnp.concatenate([ref[...] for ref in refs[:half]], axis=1)
+    return matmul(left, jnp.concatenate([ref[0] for ref in refs[half:]], axis=0))
+
+
+def down_half(table, hidden, middle, parts, turns):
+    cells, width = middle.shape
+    far, height = parts[0].shape[:2]
+
+    def kernel(table_ref, mid_ref, *rest):
+        refs, total_ref = rest[:-1], rest[-1]
+
+        @pl.when(pl.program_id(0) == 0)
+        def _():
+            total_ref[...] = mid_ref[...]
+
+        total_ref[...] += half_product(refs)
+
+    return pl.pallas_call(
+        kernel,
+        grid_spec=by_region(
+            far,
+            [whole(cells, width)] + half_specs(cells, height, width, far, turns),
+            whole(cells, width),
+            [],
+        ),
+        out_shape=jax.ShapeDtypeStruct((cells, width), FULL),
+        compiler_params=params(24),
+        cost_estimate=cost(0, 0),
+        name="down_half",
+    )(table, middle, *[hidden] * 4, *parts)
+
+
+def latent_kernel(table, hidden, middle, noise, choose, comp_tables, down, to_latent, parts=None, turns=()):
     cells, width = middle.shape
     latent = noise.shape[1]
-    parts, more = len(down.operands), len(to_latent.operands)
+    mine, more = (8 if parts else 1 + len(down.operands)), len(to_latent.operands)
     steps = down.count // 4
     tile = hidden.shape[1] // steps
 
-    def kernel(table_ref, hidden_ref, mid_ref, noise_ref, choose_ref, tables_ref, *rest):
-        refs, rest = rest[:parts], rest[parts:]
+    def kernel(table_ref, mid_ref, noise_ref, choose_ref, tables_ref, *rest):
+        refs, rest = rest[:mine], rest[mine:]
         latent_refs, rest = rest[:more], rest[more:]
-        carried_ref, moments_ref, sample_ref, kl_ref, total, held, latent_held, sems = rest
+        carried_ref, moments_ref, sample_ref, kl_ref, total, *held, latent_held, sems = rest
         step = pl.program_id(0)
 
         @pl.when(step == 0)
         def _():
-            down.start(table_ref, refs, held, sems, True)
+            if not parts:
+                down.start(table_ref, refs[1:], held[0], sems, 1)
             to_latent.start(table_ref, latent_refs, latent_held, sems.at[pl.ds(steps, 1)])
             total[...] = mid_ref[...]
 
-        some = held.at[down.region(table_ref, step)]
-        arrived(some, sems.at[step])
-        total[...] += matmul(hidden_ref[...], some[...])
+        if parts:
+            total[...] += half_product(refs)
+        else:
+            some = held[0].at[down.region(table_ref, step)]
+            arrived(some, sems.at[step])
+            total[...] += matmul(refs[0][...], some[...])
 
         @pl.when(step == steps - 1)
         def _():
@@ -369,13 +417,18 @@
         kernel,
         grid_spec=by_region(
             steps,
-            [pl.BlockSpec((cells, tile), region_columns), whole(cells, width)]
-            + [whole(cells, latent), whole(*choose.shape), whole(*comp_tables.shape)]
-            + [FAR_AWAY] * (parts + more),
+            [whole(cells, width), whole(cells, latent), whole(*choose.shape)]
+            + [whole(*comp_tables.shape)]
+            + (
+                half_specs(cells, tile // 8, width, steps, turns)
+                if parts
+                else [pl.BlockSpec((cells, tile), region_columns)] + [FAR_AWAY] * (mine - 1)
+            )
+            + [FAR_AWAY] * more,
             [whole(cells, width), whole(cells, 2 * latent), whole(cells, latent), whole(1, latent)],
             [
                 pltpu.VMEM((cells, width), FULL),
-                pltpu.VMEM(down.shape, LOW),
+                *([] if parts else [pltpu.VMEM(down.shape, LOW)]),
                 pltpu.VMEM(to_latent.shape, LOW),
                 pltpu.SemaphoreType.DMA((steps + 1,)),
             ],
@@ -389,7 +442,15 @@
         compiler_params=params(30),
         cost_estimate=cost(2 * cells * width * (hidden.shape[1] + width), 20 << 20),
         name="latent",
-    )(table, hidden, middle, noise, choose, comp_tables, *down.operands, *to_latent.operands)
+    )(
+        table,
+        middle,
+        noise,
+        choose,
+        comp_tables,
+        *([hidden] * 4 + parts if parts else [hidden, *down.operands]),
+        *to_latent.operands,
+    )
 
 
 def decode_kernel(table, sample, cotangent, turned, decode):
@@ -608,7 +669,7 @@
 
         @pl.when(step == 0)
         def _():
-            down.start(table_ref, refs, held, sems, True)
+            down.start(table_ref, refs, held, sems, 1)
 
         some = held.at[down.region(table_ref, step)]
         arrived(some, sems.at[step])
@@ -634,19 +695,20 @@
     cells, width = grad_carried.shape
     cols = grad_up_proj.shape[1]
     parts, more = len(up.operands), len(out_proj.operands)
+    steps = up.count // 8
 
     def kernel(table_ref, gu_ref, gc_ref, mid_ref, mixed_ref, turned_ref, *rest):
         refs, rest = rest[:parts], rest[parts:]
         out_refs, rest = rest[:more], rest[more:]
         gm_ref, go_ref, gx_ref, gain_ref, gu_held, second, held, out_held, sems = rest
-        loading = pltpu.make_async_copy(gu_ref, gu_held, sems.at[2])
+        loading = pltpu.make_async_copy(gu_ref, gu_held, sems.at[steps + 1])
         loading.start()
-        up.start(table_ref, refs, held, sems)
-        out_proj.start(table_ref, out_refs, out_held, sems.at[pl.ds(1, 1)])
+        up.start(table_ref, refs, held, sems, 2)
+        out_proj.start(table_ref, out_refs, out_held, sems.at[pl.ds(steps, 1)])
         loading.wait()
-        arrived(held, sems.at[0])
-        for column in range(0, width, 512):
-            some = pl.ds(column, 512)
+        for step in range(steps):
+            some = up.region(table_ref, step, 2)
+            arrived(held.at[some], sems.at[step])
             second[:, some] = right_product(gu_held[...], held[some])
         normed, scale = norm_parts(mid_ref[...])
         grad_second = second[...]
@@ -656,7 +718,7 @@
         gm_ref[...] = grad_middle
         branch = grad_middle.astype(LOW)
         go_ref[...] = left_product(mixed_ref[...], branch).astype(LOW)
-        arrived(out_held, sems.at[1])
+        arrived(out_held, sems.at[steps])
         gx_ref[...] = right_product(branch, out_held[...]).astype(LOW)
 
     return pl.pallas_call(
@@ -674,9 +736,9 @@
             pltpu.VMEM((cells, width), FULL),
             pltpu.VMEM(up.shape, LOW),
             pltpu.VMEM(out_proj.shape, LOW),
-            pltpu.SemaphoreType.DMA((3,)),
-        ],
-        compiler_params=params(),
+            pltpu.SemaphoreType.DMA((steps + 2,)),
+        ],
+        compiler_params=params(50),
         cost_estimate=cost(2 * cells * width * (cols + width), 22 << 20),
         name="middle_back",
     )(table, grad_up_proj, grad_carried, middle, mixed, turned, *up.operands, *out_proj.operands)
@@ -685,15 +747,16 @@
 def input_back_kernel(table, grad_packed, grad_middle, inputs, turned, small, columns, weight):
     cells, width = inputs.shape
     parts = len(weight.operands)
+    steps = weight.count // 8
 
     def kernel(table_ref, gq_ref, gk_ref, gv_ref, gm_ref, in_ref, turned_ref, small_ref, *rest):
         column_refs, rest = rest[: len(columns)], rest[len(columns) :]
         refs, (gx_ref, small_out, first, held, sems) = rest[:parts], rest[parts:]
-        weight.start(table_ref, refs, held, sems)
+        weight.start(table_ref, refs, held, sems, 2)
         normed, scale = norm_parts(in_ref[...].astype(FULL))
-        arrived(held, sems.at[0])
-        for column in range(0, width, 512):
-            some = pl.ds(column, 512)
+        for step in range(steps):
+            some = weight.region(table_ref, step, 2)
+            arrived(held.at[some], sems.at[step])
             first[:, some] = sum(
                 right_product(ref[...], held[some, i * width : (i + 1) * width])
                 for i, ref in enumerate((gq_ref, gk_ref, gv_ref))
@@ -719,9 +782,9 @@
         scratch_shapes=[
             pltpu.VMEM((cells, width), FULL),
             pltpu.VMEM(weight.shape, LOW),
-            pltpu.SemaphoreType.DMA((1,)),
-        ],
-        compiler_params=params(26),
+            pltpu.SemaphoreType.DMA((steps,)),
+        ],
+        compiler_params=params(44),
         cost_estimate=cost(6 * cells * width * width, 18 << 20),
         name="input_back",
     )(table, *grad_packed, grad_middle, inputs, turned, small, *columns, *weight.operands)
@@ -735,7 +798,9 @@
 
 
 def join(*parts):
-    return jnp.concatenate(parts, axis=0)
+    _, rows, cols = parts[0].shape
+    flat = jnp.concatenate([part.reshape(-1, cols) for part in parts], axis=0)
+    return flat.reshape(-1, rows, cols)
 
 
 def far_start(block):
@@ -760,6 +825,19 @@
     for one in others:
         total = total + one.astype(FULL)
     return total
+
+
+def odd_even(*terms):
+    return [add_all(one[0], one[1:]).astype(LOW) for one in zip(*[(t[1::2], t[0::2]) for t in terms])]
+
+
+def far_last(odd, even, bit):
+    got = far_exchange(odd, bit)
+    while even.shape[0] > 1:
+        bit *= 2
+        odd, even = odd_even(even, got)
+        got = far_exchange(odd, bit)
+    return even, got
 
 
 def far_slots(value, size):
@@ -891,7 +969,7 @@
         ],
         out_specs=[pl.BlockSpec((cells, 128), lambda i: (0, i))] * 3,
         out_shape=[jax.ShapeDtypeStruct((cells, width), LOW)] * 3,
-        compiler_params=params(),
+        compiler_params=params(44),
         cost_estimate=cost(10 * cells * cells * width, 24 << 20),
         name="attention_backward",
     )(packed, packed, packed, grad_mixed, mixed, attn)
@@ -1042,13 +1120,31 @@
     last_all = join(last_four, *[last_far[mask] for mask in far_masks()])
     last_there = send_core(last_all)
     down_c2, down_c3 = send_core(down_m2), send_core(down_m3)
-    last_there, down_c2, down_c3 = hold(last_there, down_c2, down_c3)
+    in_halves = down_rows % 128 == 0
+    if in_halves:
+        middle_half = down_half(
+            table, hidden, middle, [down_four, down_m1, down_c0, down_c1], (0, 1)
+        )
+        last_there, down_c2, down_c3, middle_half = hold(
+            last_there, down_c2, down_c3, middle_half
+        )
+    else:
+        last_there, down_c2, down_c3 = hold(last_there, down_c2, down_c3)
     to_latent, decode = [Rows([last_all], [last_there], piece, False) for piece in last_pieces]
     down = Rows(
         [down_four, down_m1, down_m2, down_m3], [down_c0, down_c1, down_c2, down_c3], down_pieces[0]
     )
     carried, moments, sample, kl_part = latent_kernel(
-        table, hidden, middle, noise_rows, choose, comp_tables, down, to_latent
+        table,
+        hidden,
+        middle_half if in_halves else middle,
+        noise_rows,
+        choose,
+        comp_tables,
+        down,
+        to_latent,
+        [down_m2, down_m3, down_c2, down_c3] if in_halves else None,
+        (2, 3),
     )
     kl_sum = kl_part + send_core(kl_part)
     kl_sum, sample = hold(kl_sum, sample)
@@ -1101,8 +1197,11 @@
         table, second_in, [grad_up_proj], Slots(rows, up_cols), rows, "grad_up"
     )
     down_0, down_1, down_2 = [both_cores(down_slots, down_got, turn, far) for turn in range(3)]
-    down_m3, last_m3, down_0, down_1, down_2, *up_slots = hold(
-        down_m3, last_m3, down_0, down_1, down_2, *up_slots
+    tables_grad = comp.reshape(2, comps, devices, comp_cols)
+    tables_grad = tables_grad.transpose(2, 0, 1, 3).reshape(devices * rows, lanes)
+    small_grads = jnp.pad(tables_grad, ((0, 0), (16, 112 - lanes)))
+    down_m3, last_m3, small_grads, down_0, down_1, down_2, *up_slots = hold(
+        down_m3, last_m3, small_grads, down_0, down_1, down_2, *up_slots
     )
 
     up_got = [send_core(one) for one in up_slots[2:]]
@@ -1111,11 +1210,8 @@
     grad_middle, grad_out, grad_mixed, grad_gain_two = middle_back_kernel(
         table, grad_up_proj, grad_carried, middle, mixed, turned, up, out_proj
     )
-    tables_grad = comp.reshape(2, comps, devices, comp_cols)
-    tables_grad = tables_grad.transpose(2, 0, 1, 3).reshape(devices * rows, lanes)
-    small_grads = jnp.pad(tables_grad, ((0, 0), (16, 112 - lanes)))
-    down_m2, last_m1, grad_mixed, grad_out, small_grads, *up_got = hold(
-        down_m2, last_m1, grad_mixed, grad_out, small_grads, *up_got
+    down_m2, last_m1, grad_mixed, grad_out, *up_got = hold(
+        down_m2, last_m1, grad_mixed, grad_out, *up_got
     )
 
     up_m3 = near_second(both_cores(up_slots, up_got, 3, far))
@@ -1125,8 +1221,8 @@
 
     up_m2 = near_second(both_cores(up_slots, up_got, 2, far))
     up_m1 = near_first(add_slots(far, (up_slots[0], far), (up_got[0], far), (up_m3, 0)))
-    down_low = add_slots(far, (down_0, 0), (down_m2, 0), (down_m1, 0))
-    down_far = far_slots(down_low, 1)
+    down_odd, down_even = odd_even(down_0, down_m2, down_m1)
+    down_far = far_exchange(down_odd, 1)
     grad_inputs, small_grads = input_back_kernel(
         table,
         grad_packed,
@@ -1146,31 +1242,42 @@
         "grad_qkv",
         [(grad_out, rows, 0, qkv_cols), (small_grads, rows, 0, qkv_cols + out_cols)],
     )
-    up_m2, up_m1, grad_inputs, *rest = hold(up_m2, up_m1, grad_inputs, *first_slots, *down_far)
-    first_slots, down_far = rest[:4], rest[4:]
+    up_m2, up_m1, grad_inputs, down_far, *first_slots = hold(
+        up_m2, up_m1, grad_inputs, down_far, *first_slots
+    )
 
     first_high = send_core(first_slots[3])
-    up_low = add_slots(far, (up_slots[0], 0), (up_got[0], 0), (up_m2, 0), (up_m1, 0))
-    first_high, up_low, *first_slots = hold(first_high, up_low, *first_slots)
+    up_odd, up_even = odd_even(up_slots[0][:far], up_got[0][:far], up_m2, up_m1)
+    first_high, up_odd, up_even, *first_slots = hold(first_high, up_odd, up_even, *first_slots)
     first_low = send_core(first_slots[2])
     first_got = [first_low, first_high]
     first_3, first_2 = [both_cores(first_slots, first_got, turn, far) for turn in (3, 2)]
-    first_low, first_3, first_2, up_low = hold(first_low, first_3, first_2, up_low)
+    last_odd, last_even = odd_even(last_slots[0][:far], last_got[0][:far], last_m2, last_m1)
+    down_odd, down_even = odd_even(down_even, down_far)
+    first_low, first_3, first_2, last_odd, last_even, down_odd, down_even = hold(
+        first_low, first_3, first_2, last_odd, last_even, down_odd, down_even
+    )
 
     first_m3, first_m2 = near_second(first_3), near_second(first_2)
-    up_far = far_slots(up_low, 1)
-    last_low = add_slots(far, (last_slots[0], 0), (last_got[0], 0), (last_m2, 0), (last_m1, 0))
-    down_sum = add_all(down_low[0], [one[0] for one in down_far])
-    first_m3, first_m2, down_sum, last_low, *up_far = hold(
-        first_m3, first_m2, down_sum, last_low, *up_far
+    up_far = far_exchange(up_odd, 1)
+    last_far = far_exchange(last_odd, 1)
+    down_even, down_far = far_last(down_odd, down_even, 2)
+    first_m3, first_m2, up_far, last_far, down_far = hold(
+        first_m3, first_m2, up_far, last_far, down_far
     )
 
     first_m1 = near_first(add_slots(far, (first_slots[0], far), (first_low, far), (first_m3, 0)))
     inputs_there = send_core(grad_inputs)
-    up_sum = add_all(up_low[0], [one[0] for one in up_far])
-    last_far = far_slots(last_low, 1)
-    first_m1, inputs_there, up_sum, *last_far = hold(first_m1, inputs_there, up_sum, *last_far)
-    last_sum = add_all(last_low[0], [one[0] for one in last_far])
+    up_odd, up_even = odd_even(up_even, up_far)
+    last_odd, last_even = odd_even(last_even, last_far)
+    up_even, up_far = far_last(up_odd, up_even, 2)
+    last_even, last_far = far_last(last_odd, last_even, 2)
+    down_sum = add_all(down_even[0], [down_far[0]])
+    first_m1, inputs_there, down_sum, up_far, last_far = hold(
+        first_m1, inputs_there, down_sum, up_far, last_far
+    )
+    up_sum = add_all(up_even[0], [up_far[0]])
+    last_sum = add_all(last_even[0], [last_far[0]])
 
     result = jnp.where(
         core == 0,
@@ -1179,14 +1286,19 @@
     )[None]
     first_all = add_slots(far, (first_slots[0], 0), (first_low, 0), (first_m2, 0), (first_m1, 0))
     first_far = far_slots(first_all, 1)
-    first_sum = add_all(first_all[0], [one[0] for one in first_far])
-    small_sum = first_sum[:, qkv_cols + out_cols :]
+    pieces = [first_all[0], *[one[0] for one in first_far]]
+
+    def first_sum(start, size):
+        parts = [one[:, start : start + size] for one in pieces]
+        return add_all(parts[0], parts[1:])
+
+    small_sum = first_sum(qkv_cols + out_cols, 128)
     comp_mean_sum, comp_logvar_sum = small_sum[:, 16 : 16 + lanes].reshape(2, comps, comp_cols)
     return (
         result,
         small_sum[:, 0],
-        first_sum[:, :qkv_cols],
-        first_sum[:, qkv_cols : qkv_cols + out_cols],
+        first_sum(0, qkv_cols),
+        first_sum(qkv_cols, out_cols),
         small_sum[:, 1],
         up_sum,
         down_sum,

time: 414 us -> 408 us (0.986)
  waiting for transfers between devices: 137 us -> 128 us
    ppermute x78 -> x75, waiting for transfers between devices: 137 us -> 128 us  [send(): return lax.ppermute(value, EVERY, pairs)]
    convert_element_type x13 -> x10, other arithmetic: 22.1 us -> 15.3 us  [add_slots(): return add_all(parts[0], parts[1:]).astype(LOW)]
    unnamed x181 -> x158, local copies, waits for them, and re-layouts: 14.4 us -> 8.23 us
    convert_element_type x0 -> x6, other arithmetic: none -> 5.15 us  [odd_even(): add_all(one[0], one[1:]).astype(LOW)]
    pallas_call x1 -> x2, Pallas kernels: 11.8 us -> 15.2 us  [the longest x1 9.84 us: latent_kernel(): pl.pallas_call(kernel, grid_spec=by_region(steps, [whole(cells, width), w...]
    ppermute x78 -> x75, starting transfers between devices: 63 us -> 62.4 us  [send(): return lax.ppermute(value, EVERY, pairs)]
  transfers between devices with their start and end apart: 78 -> 75, of which waited for: 37 -> 30; matrix products, arithmetic and copies ran while one was open for 11% -> 11% of each run, Pallas kernels for 29% -> 31%
where the time goes in v4:
time: 408 us; the launch traced here: 404 us
  Pallas kernels  146 us (36%)
  waiting for transfers between devices  128 us (31%)
  starting transfers between devices  62.4 us (15%)
  other arithmetic  39.8 us (10%)
  local copies, waits for them, and re-layouts  25.1 us (6%)
    ppermute x75, waiting for transfers between devices, send(): return lax.ppermute(value, EVERY, pairs)  128 us
    ppermute x75, starting transfers between devices, send(): return lax.ppermute(value, EVERY, pairs)  62.4 us
    pallas_call x3, Pallas kernels, weight_grad(): pl.pallas_call(kernel, grid=(steps,), in_specs=[SCALARS, pl.BlockSpec((ce...  25.3 us
    pallas_call x2, Pallas kernels, attention_forward(): pl.pallas_call(kernel, grid=(last - first,), in_specs=[pl.BlockSpec((cell...  15.8 us
    convert_element_type x10, other arithmetic, add_slots(): return add_all(parts[0], parts[1:]).astype(LOW)  15.3 us
    pallas_call x1, Pallas kernels, attention_backward(): pl.pallas_call(kernel, grid=(steps,), in_specs=[pl.BlockSpec((cells, 128)...  14.9 us
    pallas_call x1, Pallas kernels, middle_back_kernel(): pl.pallas_call(kernel, in_specs=[SCALARS, ANYWHERE] + [INSIDE] * 4 + [ANY...  14 us
    pallas_call x1, Pallas kernels, up_kernel(): pl.pallas_call(kernel, grid=(cols // tile,), in_specs=[SCALARS, whole(cel...  11.6 us
  transfers between devices with their start and end apart: 75, of which 30 were waited for; matrix products, arithmetic and copies ran while one was open for 11% of the time, Pallas kernels for 31%

profile of v4, /device:TPU:8, one launch (start us, length us, event | category | flops | bytes accessed | tf_op | source)
XLA Modules:
  0.0 403.6 jit_solution(3274007129359180154)
XLA Ops:
  15.8 9.4 %collective-permute-done.3 = bf16[1,32,4224]{2,1,0:T(8,128)(2,1)S(1)} collective-permute-done((bf16[1,32,4224]{2,1,0:T(8,128)(2,1)S(1)}, bf16[1,32,4224]{2,1,0:T(8,128)(2,1)S(1)}, u32[]{:S(2)}, u32[]{:S(2)}) %collective-permute-start.3) | collective-permute-done | bytes 270368 | tf_op jit(solution)/shard_map/ppermute | solution.py:31
  25.3 6.0 %collective-permute-done.4 = bf16[1,32,4224]{2,1,0:T(8,128)(2,1)S(1)} collective-permute-done((bf16[1,32,4224]{2,1,0:T(8,128)(2,1)S(1)}, bf16[1,32,4224]{2,1,0:T(8,128)(2,1)S(1)}, u32[]{:S(2)}, u32[]{:S(2)}) %collective-permute-start.4) | collective-permute-done | bytes 270368 | tf_op jit(solution)/shard_map/ppermute | solution.py:31
  45.5 9.9 %collective-permute-done.8 = bf16[1,32,4096]{2,1,0:T(8,128)(2,1)S(1)} collective-permute-done((bf16[1,32,4096]{2,1,0:T(8,128)(2,1)S(1)}, bf16[1,32,4096]{2,1,0:T(8,128)(2,1)S(1)}, u32[]{:S(2)}, u32[]{:S(2)}) %collective-permute-start.8) | collective-permute-done | bytes 262176 | tf_op jit(solution)/shard_map/ppermute | solution.py:31
  60.7 8.4 %collective-permute-done.14 = bf16[1,128,1024]{2,1,0:T(8,128)(2,1)S(1)} collective-permute-done((bf16[1,128,1024]{2,1,0:T(8,128)(2,1)}, bf16[1,128,1024]{2,1,0:T(8,128)(2,1)S(1)}, u32[]{:S(2)}, u32[]{:S(2)}) %collective-permute-start.14) | collective-permute-done | bytes 262176 | tf_op jit(solution)/shard_map/ppermute | solution.py:31
  69.1 5.7 %collective-permute-done.10.rest_3_.rest_11_.rest_5_ = bf16[4,32,4224]{2,1,0:T(8,128)(2,1)S(1)} collective-permute-done((bf16[4,32,4224]{2,1,0:T(8,128)(2,1)S(1)}, bf16[4,32,4224]{2,1,0:T(8,128)(2,1)S(1)}, u32[]{:S(2)}, u32[]{:S(2)}) %collective-permute-start.10) | collective-permute-done | bytes 1081376 | tf_op jit(solution)/shard_map/ppermute | solution.py:31
  84.5 10.1 %first.1 = (bf16[512,1024]{1,0:T(8,128)(2,1)}, bf16[512,3072]{1,0:T(8,128)(2,1)}, bf16[1024,128]{1,0:T(8,128)(2,1)}, f32[128,1024]{1,0:T(8,128)}) custom-call(s32[96]{0:T(128)} %concatenate.65.table_ref, f32[512,1024]{1,0:T(8,128)} %subtract_multiply_fusion.normed_ref, bf16[4,32,4224]{2,1,0:T(8,128)(2,1)} %bitcast.68, bf16[4,32,4224]{2,1,0:T(8,128)(2,1)} %copy-done.7, ...), custom_call_target="tpu_custom_call" | custom-call | flops 1024 | bytes 1024 | tf_op jit(solution)/shard_map/first/pallas_call | solution.py:233
  94.6 7.9 %attention_forward.2 = (bf16[512,1024]{1,0:T(8,128)(2,1)}, bf16[16,512,512]{2,1,0:T(8,128)(2,1)}) custom-call(s32[512,1]{1,0:T(8,128)} %copy.38.seg_col, s32[1,512]{1,0:T(1,128)} %constant_dynamic-slice_fusion.1.seg_row, bf16[512,3072]{1,0:T(8,128)(2,1)} %get-tuple-element.247.q_ref.k_ref.v_ref, bf16[512,3072]{1,0:T(8,128)(2,1)} %get-tuple-element.247.q_ref.k_ref.v_ref, ...), custom_call_target="tpu_custom_call" | custom-call | flops 1024 | bytes 1024 | tf_op jit(solution)/shard_map/attention_forward/pallas_call | solution.py:906
  116.9 7.9 %attention_forward.3 = (bf16[512,1024]{1,0:T(8,128)(2,1)}, bf16[16,512,512]{2,1,0:T(8,128)(2,1)}) custom-call(s32[512,1]{1,0:T(8,128)} %copy.38.seg_col, s32[1,512]{1,0:T(1,128)} %constant_dynamic-slice_fusion.1.seg_row, bf16[512,3072]{1,0:T(8,128)(2,1)} %get-tuple-element.247.q_ref.k_ref.v_ref, ...), custom_call_target="tpu_custom_call", output_to_operand_aliasing={{0}: (5, {}), {1}: (6, {})} | custom-call | flops 1024 | bytes 1024 | tf_op jit(solution)/shard_map/attention_forward/pallas_call | solution.py:906
  124.8 5.9 %branch.1 = (f32[512,1024]{1,0:T(8,128)}, bf16[512,1024]{1,0:T(8,128)(2,1)}) custom-call(s32[96]{0:T(128)} %concatenate.65.table_ref, bf16[512,1024]{1,0:T(8,128)(2,1)} %get-tuple-element.250.mixed_ref, f32[512,1024]{1,0:T(8,128)} %get-tuple-element.413.in_ref, f32[128,1024]{1,0:T(8,128)} %get-tuple-element.251.turned_ref, bf16[4,32,4224]{2,1,0:T(8,128)(2,1)} %bitcast.70, ...), custom_call_target="tpu_custom_call" | custom-call | flops 1024 | bytes 1024 | tf_op jit(solution)/shard_map/branch/pallas_call | solution.py:274
  143.6 11.6 %up.1 = (bf16[512,4096]{1,0:T(8,128)(2,1)S(1)}, bf16[512,4096]{1,0:T(8,128)(2,1)S(1)}) custom-call(s32[96]{0:T(128)S(1)} %copy-done.39, bf16[512,1024]{1,0:T(8,128)(2,1)S(1)} %copy-done.30, bf16[4,32,4096]{2,1,0:T(8,128)(2,1)S(1)} %bitcast.80, bf16[4,32,4096]{2,1,0:T(8,128)(2,1)} %collective-permute-done.16.rest_1_, ...), custom_call_target="tpu_custom_call" | custom-call | flops 1024 | bytes 1024 | tf_op jit(solution)/shard_map/up/pallas_call | solution.py:317
  155.3 5.8 %collective-permute-done.30.rest_5_.rest_3_ = bf16[4,128,1024]{2,1,0:T(8,128)(2,1)S(1)} collective-permute-done((bf16[4,128,1024]{2,1,0:T(8,128)(2,1)}, bf16[4,128,1024]{2,1,0:T(8,128)(2,1)S(1)}, u32[]{:S(2)}, u32[]{:S(2)}) %collective-permute-start.30) | collective-permute-done | bytes 1048608 | tf_op jit(solution)/shard_map/ppermute | solution.py:31
  169.3 9.8 %latent.1 = (bf16[512,1024]{1,0:T(8,128)(2,1)S(1)}, f32[512,1024]{1,0:T(8,128)S(1)}, bf16[512,512]{1,0:T(8,128)(2,1)S(1)}, f32[1,512]{1,0:T(1,128)S(1)}) custom-call(s32[96]{0:T(128)S(1)} %copy-done.39, f32[512,1024]{1,0:T(8,128)S(1)} %down_half.1.mid_ref, f32[512,512]{1,0:T(8,128)S(1)} %copy-done.17, bf16[512,16]{1,0:T(8,128)(2,1)S(1)} %fusion.choose_ref, ...), custom_call_target="tpu_custom_call" | custom-call | flops 1024 | bytes 1024 | tf_op jit(solution)/shard_map/latent/pallas_call | solution.py:416
  195.0 10.3 %moments.1 = (bf16[512,1024]{1,0:T(8,128)(2,1)S(1)}, f32[2,16,512]{2,1,0:T(8,128)S(1)}, bf16[8,48,1024]{2,1,0:T(8,128)(2,1)S(1)}, bf16[8,48,1024]{2,1,0:T(8,128)...) custom-call(s32[96]{0:T(128)S(1)} %copy-done.39, f32[1]{0:T(128)S(6)} %min.3.weight_ref, ...), custom_call_target="tpu_custom_call" | custom-call | flops 1024 | bytes 1024 | tf_op jit(solution)/shard_map/moments/pallas_call | solution.py:570
  206.0 8.3 %grad_down.1 = (bf16[8,128,1024]{2,1,0:T(8,128)(2,1)S(1)}, bf16[8,128,1024]{2,1,0:T(8,128)(2,1)S(1)}, bf16[8,128,1024]{2,1,0:T(8,128)(2,1)S(1)}, bf16[8,128,1024]{2,1,0:T(8,128)(2,1)S(1)}) custom-call(s32[96]{0:T(128)S(1)} %copy-done.39, bf16[512,4096]{1,0:T(8,128)(2,1)S(1)} %get-tuple-element.316.rest_0_.rest_1_.rest_2_.rest_3_.left_ref, ...), custom_call_target="tpu_custom_call" | custom-call | flops 1024 | bytes 1024 | tf_op jit(solution)/shard_map/grad_down/pallas_call | solution.py:639
  217.5 7.5 %up_back.1.rest_0_.gu_ref = bf16[512,4096]{1,0:T(8,128)(2,1)S(1)} custom-call(s32[96]{0:T(128)S(1)} %copy-done.39, bf16[512,1024]{1,0:T(8,128)(2,1)S(1)} %get-tuple-element.322.rest_0_.grad_ref.gc_ref, bf16[512,4096]{1,0:T(8,128)(2,1)S(1)} %get-tuple-element.323.slope_ref, bf16[4,128,1024]{2,1,0:T(8,128)(2,1)S(1)} %bitcast.86, ...), custom_call_target="tpu_custom_call" | custom-call | flops 1024 | bytes 1024 | tf_op jit(solution)/shard_map/up_back/pallas_call | solution.py:678
  235.4 7.9 %grad_up.1 = (bf16[8,32,4096]{2,1,0:T(8,128)(2,1)S(1)}, bf16[8,32,4096]{2,1,0:T(8,128)(2,1)S(1)}, bf16[8,32,4096]{2,1,0:T(8,128)(2,1)}, bf16[8,32,4096]{2,1,0:T(8,128)(2,1)S(1)}) custom-call(s32[96]{0:T(128)S(1)} %copy-done.39, bf16[512,1024]{1,0:T(8,128)(2,1)S(1)} %copy-done.31, bf16[512,4096]{1,0:T(8,128)(2,1)S(1)} %copy-done.6), custom_call_target="tpu_custom_call" | custom-call | flops 1024 | bytes 1024 | tf_op jit(solution)/shard_map/grad_up/pallas_call | solution.py:639
  249.0 14.0 %middle_back.1 = (f32[512,1024]{1,0:T(8,128)}, bf16[1024,1024]{1,0:T(8,128)(2,1)}, bf16[512,1024]{1,0:T(8,128)(2,1)S(1)}, f32[1,1024]{1,0:T(1,128)S(1)}) custom-call(s32[96]{0:T(128)S(1)} %copy-done.39, bf16[512,4096]{1,0:T(8,128)(2,1)} %copy-done.5, bf16[512,1024]{1,0:T(8,128)(2,1)S(1)} %get-tuple-element.322.rest_0_.grad_ref.gc_ref, ...), custom_call_target="tpu_custom_call" | custom-call | flops 1024 | bytes 1024 | tf_op jit(solution)/shard_map/middle_back/pallas_call | solution.py:724
  271.7 14.9 %attention_backward.1 = (bf16[512,1024]{1,0:T(8,128)(2,1)S(1)}, bf16[512,1024]{1,0:T(8,128)(2,1)S(1)}, bf16[512,1024]{1,0:T(8,128)(2,1)S(1)}) custom-call(bf16[512,3072]{1,0:T(8,128)(2,1)S(1)} %copy-done.2, bf16[512,3072]{1,0:T(8,128)(2,1)S(1)} %copy-done.2, bf16[512,3072]{1,0:T(8,128)(2,1)S(1)} %copy-done.2, ...), custom_call_target="tpu_custom_call" | custom-call | flops 1024 | bytes 1024 | tf_op jit(solution)/shard_map/attention_backward/pallas_call | solution.py:959
  298.4 9.6 %input_back.1 = (f32[512,1024]{1,0:T(8,128)}, bf16[1024,128]{1,0:T(8,128)(2,1)S(1)}) custom-call(s32[96]{0:T(128)S(1)} %copy-done.39, bf16[512,1024]{1,0:T(8,128)(2,1)S(1)} %get-tuple-element.358.gq_ref.rest_0_, bf16[512,1024]{1,0:T(8,128)(2,1)S(1)} %get-tuple-element.359.gk_ref.rest_1_, bf16[512,1024]{1,0:T(8,128)(2,1)S(1)} %get-tuple-element.360.gv_ref.rest_2_, ...), custom_call_target="tpu_custom_call" | custom-call | flops 1024 | bytes 1024 | tf_op jit(solution)/shard_map/input_back/pallas_call | solution.py:774
  308.0 9.0 %grad_qkv.1 = (bf16[8,32,4224]{2,1,0:T(8,128)(2,1)S(1)}, bf16[8,32,4224]{2,1,0:T(8,128)(2,1)S(1)}, bf16[8,32,4224]{2,1,0:T(8,128)(2,1)S(1)}, bf16[8,32,4224]{2,1,0:T(8,128)(2,1)S(1)}) custom-call(s32[96]{0:T(128)S(1)} %copy-done.39, bf16[512,1024]{1,0:T(8,128)(2,1)S(1)} %copy-done.36, bf16[512,1024]{1,0:T(8,128)(2,1)S(1)} %get-tuple-element.358.gq_ref.rest_0_, ...), custom_call_target="tpu_custom_call" | custom-call | flops 1024 | bytes 1024 | tf_op jit(solution)/shard_map/grad_qkv/pallas_call | solution.py:639
  331.7 16.1 %collective-permute-done.65 = bf16[2,32,4096]{2,1,0:T(8,128)(2,1)S(1)} collective-permute-done((bf16[2,32,4096]{2,1,0:T(8,128)(2,1)S(1)}, bf16[2,32,4096]{2,1,0:T(8,128)(2,1)S(1)}, u32[]{:S(2)}, u32[]{:S(2)}) %collective-permute-start.65) | collective-permute-done | bytes 524320 | tf_op jit(solution)/shard_map/ppermute | solution.py:31
  359.8 10.9 %collective-permute-done.71 = bf16[1,48,1024]{2,1,0:T(8,128)(2,1)S(1)} collective-permute-done((bf16[1,48,1024]{2,1,0:T(8,128)(2,1)S(1)}, bf16[1,48,1024]{2,1,0:T(8,128)(2,1)S(1)}, u32[]{:S(2)}, u32[]{:S(2)}) %collective-permute-start.71) | collective-permute-done | bytes 98336 | tf_op jit(solution)/shard_map/ppermute | solution.py:31
  385.4 9.6 %collective-permute-done.73 = bf16[1,32,4224]{2,1,0:T(8,128)(2,1)S(1)} collective-permute-done((bf16[1,32,4224]{2,1,0:T(8,128)(2,1)S(1)}, bf16[1,32,4224]{2,1,0:T(8,128)(2,1)S(1)}, u32[]{:S(2)}, u32[]{:S(2)}) %collective-permute-start.73) | collective-permute-done | bytes 270368 | tf_op jit(solution)/shard_map/ppermute | solution.py:31
  395.0 5.5 %collective-permute-done.74 = bf16[1,32,4224]{2,1,0:T(8,128)(2,1)S(1)} collective-permute-done((bf16[1,32,4224]{2,1,0:T(8,128)(2,1)S(1)}, bf16[1,32,4224]{2,1,0:T(8,128)(2,1)S(1)}, u32[]{:S(2)}, u32[]{:S(2)}) %collective-permute-start.74) | collective-permute-done | bytes 270368 | tf_op jit(solution)/shard_map/ppermute | solution.py:31
  (373 shorter events, 179.0 us)
Async XLA Ops:
  3.2 28.0 %collective-permute-start = (bf16[512,1024]{1,0:T(8,128)(2,1)}, bf16[512,1024]{1,0:T(8,128)(2,1)}, u32[]{:S(2)}, u32[]{:S(2)}) collective-permute-start(bf16[512,1024]{1,0:T(8,128)(2,1)} %dynamic-slice_bitcast_fusion), channel_id=1, source_target_pairs={{0,1},{1,0},{2,3},{3,2},{4,5},{5,4},{6,7},{7,6},{8,9},{9,8},{10,11... | collective-permute-start | bytes 3145736 | tf_op jit(solution)/shard_map/ppermute | solution.py:31
  3.8 21.5 %collective-permute-start.3 = (bf16[1,32,4224]{2,1,0:T(8,128)(2,1)S(1)}, bf16[1,32,4224]{2,1,0:T(8,128)(2,1)S(1)}, u32[]{:S(2)}, u32[]{:S(2)}) collective-permute-start(bf16[1,32,4224]{2,1,0:T(8,128)(2,1)S(1)} %bitcast.93), channel_id=1, source_target_pairs={{0,16},{1,17},{2,18},{3,19},{4,20},{5,21},{6,22},{7,23},{8,24},{9,... | collective-permute-start | bytes 811016 | tf_op jit(solution)/shard_map/ppermute | solution.py:31
  6.8 24.5 %collective-permute-start.4 = (bf16[1,32,4224]{2,1,0:T(8,128)(2,1)S(1)}, bf16[1,32,4224]{2,1,0:T(8,128)(2,1)S(1)}, u32[]{:S(2)}, u32[]{:S(2)}) collective-permute-start(bf16[1,32,4224]{2,1,0:T(8,128)(2,1)S(1)} %bitcast.94), channel_id=1, source_target_pairs={{0,24},{1,25},{2,26},{3,27},{4,28},{5,29},{6,30},{7,31},{8,16},{9,... | collective-permute-start | bytes 811016 | tf_op jit(solution)/shard_map/ppermute | solution.py:31
  31.4 28.2 %collective-permute-start.5 = (bf16[4,32,4224]{2,1,0:T(8,128)(2,1)S(1)}, bf16[4,32,4224]{2,1,0:T(8,128)(2,1)S(1)}, u32[]{:S(2)}, u32[]{:S(2)}) collective-permute-start(bf16[4,32,4224]{2,1,0:T(8,128)(2,1)S(1)} %bitcast.65), channel_id=1, source_target_pairs={{0,2},{1,5},{2,0},{3,7},{4,6},{5,1},{6,4},{7,3},{8,10},{9,13},{10,... | collective-permute-start | bytes 3244040 | tf_op jit(solution)/shard_map/ppermute | solution.py:31
  32.9 26.7 %collective-permute-start.6 = (bf16[4,32,4224]{2,1,0:T(8,128)(2,1)S(1)}, bf16[4,32,4224]{2,1,0:T(8,128)(2,1)S(1)}, u32[]{:S(2)}, u32[]{:S(2)}) collective-permute-start(bf16[4,32,4224]{2,1,0:T(8,128)(2,1)S(1)} %bitcast.66), channel_id=1, source_target_pairs={{0,4},{1,3},{2,6},{3,1},{4,0},{5,7},{6,2},{7,5},{8,12},{9,11},{10,... | collective-permute-start | bytes 3244040 | tf_op jit(solution)/shard_map/ppermute | solution.py:31
  34.4 20.9 %collective-permute-start.8 = (bf16[1,32,4096]{2,1,0:T(8,128)(2,1)S(1)}, bf16[1,32,4096]{2,1,0:T(8,128)(2,1)S(1)}, u32[]{:S(2)}, u32[]{:S(2)}) collective-permute-start(bf16[1,32,4096]{2,1,0:T(8,128)(2,1)S(1)} %bitcast.112), channel_id=1, source_target_pairs={{0,16},{1,17},{2,18},{3,19},{4,20},{5,21},{6,22},{7,23},{8,24},{9,... | collective-permute-start | bytes 786440 | tf_op jit(solution)/shard_map/ppermute | solution.py:31
  37.5 22.1 %collective-permute-start.9 = (bf16[1,32,4096]{2,1,0:T(8,128)(2,1)S(1)}, bf16[1,32,4096]{2,1,0:T(8,128)(2,1)S(1)}, u32[]{:S(2)}, u32[]{:S(2)}) collective-permute-start(bf16[1,32,4096]{2,1,0:T(8,128)(2,1)S(1)} %bitcast.113), channel_id=1, source_target_pairs={{0,24},{1,25},{2,26},{3,27},{4,28},{5,29},{6,30},{7,31},{8,16},{9,... | collective-permute-start | bytes 786440 | tf_op jit(solution)/shard_map/ppermute | solution.py:31
  79.5 27.5 %collective-permute-start.16 = (bf16[4,32,4096]{2,1,0:T(8,128)(2,1)S(1)}, bf16[4,32,4096]{2,1,0:T(8,128)(2,1)}, u32[]{:S(2)}, u32[]{:S(2)}) collective-permute-start(bf16[4,32,4096]{2,1,0:T(8,128)(2,1)S(1)} %bitcast.77), channel_id=1, source_target_pairs={{0,2},{1,5},{2,0},{3,7},{4,6},{5,1},{6,4},{7,3},{8,10},{9,13},{10,... | collective-permute-start | bytes 3145736 | tf_op jit(solution)/shard_map/ppermute | solution.py:31
  80.0 27.0 %collective-permute-start.17 = (bf16[4,32,4096]{2,1,0:T(8,128)(2,1)S(1)}, bf16[4,32,4096]{2,1,0:T(8,128)(2,1)}, u32[]{:S(2)}, u32[]{:S(2)}) collective-permute-start(bf16[4,32,4096]{2,1,0:T(8,128)(2,1)S(1)} %bitcast.78), channel_id=1, source_target_pairs={{0,4},{1,3},{2,6},{3,1},{4,0},{5,7},{6,2},{7,5},{8,12},{9,11},{10,... | collective-permute-start | bytes 3145736 | tf_op jit(solution)/shard_map/ppermute | solution.py:31
  80.5 26.5 %collective-permute-start.19 = (bf16[1,128,1024]{2,1,0:T(8,128)(2,1)}, bf16[1,128,1024]{2,1,0:T(8,128)(2,1)}, u32[]{:S(2)}, u32[]{:S(2)}) collective-permute-start(bf16[1,128,1024]{2,1,0:T(8,128)(2,1)} %bitcast.15), channel_id=1, source_target_pairs={{0,16},{1,17},{2,18},{3,19},{4,20},{5,21},{6,22},{7,23},{8,24},{9,... | collective-permute-start | bytes 786440 | tf_op jit(solution)/shard_map/ppermute | solution.py:31
  80.5 26.5 %collective-permute-start.20 = (bf16[1,128,1024]{2,1,0:T(8,128)(2,1)}, bf16[1,128,1024]{2,1,0:T(8,128)(2,1)}, u32[]{:S(2)}, u32[]{:S(2)}) collective-permute-start(bf16[1,128,1024]{2,1,0:T(8,128)(2,1)} %bitcast.15), channel_id=1, source_target_pairs={{0,24},{1,25},{2,26},{3,27},{4,28},{5,29},{6,30},{7,31},{8,16},{9,... | collective-permute-start | bytes 786440 | tf_op jit(solution)/shard_map/ppermute | solution.py:31
  82.1 24.8 %collective-permute-start.18 = (bf16[2,48,1024]{2,1,0:T(8,128)(2,1)}, bf16[2,48,1024]{2,1,0:T(8,128)(2,1)}, u32[]{:S(2)}, u32[]{:S(2)}) collective-permute-start(bf16[2,48,1024]{2,1,0:T(8,128)(2,1)} %bitcast.13), channel_id=1, source_target_pairs={{0,4},{1,3},{2,6},{3,1},{4,0},{5,7},{6,2},{7,5},{8,12},{9,11},{10,... | collective-permute-start | bytes 589832 | tf_op jit(solution)/shard_map/ppermute | solution.py:31
  106.9 23.8 %collective-permute-start.23 = (bf16[4,32,4096]{2,1,0:T(8,128)(2,1)S(1)}, bf16[4,32,4096]{2,1,0:T(8,128)(2,1)S(1)}, u32[]{:S(2)}, u32[]{:S(2)}) collective-permute-start(bf16[4,32,4096]{2,1,0:T(8,128)(2,1)S(1)} %bitcast.79), channel_id=1, source_target_pairs={{0,1},{1,0},{2,3},{3,2},{4,5},{5,4},{6,7},{7,6},{8,9},{9,8},{10,11... | collective-permute-start | bytes 3145736 | tf_op jit(solution)/shard_map/ppermute | solution.py:31
  108.2 26.2 %collective-permute-start.22 = (bf16[4,128,1024]{2,1,0:T(8,128)(2,1)S(1)}, bf16[4,128,1024]{2,1,0:T(8,128)(2,1)}, u32[]{:S(2)}, u32[]{:S(2)}) collective-permute-start(bf16[4,128,1024]{2,1,0:T(8,128)(2,1)S(1)} %bitcast.82), channel_id=1, source_target_pairs={{0,2},{1,5},{2,0},{3,7},{4,6},{5,1},{6,4},{7,3},{8,10},{9,13},{10,... | collective-permute-start | bytes 3145736 | tf_op jit(solution)/shard_map/ppermute | solution.py:31
  108.8 25.6 %collective-permute-start.21 = (bf16[4,32,4096]{2,1,0:T(8,128)(2,1)}, bf16[4,32,4096]{2,1,0:T(8,128)(2,1)}, u32[]{:S(2)}, u32[]{:S(2)}) collective-permute-start(bf16[4,32,4096]{2,1,0:T(8,128)(2,1)} %collective-permute-done.16.rest_1_), channel_id=1, source_target_pairs={{0,4},{1,3},{2,6},{3,1},{4,0},{5,7},{6,2},{7,5},{8,12},{9,11},{10,... | collective-permute-start | bytes 3145736 | tf_op jit(solution)/shard_map/ppermute | solution.py:31
  135.8 25.3 %collective-permute-start.30 = (bf16[4,128,1024]{2,1,0:T(8,128)(2,1)}, bf16[4,128,1024]{2,1,0:T(8,128)(2,1)S(1)}, u32[]{:S(2)}, u32[]{:S(2)}) collective-permute-start(bf16[4,128,1024]{2,1,0:T(8,128)(2,1)} %collective-permute-done.22.rest_5_.rest_1_), channel_id=1, source_target_pairs={{0,4},{1,3},{2,6},{3,1},{4,0},{5,7},{6,2},{7,5},{8,12},{9,11},{10,... | collective-permute-start | bytes 3145736 | tf_op jit(solution)/shard_map/ppermute | solution.py:31
  264.7 23.5 %collective-permute-start.58 = (bf16[4,128,1024]{2,1,0:T(8,128)(2,1)S(1)}, bf16[4,128,1024]{2,1,0:T(8,128)(2,1)S(1)}, u32[]{:S(2)}, u32[]{:S(2)}) collective-permute-start(bf16[4,128,1024]{2,1,0:T(8,128)(2,1)S(1)} %add_convert_fusion.5), channel_id=1, source_target_pairs={{0,2},{1,5},{2,0},{3,7},{4,6},{5,1},{6,4},{7,3},{8,10},{9,13},{10,... | collective-permute-start | bytes 3145736 | tf_op jit(solution)/shard_map/ppermute | solution.py:31
  270.4 46.6 %collective-permute-start.56 = (bf16[4,32,4096]{2,1,0:T(8,128)(2,1)}, bf16[4,32,4096]{2,1,0:T(8,128)(2,1)S(1)}, u32[]{:S(2)}, u32[]{:S(2)}) collective-permute-start(bf16[4,32,4096]{2,1,0:T(8,128)(2,1)} %get-tuple-element.420), channel_id=1, source_target_pairs={{0,4},{1,3},{2,6},{3,1},{4,0},{5,7},{6,2},{7,5},{8,12},{9,11},{10,... | collective-permute-start | bytes 3145736 | tf_op jit(solution)/shard_map/ppermute | solution.py:31
  292.2 24.9 %collective-permute-start.59 = (bf16[4,32,4096]{2,1,0:T(8,128)(2,1)}, bf16[4,32,4096]{2,1,0:T(8,128)(2,1)S(1)}, u32[]{:S(2)}, u32[]{:S(2)}) collective-permute-start(bf16[4,32,4096]{2,1,0:T(8,128)(2,1)} %add_convert_fusion.4), channel_id=1, source_target_pairs={{0,2},{1,5},{2,0},{3,7},{4,6},{5,1},{6,4},{7,3},{8,10},{9,13},{10,... | collective-permute-start | bytes 3145736 | tf_op jit(solution)/shard_map/ppermute | solution.py:31
  327.4 25.5 %collective-permute-start.63 = (bf16[4,32,4224]{2,1,0:T(8,128)(2,1)S(1)}, bf16[4,32,4224]{2,1,0:T(8,128)(2,1)S(1)}, u32[]{:S(2)}, u32[]{:S(2)}) collective-permute-start(bf16[4,32,4224]{2,1,0:T(8,128)(2,1)S(1)} %get-tuple-element.391), channel_id=1, source_target_pairs={{0,4},{1,3},{2,6},{3,1},{4,0},{5,7},{6,2},{7,5},{8,12},{9,11},{10,... | collective-permute-start | bytes 3244040 | tf_op jit(solution)/shard_map/ppermute | solution.py:31
  328.3 25.9 %collective-permute-start.64 = (bf16[4,32,4224]{2,1,0:T(8,128)(2,1)S(1)}, bf16[4,32,4224]{2,1,0:T(8,128)(2,1)S(1)}, u32[]{:S(2)}, u32[]{:S(2)}) collective-permute-start(bf16[4,32,4224]{2,1,0:T(8,128)(2,1)S(1)} %get-tuple-element.392), channel_id=1, source_target_pairs={{0,4},{1,3},{2,6},{3,1},{4,0},{5,7},{6,2},{7,5},{8,12},{9,11},{10,... | collective-permute-start | bytes 3244040 | tf_op jit(solution)/shard_map/ppermute | solution.py:31
  329.8 23.1 %collective-permute-start.67 = (bf16[1,128,1024]{2,1,0:T(8,128)(2,1)S(1)}, bf16[1,128,1024]{2,1,0:T(8,128)(2,1)S(1)}, u32[]{:S(2)}, u32[]{:S(2)}) collective-permute-start(bf16[1,128,1024]{2,1,0:T(8,128)(2,1)S(1)} %get-tuple-element.395), channel_id=1, source_target_pairs={{0,16},{1,17},{2,18},{3,19},{4,20},{5,21},{6,22},{7,23},{8,24},{9,... | collective-permute-start | bytes 786440 | tf_op jit(solution)/shard_map/ppermute | solution.py:31
  331.4 21.5 %collective-permute-start.66 = (bf16[2,48,1024]{2,1,0:T(8,128)(2,1)S(1)}, bf16[2,48,1024]{2,1,0:T(8,128)(2,1)S(1)}, u32[]{:S(2)}, u32[]{:S(2)}) collective-permute-start(bf16[2,48,1024]{2,1,0:T(8,128)(2,1)S(1)} %get-tuple-element.394), channel_id=1, source_target_pairs={{0,8},{1,9},{2,10},{3,11},{4,12},{5,13},{6,14},{7,15},{8,0},{9,1},... | collective-permute-start | bytes 589832 | tf_op jit(solution)/shard_map/ppermute | solution.py:31
  376.4 24.0 %collective-permute-start.74 = (bf16[1,32,4224]{2,1,0:T(8,128)(2,1)S(1)}, bf16[1,32,4224]{2,1,0:T(8,128)(2,1)S(1)}, u32[]{:S(2)}, u32[]{:S(2)}) collective-permute-start(bf16[1,32,4224]{2,1,0:T(8,128)(2,1)S(1)} %get-tuple-element.433), channel_id=1, source_target_pairs={{0,24},{1,25},{2,26},{3,27},{4,28},{5,29},{6,30},{7,31},{8,16},{9,... | collective-permute-start | bytes 811016 | tf_op jit(solution)/shard_map/ppermute | solution.py:31
  (130 other events, 1305.4 us)

commit v5 on v4

--- a/solution.py
+++ b/solution.py
@@ -453,26 +453,24 @@
     )
 
 
-def decode_kernel(table, sample, cotangent, turned, decode):
+def decode_kernel(table, sample, cotangent, decode):
     cells, width = cotangent.shape
     latent = sample.shape[1]
     parts = len(decode.operands)
 
-    def kernel(table_ref, sample_ref, dy_ref, turned_ref, *rest):
-        refs, (out_ref, grad_ref, back_ref, bias_ref, held, sem) = rest[:parts], rest[parts:]
+    def kernel(table_ref, sample_ref, dy_ref, *rest):
+        refs, (grad_ref, back_ref, bias_ref, held, sem) = rest[:parts], rest[parts:]
         decode.start(table_ref, refs, held, sem)
         grad_ref[...] = left_product(sample_ref[...], dy_ref[...]).astype(LOW)
         bias_ref[...] = jnp.sum(dy_ref[...].astype(FULL), axis=0, keepdims=True)
         arrived(held, sem.at[0])
         back_ref[...] = right_product(dy_ref[...], held[...])
-        out_ref[...] = (matmul(sample_ref[...], held[...]) + turned_ref[2:3]).astype(LOW)
 
     return pl.pallas_call(
         kernel,
-        in_specs=[SCALARS] + [INSIDE] * 3 + [FAR_AWAY] * parts,
-        out_specs=[INSIDE] * 4,
+        in_specs=[SCALARS] + [INSIDE] * 2 + [FAR_AWAY] * parts,
+        out_specs=[INSIDE] * 3,
         out_shape=[
-            jax.ShapeDtypeStruct((cells, width), LOW),
             jax.ShapeDtypeStruct((latent, width), LOW),
             jax.ShapeDtypeStruct((cells, latent), FULL),
             jax.ShapeDtypeStruct((1, width), FULL),
@@ -481,7 +479,30 @@
         compiler_params=params(16),
         cost_estimate=cost(6 * cells * width * latent, 8 << 20),
         name="decode",
-    )(table, sample, cotangent, turned, *decode.operands)
+    )(table, sample, cotangent, *decode.operands)
+
+
+def output_kernel(table, sample, turned, decode):
+    cells = sample.shape[0]
+    width = decode.shape[1]
+    parts = len(decode.operands)
+
+    def kernel(table_ref, sample_ref, turned_ref, *rest):
+        refs, (out_ref, held, sem) = rest[:parts], rest[parts:]
+        decode.start(table_ref, refs, held, sem)
+        arrived(held, sem.at[0])
+        out_ref[...] = (matmul(sample_ref[...], held[...]) + turned_ref[2:3]).astype(LOW)
+
+    return pl.pallas_call(
+        kernel,
+        in_specs=[SCALARS] + [INSIDE] * 2 + [FAR_AWAY] * parts,
+        out_specs=INSIDE,
+        out_shape=jax.ShapeDtypeStruct((cells, width), LOW),
+        scratch_shapes=[pltpu.VMEM(decode.shape, LOW), pltpu.SemaphoreType.DMA((1,))],
+        compiler_params=params(16),
+        cost_estimate=cost(2 * cells * width * sample.shape[1], 4 << 20),
+        name="output",
+    )(table, sample, turned, *decode.operands)
 
 
 def factors_kernel(back, moments, noise, choose, comp_tables):
@@ -828,7 +849,10 @@
 
 
 def odd_even(*terms):
-    return [add_all(one[0], one[1:]).astype(LOW) for one in zip(*[(t[1::2], t[0::2]) for t in terms])]
+    pairs = [term.reshape(-1, 2, *term.shape[1:]) for term in terms]
+    return [
+        add_all(pairs[0][:, k], [pair[:, k] for pair in pairs[1:]]).astype(LOW) for k in (1, 0)
+    ]
 
 
 def far_last(odd, even, bit):
@@ -969,7 +993,7 @@
         ],
         out_specs=[pl.BlockSpec((cells, 128), lambda i: (0, i))] * 3,
         out_shape=[jax.ShapeDtypeStruct((cells, width), LOW)] * 3,
-        compiler_params=params(44),
+        compiler_params=params(20),
         cost_estimate=cost(10 * cells * cells * width, 24 << 20),
         name="attention_backward",
     )(packed, packed, packed, grad_mixed, mixed, attn)
@@ -1148,17 +1172,15 @@
     )
     kl_sum = kl_part + send_core(kl_part)
     kl_sum, sample = hold(kl_sum, sample)
-    decoded, grad_decode, grad_sample, grad_bias = decode_kernel(
-        table, sample, cotangent, turned, decode
-    )
+    grad_decode, grad_sample, grad_bias = decode_kernel(table, sample, cotangent, decode)
     kl_near = [send(kl_sum, bit, bit) for bit in (2, 4, 6)]
     kl_sum = sum(kl_near, kl_sum)
-    kl_sum, grad_sample, decoded = hold(kl_sum, grad_sample, decoded)
+    kl_sum, grad_sample = hold(kl_sum, grad_sample)
     kl_far = [far_exchange(kl_sum, mask) for mask in far_masks()]
     plain, factor, comp = factors_kernel(grad_sample, moments, noise_rows, choose, comp_tables)
     kl_sum = sum(kl_far, kl_sum)
-    kl_sum, grad_decode, plain, factor, grad_bias, decoded = hold(
-        kl_sum, grad_decode, plain, factor, grad_bias, decoded
+    kl_sum, grad_decode, plain, factor, grad_bias = hold(
+        kl_sum, grad_decode, plain, factor, grad_bias
     )
 
     far = lax.axis_size("dp") // 4
@@ -1176,15 +1198,12 @@
         to_latent,
         Slots(rows + decode_rows, width),
     )
-    grad_carried, hidden, decoded, *last_slots = hold(grad_carried, hidden, decoded, *last_slots)
-    decoded_there = send_core(decoded)
+    grad_carried, hidden, *last_slots = hold(grad_carried, hidden, *last_slots)
     last_got = [send_core(one) for one in last_slots[2:]]
     down_slots = weight_grad(
         table, hidden, [grad_carried], Slots(down_rows, width), down_rows, "grad_down"
     )
-    grad_carried, decoded_there, *rest = hold(
-        grad_carried, decoded_there, *last_got, *down_slots
-    )
+    grad_carried, *rest = hold(grad_carried, *last_got, *down_slots)
     last_got, down_slots = rest[:2], rest[2:]
 
     down_got = [send_core(one) for one in down_slots[2:]]
@@ -1248,36 +1267,39 @@
 
     first_high = send_core(first_slots[3])
     up_odd, up_even = odd_even(up_slots[0][:far], up_got[0][:far], up_m2, up_m1)
-    first_high, up_odd, up_even, *first_slots = hold(first_high, up_odd, up_even, *first_slots)
+    last_odd, last_even = odd_even(last_slots[0][:far], last_got[0][:far], last_m2, last_m1)
+    first_high, up_odd, up_even, last_odd, *first_slots = hold(
+        first_high, up_odd, up_even, last_odd, *first_slots
+    )
+    last_far = far_exchange(last_odd, 1)
     first_low = send_core(first_slots[2])
     first_got = [first_low, first_high]
     first_3, first_2 = [both_cores(first_slots, first_got, turn, far) for turn in (3, 2)]
-    last_odd, last_even = odd_even(last_slots[0][:far], last_got[0][:far], last_m2, last_m1)
     down_odd, down_even = odd_even(down_even, down_far)
-    first_low, first_3, first_2, last_odd, last_even, down_odd, down_even = hold(
-        first_low, first_3, first_2, last_odd, last_even, down_odd, down_even
-    )
+    first_low, first_3, first_2, last_far, down_odd, down_even, sample = hold(
+        first_low, first_3, first_2, last_far, down_odd, down_even, sample
+    )
+    last_odd, last_even = odd_even(last_even, last_far)
 
     first_m3, first_m2 = near_second(first_3), near_second(first_2)
     up_far = far_exchange(up_odd, 1)
-    last_far = far_exchange(last_odd, 1)
+    last_even, last_far = far_last(last_odd, last_even, 2)
     down_even, down_far = far_last(down_odd, down_even, 2)
-    first_m3, first_m2, up_far, last_far, down_far = hold(
-        first_m3, first_m2, up_far, last_far, down_far
+    decoded = output_kernel(table, sample, turned, decode)
+    first_m3, first_m2, up_far, last_far, down_far, decoded = hold(
+        first_m3, first_m2, up_far, last_far, down_far, decoded
     )
 
     first_m1 = near_first(add_slots(far, (first_slots[0], far), (first_low, far), (first_m3, 0)))
-    inputs_there = send_core(grad_inputs)
+    inputs_there, decoded_there = send_core(grad_inputs), send_core(decoded)
     up_odd, up_even = odd_even(up_even, up_far)
-    last_odd, last_even = odd_even(last_even, last_far)
     up_even, up_far = far_last(up_odd, up_even, 2)
-    last_even, last_far = far_last(last_odd, last_even, 2)
     down_sum = add_all(down_even[0], [down_far[0]])
-    first_m1, inputs_there, down_sum, up_far, last_far = hold(
-        first_m1, inputs_there, down_sum, up_far, last_far
+    last_sum = add_all(last_even[0], [last_far[0]])
+    first_m1, inputs_there, decoded_there, down_sum, up_far, last_sum = hold(
+        first_m1, inputs_there, decoded_there, down_sum, up_far, last_sum
     )
     up_sum = add_all(up_even[0], [up_far[0]])
-    last_sum = add_all(last_even[0], [last_far[0]])
 
     result = jnp.where(
         core == 0,

time: 408 us -> 406 us (level)
    unnamed x158 -> x170, local copies, waits for them, and re-layouts: 8.23 us -> 10.6 us
  transfers between devices with their start and end apart: 75 -> 75, of which waited for: 30 -> 29; matrix products, arithmetic and copies ran while one was open for 11% -> 11% of each run, Pallas kernels for 31% -> 32%
where the time goes in v5:
time: 406 us; the launch traced here: 402 us
  Pallas kernels  147 us (36%)
  waiting for transfers between devices  127 us (31%)
  starting transfers between devices  59.3 us (15%)
  other arithmetic  39.8 us (10%)
  local copies, waits for them, and re-layouts  25.3 us (6%)
    ppermute x75, waiting for transfers between devices, send(): return lax.ppermute(value, EVERY, pairs)  127 us
    ppermute x75, starting transfers between devices, send(): return lax.ppermute(value, EVERY, pairs)  59.3 us
    pallas_call x3, Pallas kernels, weight_grad(): pl.pallas_call(kernel, grid=(steps,), in_specs=[SCALARS, pl.BlockSpec((ce...  25.2 us
    pallas_call x2, Pallas kernels, attention_forward(): pl.pallas_call(kernel, grid=(last - first,), in_specs=[pl.BlockSpec((cell...  15.8 us
    convert_element_type x10, other arithmetic, add_slots(): return add_all(parts[0], parts[1:]).astype(LOW)  15.1 us
    pallas_call x1, Pallas kernels, middle_back_kernel(): pl.pallas_call(kernel, in_specs=[SCALARS, ANYWHERE] + [INSIDE] * 4 + [ANY...  14 us
    pallas_call x1, Pallas kernels, attention_backward(): pl.pallas_call(kernel, grid=(steps,), in_specs=[pl.BlockSpec((cells, 128)...  13.8 us
    pallas_call x1, Pallas kernels, up_kernel(): pl.pallas_call(kernel, grid=(cols // tile,), in_specs=[SCALARS, whole(cel...  11.6 us
  transfers between devices with their start and end apart: 75, of which 29 were waited for; matrix products, arithmetic and copies ran while one was open for 11% of the time, Pallas kernels for 32%

profile of v5, /device:TPU:8, one launch (start us, length us, event | category | flops | bytes accessed | tf_op | source)
XLA Modules:
  0.0 401.8 jit_solution(12445043473841839081)
XLA Ops:
  15.8 9.4 %collective-permute-done.3 = bf16[1,32,4224]{2,1,0:T(8,128)(2,1)S(1)} collective-permute-done((bf16[1,32,4224]{2,1,0:T(8,128)(2,1)S(1)}, bf16[1,32,4224]{2,1,0:T(8,128)(2,1)S(1)}, u32[]{:S(2)}, u32[]{:S(2)}) %collective-permute-start.3) | collective-permute-done | bytes 270368 | tf_op jit(solution)/shard_map/ppermute | solution.py:31
  25.3 6.1 %collective-permute-done.4 = bf16[1,32,4224]{2,1,0:T(8,128)(2,1)} collective-permute-done((bf16[1,32,4224]{2,1,0:T(8,128)(2,1)S(1)}, bf16[1,32,4224]{2,1,0:T(8,128)(2,1)}, u32[]{:S(2)}, u32[]{:S(2)}) %collective-permute-start.4) | collective-permute-done | bytes 270368 | tf_op jit(solution)/shard_map/ppermute | solution.py:31
  46.1 10.5 %collective-permute-done.8 = bf16[1,32,4096]{2,1,0:T(8,128)(2,1)S(1)} collective-permute-done((bf16[1,32,4096]{2,1,0:T(8,128)(2,1)S(1)}, bf16[1,32,4096]{2,1,0:T(8,128)(2,1)S(1)}, u32[]{:S(2)}, u32[]{:S(2)}) %collective-permute-start.8) | collective-permute-done | bytes 262176 | tf_op jit(solution)/shard_map/ppermute | solution.py:31
  61.9 8.4 %collective-permute-done.14 = bf16[1,128,1024]{2,1,0:T(8,128)(2,1)S(1)} collective-permute-done((bf16[1,128,1024]{2,1,0:T(8,128)(2,1)}, bf16[1,128,1024]{2,1,0:T(8,128)(2,1)S(1)}, u32[]{:S(2)}, u32[]{:S(2)}) %collective-permute-start.14) | collective-permute-done | bytes 262176 | tf_op jit(solution)/shard_map/ppermute | solution.py:31
  70.3 5.7 %collective-permute-done.10.rest_3_.rest_11_.rest_5_ = bf16[4,32,4224]{2,1,0:T(8,128)(2,1)S(1)} collective-permute-done((bf16[4,32,4224]{2,1,0:T(8,128)(2,1)S(1)}, bf16[4,32,4224]{2,1,0:T(8,128)(2,1)S(1)}, u32[]{:S(2)}, u32[]{:S(2)}) %collective-permute-start.10) | collective-permute-done | bytes 1081376 | tf_op jit(solution)/shard_map/ppermute | solution.py:31
  85.2 10.1 %first.1 = (bf16[512,1024]{1,0:T(8,128)(2,1)}, bf16[512,3072]{1,0:T(8,128)(2,1)}, bf16[1024,128]{1,0:T(8,128)(2,1)}, f32[128,1024]{1,0:T(8,128)}) custom-call(s32[96]{0:T(128)} %concatenate.65.table_ref, f32[512,1024]{1,0:T(8,128)} %subtract_multiply_fusion.normed_ref, bf16[4,32,4224]{2,1,0:T(8,128)(2,1)} %bitcast.206, bf16[4,32,4224]{2,1,0:T(8,128)(2,1)} %copy-done.8, ...), custom_call_target="tpu_custom_call" | custom-call | flops 1024 | bytes 1024 | tf_op jit(solution)/shard_map/first/pallas_call | solution.py:233
  95.3 7.9 %attention_forward.2 = (bf16[512,1024]{1,0:T(8,128)(2,1)}, bf16[16,512,512]{2,1,0:T(8,128)(2,1)}) custom-call(s32[512,1]{1,0:T(8,128)} %copy.60.seg_col, s32[1,512]{1,0:T(1,128)} %constant_dynamic-slice_fusion.1.seg_row, bf16[512,3072]{1,0:T(8,128)(2,1)} %get-tuple-element.245.q_ref.k_ref.v_ref, bf16[512,3072]{1,0:T(8,128)(2,1)} %get-tuple-element.245.q_ref.k_ref.v_ref, ...), custom_call_target="tpu_custom_call" | custom-call | flops 1024 | bytes 1024 | tf_op jit(solution)/shard_map/attention_forward/pallas_call | solution.py:930
  117.5 7.9 %attention_forward.3 = (bf16[512,1024]{1,0:T(8,128)(2,1)}, bf16[16,512,512]{2,1,0:T(8,128)(2,1)}) custom-call(s32[512,1]{1,0:T(8,128)} %copy.60.seg_col, s32[1,512]{1,0:T(1,128)} %constant_dynamic-slice_fusion.1.seg_row, bf16[512,3072]{1,0:T(8,128)(2,1)} %get-tuple-element.245.q_ref.k_ref.v_ref, ...), custom_call_target="tpu_custom_call", output_to_operand_aliasing={{0}: (5, {}), {1}: (6, {})} | custom-call | flops 1024 | bytes 1024 | tf_op jit(solution)/shard_map/attention_forward/pallas_call | solution.py:930
  125.5 6.0 %branch.1 = (f32[512,1024]{1,0:T(8,128)}, bf16[512,1024]{1,0:T(8,128)(2,1)}) custom-call(s32[96]{0:T(128)} %concatenate.65.table_ref, bf16[512,1024]{1,0:T(8,128)(2,1)} %get-tuple-element.248.mixed_ref, f32[512,1024]{1,0:T(8,128)} %get-tuple-element.409.in_ref, f32[128,1024]{1,0:T(8,128)} %get-tuple-element.249.turned_ref, bf16[4,32,4224]{2,1,0:T(8,128)(2,1)} %bitcast.208, ...), custom_call_target="tpu_custom_call" | custom-call | flops 1024 | bytes 1024 | tf_op jit(solution)/shard_map/branch/pallas_call | solution.py:274
  144.1 11.6 %up.1 = (bf16[512,4096]{1,0:T(8,128)(2,1)S(1)}, bf16[512,4096]{1,0:T(8,128)(2,1)S(1)}) custom-call(s32[96]{0:T(128)S(1)} %copy-done.45, bf16[512,1024]{1,0:T(8,128)(2,1)S(1)} %copy-done.33, bf16[4,32,4096]{2,1,0:T(8,128)(2,1)S(1)} %bitcast.214, bf16[4,32,4096]{2,1,0:T(8,128)(2,1)S(1)} %collective-permute-done.16.rest_1_, ...), custom_call_target="tpu_custom_call" | custom-call | flops 1024 | bytes 1024 | tf_op jit(solution)/shard_map/up/pallas_call | solution.py:317
  169.3 9.8 %latent.1 = (bf16[512,1024]{1,0:T(8,128)(2,1)S(1)}, f32[512,1024]{1,0:T(8,128)S(1)}, bf16[512,512]{1,0:T(8,128)(2,1)S(1)}, f32[1,512]{1,0:T(1,128)S(1)}) custom-call(s32[96]{0:T(128)S(1)} %copy-done.45, f32[512,1024]{1,0:T(8,128)S(1)} %down_half.1.mid_ref, f32[512,512]{1,0:T(8,128)S(1)} %copy-done.20, bf16[512,16]{1,0:T(8,128)(2,1)S(1)} %fusion.8.choose_ref, ...), custom_call_target="tpu_custom_call" | custom-call | flops 1024 | bytes 1024 | tf_op jit(solution)/shard_map/latent/pallas_call | solution.py:416
  194.5 10.3 %moments.1 = (bf16[512,1024]{1,0:T(8,128)(2,1)S(1)}, f32[2,16,512]{2,1,0:T(8,128)S(1)}, bf16[8,48,1024]{2,1,0:T(8,128)(2,1)S(1)}, bf16[8,48,1024]{2,1,0:T(8,128)...) custom-call(s32[96]{0:T(128)S(1)} %copy-done.45, f32[1]{0:T(128)S(6)} %min.3.weight_ref, ...), custom_call_target="tpu_custom_call" | custom-call | flops 1024 | bytes 1024 | tf_op jit(solution)/shard_map/moments/pallas_call | solution.py:591
  205.4 8.5 %grad_down.1 = (bf16[8,128,1024]{2,1,0:T(8,128)(2,1)S(1)}, bf16[8,128,1024]{2,1,0:T(8,128)(2,1)S(1)}, bf16[8,128,1024]{2,1,0:T(8,128)(2,1)S(1)}, bf16[8,128,1024]{2,1,0:T(8,128)(2,1)S(1)}) custom-call(s32[96]{0:T(128)S(1)} %copy-done.45, bf16[512,4096]{1,0:T(8,128)(2,1)S(1)} %get-tuple-element.310.rest_0_.rest_1_.rest_2_.rest_3_.left_ref, ...), custom_call_target="tpu_custom_call" | custom-call | flops 1024 | bytes 1024 | tf_op jit(solution)/shard_map/grad_down/pallas_call | solution.py:660
  217.8 7.6 %up_back.1.rest_0_.gu_ref = bf16[512,4096]{1,0:T(8,128)(2,1)S(1)} custom-call(s32[96]{0:T(128)S(1)} %copy-done.45, bf16[512,1024]{1,0:T(8,128)(2,1)S(1)} %get-tuple-element.316.rest_0_.grad_ref.gc_ref, bf16[512,4096]{1,0:T(8,128)(2,1)S(1)} %get-tuple-element.317.slope_ref, bf16[4,128,1024]{2,1,0:T(8,128)(2,1)S(1)} %bitcast.220, ...), custom_call_target="tpu_custom_call" | custom-call | flops 1024 | bytes 1024 | tf_op jit(solution)/shard_map/up_back/pallas_call | solution.py:699
  236.1 7.9 %grad_up.1 = (bf16[8,32,4096]{2,1,0:T(8,128)(2,1)S(1)}, bf16[8,32,4096]{2,1,0:T(8,128)(2,1)S(1)}, bf16[8,32,4096]{2,1,0:T(8,128)(2,1)}, bf16[8,32,4096]{2,1,0:T(8,128)(2,1)}) custom-call(s32[96]{0:T(128)S(1)} %copy-done.45, bf16[512,1024]{1,0:T(8,128)(2,1)S(1)} %copy-done.34, bf16[512,4096]{1,0:T(8,128)(2,1)S(1)} %copy-done.6), custom_call_target="tpu_custom_call" | custom-call | flops 1024 | bytes 1024 | tf_op jit(solution)/shard_map/grad_up/pallas_call | solution.py:660
  249.4 14.0 %middle_back.1 = (f32[512,1024]{1,0:T(8,128)}, bf16[1024,1024]{1,0:T(8,128)(2,1)}, bf16[512,1024]{1,0:T(8,128)(2,1)S(1)}, f32[1,1024]{1,0:T(1,128)S(1)}) custom-call(s32[96]{0:T(128)S(1)} %copy-done.45, bf16[512,4096]{1,0:T(8,128)(2,1)} %copy-done.5, bf16[512,1024]{1,0:T(8,128)(2,1)S(1)} %copy-done.22, f32[512,1024]{1,0:T(8,128)} %get-tuple-element.273.mid_ref, ...), custom_call_target="tpu_custom_call" | custom-call | flops 1024 | bytes 1024 | tf_op jit(solution)/shard_map/middle_back/pallas_call | solution.py:745
  276.7 13.8 %attention_backward.1 = (bf16[512,1024]{1,0:T(8,128)(2,1)S(1)}, bf16[512,1024]{1,0:T(8,128)(2,1)S(1)}, bf16[512,1024]{1,0:T(8,128)(2,1)S(1)}) custom-call(bf16[512,3072]{1,0:T(8,128)(2,1)S(1)} %copy-done.2, bf16[512,3072]{1,0:T(8,128)(2,1)S(1)} %copy-done.2, bf16[512,3072]{1,0:T(8,128)(2,1)S(1)} %copy-done.2, ...), custom_call_target="tpu_custom_call" | custom-call | flops 1024 | bytes 1024 | tf_op jit(solution)/shard_map/attention_backward/pallas_call | solution.py:983
  297.7 9.6 %input_back.1 = (f32[512,1024]{1,0:T(8,128)}, bf16[1024,128]{1,0:T(8,128)(2,1)S(1)}) custom-call(s32[96]{0:T(128)S(1)} %copy-done.45, bf16[512,1024]{1,0:T(8,128)(2,1)S(1)} %get-tuple-element.352.gq_ref.rest_0_, bf16[512,1024]{1,0:T(8,128)(2,1)S(1)} %get-tuple-element.353.gk_ref.rest_1_, bf16[512,1024]{1,0:T(8,128)(2,1)S(1)} %get-tuple-element.354.gv_ref.rest_2_, ...), custom_call_target="tpu_custom_call" | custom-call | flops 1024 | bytes 1024 | tf_op jit(solution)/shard_map/input_back/pallas_call | solution.py:795
  307.3 8.9 %grad_qkv.1 = (bf16[8,32,4224]{2,1,0:T(8,128)(2,1)S(1)}, bf16[8,32,4224]{2,1,0:T(8,128)(2,1)S(1)}, bf16[8,32,4224]{2,1,0:T(8,128)(2,1)S(1)}, bf16[8,32,4224]{2,1,0:T(8,128)(2,1)S(1)}) custom-call(s32[96]{0:T(128)S(1)} %copy-done.45, bf16[512,1024]{1,0:T(8,128)(2,1)S(1)} %copy-done.41, bf16[512,1024]{1,0:T(8,128)(2,1)S(1)} %get-tuple-element.352.gq_ref.rest_0_, ...), custom_call_target="tpu_custom_call" | custom-call | flops 1024 | bytes 1024 | tf_op jit(solution)/shard_map/grad_qkv/pallas_call | solution.py:660
  323.0 6.2 %collective-permute-done.62 = bf16[2,48,1024]{2,1,0:T(8,128)(2,1)S(1)} collective-permute-done((bf16[2,48,1024]{2,1,0:T(8,128)(2,1)S(1)}, bf16[2,48,1024]{2,1,0:T(8,128)(2,1)S(1)}, u32[]{:S(2)}, u32[]{:S(2)}) %collective-permute-start.62) | collective-permute-done | bytes 196640 | tf_op jit(solution)/shard_map/ppermute | solution.py:31
  337.5 11.9 %collective-permute-done.65 = bf16[2,32,4096]{2,1,0:T(8,128)(2,1)S(1)} collective-permute-done((bf16[2,32,4096]{2,1,0:T(8,128)(2,1)S(1)}, bf16[2,32,4096]{2,1,0:T(8,128)(2,1)S(1)}, u32[]{:S(2)}, u32[]{:S(2)}) %collective-permute-start.65) | collective-permute-done | bytes 524320 | tf_op jit(solution)/shard_map/ppermute | solution.py:31
  358.5 11.0 %collective-permute-done.71 = bf16[1,32,4096]{2,1,0:T(8,128)(2,1)S(1)} collective-permute-done((bf16[1,32,4096]{2,1,0:T(8,128)(2,1)S(1)}, bf16[1,32,4096]{2,1,0:T(8,128)(2,1)S(1)}, u32[]{:S(2)}, u32[]{:S(2)}) %collective-permute-start.71) | collective-permute-done | bytes 262176 | tf_op jit(solution)/shard_map/ppermute | solution.py:31
  383.7 9.0 %collective-permute-done.73 = bf16[1,32,4224]{2,1,0:T(8,128)(2,1)S(1)} collective-permute-done((bf16[1,32,4224]{2,1,0:T(8,128)(2,1)S(1)}, bf16[1,32,4224]{2,1,0:T(8,128)(2,1)S(1)}, u32[]{:S(2)}, u32[]{:S(2)}) %collective-permute-start.73) | collective-permute-done | bytes 270368 | tf_op jit(solution)/shard_map/ppermute | solution.py:31
  392.7 6.0 %collective-permute-done.74 = bf16[1,32,4224]{2,1,0:T(8,128)(2,1)S(1)} collective-permute-done((bf16[1,32,4224]{2,1,0:T(8,128)(2,1)S(1)}, bf16[1,32,4224]{2,1,0:T(8,128)(2,1)S(1)}, u32[]{:S(2)}, u32[]{:S(2)}) %collective-permute-start.74) | collective-permute-done | bytes 270368 | tf_op jit(solution)/shard_map/ppermute | solution.py:31
  (388 shorter events, 181.1 us)
Async XLA Ops:
  3.2 28.1 %collective-permute-start = (bf16[512,1024]{1,0:T(8,128)(2,1)}, bf16[512,1024]{1,0:T(8,128)(2,1)}, u32[]{:S(2)}, u32[]{:S(2)}) collective-permute-start(bf16[512,1024]{1,0:T(8,128)(2,1)} %dynamic-slice_bitcast_fusion), channel_id=1, source_target_pairs={{0,1},{1,0},{2,3},{3,2},{4,5},{5,4},{6,7},{7,6},{8,9},{9,8},{10,11... | collective-permute-start | bytes 3145736 | tf_op jit(solution)/shard_map/ppermute | solution.py:31
  3.8 21.5 %collective-permute-start.3 = (bf16[1,32,4224]{2,1,0:T(8,128)(2,1)S(1)}, bf16[1,32,4224]{2,1,0:T(8,128)(2,1)S(1)}, u32[]{:S(2)}, u32[]{:S(2)}) collective-permute-start(bf16[1,32,4224]{2,1,0:T(8,128)(2,1)S(1)} %bitcast.234), channel_id=1, source_target_pairs={{0,16},{1,17},{2,18},{3,19},{4,20},{5,21},{6,22},{7,23},{8,24},{9,... | collective-permute-start | bytes 811016 | tf_op jit(solution)/shard_map/ppermute | solution.py:31
  6.8 24.6 %collective-permute-start.4 = (bf16[1,32,4224]{2,1,0:T(8,128)(2,1)S(1)}, bf16[1,32,4224]{2,1,0:T(8,128)(2,1)}, u32[]{:S(2)}, u32[]{:S(2)}) collective-permute-start(bf16[1,32,4224]{2,1,0:T(8,128)(2,1)S(1)} %bitcast.235), channel_id=1, source_target_pairs={{0,24},{1,25},{2,26},{3,27},{4,28},{5,29},{6,30},{7,31},{8,16},{9,... | collective-permute-start | bytes 811016 | tf_op jit(solution)/shard_map/ppermute | solution.py:31
  32.6 28.2 %collective-permute-start.5 = (bf16[4,32,4224]{2,1,0:T(8,128)(2,1)S(1)}, bf16[4,32,4224]{2,1,0:T(8,128)(2,1)S(1)}, u32[]{:S(2)}, u32[]{:S(2)}) collective-permute-start(bf16[4,32,4224]{2,1,0:T(8,128)(2,1)S(1)} %bitcast.203), channel_id=1, source_target_pairs={{0,2},{1,5},{2,0},{3,7},{4,6},{5,1},{6,4},{7,3},{8,10},{9,13},{10,... | collective-permute-start | bytes 3244040 | tf_op jit(solution)/shard_map/ppermute | solution.py:31
  34.1 26.7 %collective-permute-start.6 = (bf16[4,32,4224]{2,1,0:T(8,128)(2,1)S(1)}, bf16[4,32,4224]{2,1,0:T(8,128)(2,1)S(1)}, u32[]{:S(2)}, u32[]{:S(2)}) collective-permute-start(bf16[4,32,4224]{2,1,0:T(8,128)(2,1)S(1)} %bitcast.204), channel_id=1, source_target_pairs={{0,4},{1,3},{2,6},{3,1},{4,0},{5,7},{6,2},{7,5},{8,12},{9,11},{10,... | collective-permute-start | bytes 3244040 | tf_op jit(solution)/shard_map/ppermute | solution.py:31
  35.7 20.9 %collective-permute-start.8 = (bf16[1,32,4096]{2,1,0:T(8,128)(2,1)S(1)}, bf16[1,32,4096]{2,1,0:T(8,128)(2,1)S(1)}, u32[]{:S(2)}, u32[]{:S(2)}) collective-permute-start(bf16[1,32,4096]{2,1,0:T(8,128)(2,1)S(1)} %bitcast.259), channel_id=1, source_target_pairs={{0,16},{1,17},{2,18},{3,19},{4,20},{5,21},{6,22},{7,23},{8,24},{9,... | collective-permute-start | bytes 786440 | tf_op jit(solution)/shard_map/ppermute | solution.py:31
  38.7 22.1 %collective-permute-start.9 = (bf16[1,32,4096]{2,1,0:T(8,128)(2,1)S(1)}, bf16[1,32,4096]{2,1,0:T(8,128)(2,1)S(1)}, u32[]{:S(2)}, u32[]{:S(2)}) collective-permute-start(bf16[1,32,4096]{2,1,0:T(8,128)(2,1)S(1)} %bitcast.260), channel_id=1, source_target_pairs={{0,24},{1,25},{2,26},{3,27},{4,28},{5,29},{6,30},{7,31},{8,16},{9,... | collective-permute-start | bytes 786440 | tf_op jit(solution)/shard_map/ppermute | solution.py:31
  79.7 28.1 %collective-permute-start.16 = (bf16[4,32,4096]{2,1,0:T(8,128)(2,1)S(1)}, bf16[4,32,4096]{2,1,0:T(8,128)(2,1)S(1)}, u32[]{:S(2)}, u32[]{:S(2)}) collective-permute-start(bf16[4,32,4096]{2,1,0:T(8,128)(2,1)S(1)} %bitcast.211), channel_id=1, source_target_pairs={{0,2},{1,5},{2,0},{3,7},{4,6},{5,1},{6,4},{7,3},{8,10},{9,13},{10,... | collective-permute-start | bytes 3145736 | tf_op jit(solution)/shard_map/ppermute | solution.py:31
  80.7 27.2 %collective-permute-start.17 = (bf16[4,32,4096]{2,1,0:T(8,128)(2,1)S(1)}, bf16[4,32,4096]{2,1,0:T(8,128)(2,1)}, u32[]{:S(2)}, u32[]{:S(2)}) collective-permute-start(bf16[4,32,4096]{2,1,0:T(8,128)(2,1)S(1)} %bitcast.212), channel_id=1, source_target_pairs={{0,4},{1,3},{2,6},{3,1},{4,0},{5,7},{6,2},{7,5},{8,12},{9,11},{10,... | collective-permute-start | bytes 3145736 | tf_op jit(solution)/shard_map/ppermute | solution.py:31
  81.2 26.6 %collective-permute-start.19 = (bf16[1,128,1024]{2,1,0:T(8,128)(2,1)}, bf16[1,128,1024]{2,1,0:T(8,128)(2,1)}, u32[]{:S(2)}, u32[]{:S(2)}) collective-permute-start(bf16[1,128,1024]{2,1,0:T(8,128)(2,1)} %bitcast.15), channel_id=1, source_target_pairs={{0,16},{1,17},{2,18},{3,19},{4,20},{5,21},{6,22},{7,23},{8,24},{9,... | collective-permute-start | bytes 786440 | tf_op jit(solution)/shard_map/ppermute | solution.py:31
  81.2 26.6 %collective-permute-start.20 = (bf16[1,128,1024]{2,1,0:T(8,128)(2,1)}, bf16[1,128,1024]{2,1,0:T(8,128)(2,1)}, u32[]{:S(2)}, u32[]{:S(2)}) collective-permute-start(bf16[1,128,1024]{2,1,0:T(8,128)(2,1)} %bitcast.15), channel_id=1, source_target_pairs={{0,24},{1,25},{2,26},{3,27},{4,28},{5,29},{6,30},{7,31},{8,16},{9,... | collective-permute-start | bytes 786440 | tf_op jit(solution)/shard_map/ppermute | solution.py:31
  82.8 24.4 %collective-permute-start.18 = (bf16[2,48,1024]{2,1,0:T(8,128)(2,1)S(1)}, bf16[2,48,1024]{2,1,0:T(8,128)(2,1)}, u32[]{:S(2)}, u32[]{:S(2)}) collective-permute-start(bf16[2,48,1024]{2,1,0:T(8,128)(2,1)S(1)} %bitcast.239), channel_id=1, source_target_pairs={{0,4},{1,3},{2,6},{3,1},{4,0},{5,7},{6,2},{7,5},{8,12},{9,11},{10,... | collective-permute-start | bytes 589832 | tf_op jit(solution)/shard_map/ppermute | solution.py:31
  107.2 24.3 %collective-permute-start.23 = (bf16[4,32,4096]{2,1,0:T(8,128)(2,1)S(1)}, bf16[4,32,4096]{2,1,0:T(8,128)(2,1)}, u32[]{:S(2)}, u32[]{:S(2)}) collective-permute-start(bf16[4,32,4096]{2,1,0:T(8,128)(2,1)S(1)} %bitcast.213), channel_id=1, source_target_pairs={{0,1},{1,0},{2,3},{3,2},{4,5},{5,4},{6,7},{7,6},{8,9},{9,8},{10,11... | collective-permute-start | bytes 3145736 | tf_op jit(solution)/shard_map/ppermute | solution.py:31
  109.5 25.5 %collective-permute-start.22 = (bf16[4,128,1024]{2,1,0:T(8,128)(2,1)S(1)}, bf16[4,128,1024]{2,1,0:T(8,128)(2,1)}, u32[]{:S(2)}, u32[]{:S(2)}) collective-permute-start(bf16[4,128,1024]{2,1,0:T(8,128)(2,1)S(1)} %bitcast.216), channel_id=1, source_target_pairs={{0,2},{1,5},{2,0},{3,7},{4,6},{5,1},{6,4},{7,3},{8,10},{9,13},{10,... | collective-permute-start | bytes 3145736 | tf_op jit(solution)/shard_map/ppermute | solution.py:31
  110.1 24.9 %collective-permute-start.21 = (bf16[4,32,4096]{2,1,0:T(8,128)(2,1)S(1)}, bf16[4,32,4096]{2,1,0:T(8,128)(2,1)}, u32[]{:S(2)}, u32[]{:S(2)}) collective-permute-start(bf16[4,32,4096]{2,1,0:T(8,128)(2,1)S(1)} %collective-permute-done.16.rest_1_), channel_id=1, source_target_pairs={{0,4},{1,3},{2,6},{3,1},{4,0},{5,7},{6,2},{7,5},{8,12},{9,11},{10,... | collective-permute-start | bytes 3145736 | tf_op jit(solution)/shard_map/ppermute | solution.py:31
  136.5 25.0 %collective-permute-start.30 = (bf16[4,128,1024]{2,1,0:T(8,128)(2,1)}, bf16[4,128,1024]{2,1,0:T(8,128)(2,1)S(1)}, u32[]{:S(2)}, u32[]{:S(2)}) collective-permute-start(bf16[4,128,1024]{2,1,0:T(8,128)(2,1)} %collective-permute-done.22.rest_5_.rest_1_), channel_id=1, source_target_pairs={{0,4},{1,3},{2,6},{3,1},{4,0},{5,7},{6,2},{7,5},{8,12},{9,11},{10,... | collective-permute-start | bytes 3145736 | tf_op jit(solution)/shard_map/ppermute | solution.py:31
  140.8 20.7 %collective-permute-start.31 = (bf16[4,128,1024]{2,1,0:T(8,128)(2,1)S(1)}, bf16[4,128,1024]{2,1,0:T(8,128)(2,1)S(1)}, u32[]{:S(2)}, u32[]{:S(2)}) collective-permute-start(bf16[4,128,1024]{2,1,0:T(8,128)(2,1)S(1)} %bitcast.218), channel_id=1, source_target_pairs={{0,1},{1,0},{2,3},{3,2},{4,5},{5,4},{6,7},{7,6},{8,9},{9,8},{10,11... | collective-permute-start | bytes 3145736 | tf_op jit(solution)/shard_map/ppermute | solution.py:31
  141.0 20.5 %collective-permute-start.32 = (bf16[4,128,1024]{2,1,0:T(8,128)(2,1)}, bf16[4,128,1024]{2,1,0:T(8,128)(2,1)S(1)}, u32[]{:S(2)}, u32[]{:S(2)}) collective-permute-start(bf16[4,128,1024]{2,1,0:T(8,128)(2,1)} %collective-permute-done.22.rest_5_.rest_1_), channel_id=1, source_target_pairs={{0,1},{1,0},{2,3},{3,2},{4,5},{5,4},{6,7},{7,6},{8,9},{9,8},{10,11... | collective-permute-start | bytes 3145736 | tf_op jit(solution)/shard_map/ppermute | solution.py:31
  265.4 25.0 %collective-permute-start.57 = (bf16[4,128,1024]{2,1,0:T(8,128)(2,1)S(1)}, bf16[4,128,1024]{2,1,0:T(8,128)(2,1)S(1)}, u32[]{:S(2)}, u32[]{:S(2)}) collective-permute-start(bf16[4,128,1024]{2,1,0:T(8,128)(2,1)S(1)} %add_convert_fusion.5), channel_id=1, source_target_pairs={{0,2},{1,5},{2,0},{3,7},{4,6},{5,1},{6,4},{7,3},{8,10},{9,13},{10,... | collective-permute-start | bytes 3145736 | tf_op jit(solution)/shard_map/ppermute | solution.py:31
  272.3 43.9 %collective-permute-start.55 = (bf16[4,32,4096]{2,1,0:T(8,128)(2,1)}, bf16[4,32,4096]{2,1,0:T(8,128)(2,1)}, u32[]{:S(2)}, u32[]{:S(2)}) collective-permute-start(bf16[4,32,4096]{2,1,0:T(8,128)(2,1)} %get-tuple-element.416), channel_id=1, source_target_pairs={{0,4},{1,3},{2,6},{3,1},{4,0},{5,7},{6,2},{7,5},{8,12},{9,11},{10,... | collective-permute-start | bytes 3145736 | tf_op jit(solution)/shard_map/ppermute | solution.py:31
  292.0 24.3 %collective-permute-start.58 = (bf16[4,32,4096]{2,1,0:T(8,128)(2,1)}, bf16[4,32,4096]{2,1,0:T(8,128)(2,1)}, u32[]{:S(2)}, u32[]{:S(2)}) collective-permute-start(bf16[4,32,4096]{2,1,0:T(8,128)(2,1)} %add_convert_fusion.4), channel_id=1, source_target_pairs={{0,2},{1,5},{2,0},{3,7},{4,6},{5,1},{6,4},{7,3},{8,10},{9,13},{10,... | collective-permute-start | bytes 3145736 | tf_op jit(solution)/shard_map/ppermute | solution.py:31
  329.2 22.3 %collective-permute-start.63 = (bf16[4,32,4224]{2,1,0:T(8,128)(2,1)S(1)}, bf16[4,32,4224]{2,1,0:T(8,128)(2,1)S(1)}, u32[]{:S(2)}, u32[]{:S(2)}) collective-permute-start(bf16[4,32,4224]{2,1,0:T(8,128)(2,1)S(1)} %get-tuple-element.386), channel_id=1, source_target_pairs={{0,4},{1,3},{2,6},{3,1},{4,0},{5,7},{6,2},{7,5},{8,12},{9,11},{10,... | collective-permute-start | bytes 3244040 | tf_op jit(solution)/shard_map/ppermute | solution.py:31
  329.7 26.3 %collective-permute-start.64 = (bf16[4,32,4224]{2,1,0:T(8,128)(2,1)S(1)}, bf16[4,32,4224]{2,1,0:T(8,128)(2,1)S(1)}, u32[]{:S(2)}, u32[]{:S(2)}) collective-permute-start(bf16[4,32,4224]{2,1,0:T(8,128)(2,1)S(1)} %get-tuple-element.387), channel_id=1, source_target_pairs={{0,4},{1,3},{2,6},{3,1},{4,0},{5,7},{6,2},{7,5},{8,12},{9,11},{10,... | collective-permute-start | bytes 3244040 | tf_op jit(solution)/shard_map/ppermute | solution.py:31
  374.2 24.5 %collective-permute-start.74 = (bf16[1,32,4224]{2,1,0:T(8,128)(2,1)S(1)}, bf16[1,32,4224]{2,1,0:T(8,128)(2,1)S(1)}, u32[]{:S(2)}, u32[]{:S(2)}) collective-permute-start(bf16[1,32,4224]{2,1,0:T(8,128)(2,1)S(1)} %get-tuple-element.429), channel_id=1, source_target_pairs={{0,24},{1,25},{2,26},{3,27},{4,28},{5,29},{6,30},{7,31},{8,16},{9,... | collective-permute-start | bytes 811016 | tf_op jit(solution)/shard_map/ppermute | solution.py:31
  (138 other events, 1400.8 us)
